TPU v7x, 32 devices: a whole 2x2x4 slice. The times are simulated.
32 devices in a mesh: dp: 16 (over z, x, core), seq: 2 (over y).
Axes of the slice: x: 2, y: 2, z: 4, core: 2. Of those that a mesh axis runs over, the one named last changes fastest.
Arguments:
- hidden_in: bfloat16 [16, 1024, 1408], P('dp', 'seq'), may hold values from -6 to 6
- skip_in: bfloat16 [16, 1024, 1408], P('dp', 'seq'), may hold values from -6 to 6
- clip_text: bfloat16 [16, 77, 1024], P('dp'), may hold values from -6 to 6
- mt5_text: bfloat16 [16, 256, 2048], P('dp'), may hold values from -6 to 6
- time_ids: int32 [16], P('dp'), may hold values from 0 to 999
- null_text: int32 [16], P('dp'), may hold values 0 or 1
- loss_weight: float32 [16], P('dp'), may hold values from 0.3 to 3
- patch_pos: int32 [2, 16, 1024], P(None, 'dp', 'seq'), may hold values from 0 to 63, as said below
- out_cot: bfloat16 [16, 1024, 1408], P('dp', 'seq'), may hold values from -6 to 6
- skip_weight: bfloat16 [2816, 1408], P('dp', 'seq'), may hold values from -0.109375 to 0.109375
- time_first: bfloat16 [256, 1408], P('dp', 'seq'), may hold values from -0.375 to 0.375
- time_second: bfloat16 [1408, 1408], P('dp', 'seq'), may hold values from -0.15625 to 0.15625
- attn_qkv: bfloat16 [1408, 4224], P('dp', 'seq'), may hold values from -0.15625 to 0.15625
- attn_out: bfloat16 [1408, 1408], P('dp', 'seq'), may hold values from -2.5 to 2.5
- cross_qproj: bfloat16 [1408, 1408], P('dp', 'seq'), may hold values from -0.15625 to 0.15625
- cross_kvproj: bfloat16 [1024, 2816], P('dp', 'seq'), may hold values from -0.1875 to 0.1875
- cross_out: bfloat16 [1408, 1408], P('dp', 'seq'), may hold values from -1.5 to 1.5
- text_proj: bfloat16 [2048, 1024], P('dp', 'seq'), may hold values from -0.125 to 0.125
- mlp_up: bfloat16 [1408, 6336], P('dp', 'seq'), may hold values from -0.15625 to 0.15625
- mlp_down: bfloat16 [6336, 1408], P('dp', 'seq'), may hold values from -0.078125 to 0.078125
- norm_gains: float32 [4, 1408], replicated, may hold values from 0.5 to 1.5
- head_gains: float32 [4, 88], replicated, may hold values from 0.5 to 1.5
Outputs:
- block_out: bfloat16 [16, 1024, 1408], P('dp', 'seq')
- hidden_grad: float32 [16, 1024, 1408], P('dp', 'seq')
- skip_grad: float32 [16, 1024, 1408], P('dp', 'seq')
- grad_skipw: float32 [2816, 1408], P('dp', 'seq')
- grad_tfirst: float32 [256, 1408], P('dp', 'seq')
- grad_tsecond: float32 [1408, 1408], P('dp', 'seq')
- grad_qkv: float32 [1408, 4224], P('dp', 'seq')
- grad_aout: float32 [1408, 1408], P('dp', 'seq')
- grad_cquery: float32 [1408, 1408], P('dp', 'seq')
- grad_ckv: float32 [1024, 2816], P('dp', 'seq')
- grad_cout: float32 [1408, 1408], P('dp', 'seq')
- grad_tproj: float32 [2048, 1024], P('dp', 'seq')
- grad_up: float32 [1408, 6336], P('dp', 'seq')
- grad_down: float32 [6336, 1408], P('dp', 'seq')
- grad_ngains: float32 [4, 1408], replicated
- grad_hgains: float32 [4, 88], replicated
Inputs may be any that keep to these rules, and one draw needn't show every extreme that they name: `patch_pos`: each image's patches are the cells of a 32 x 32 grid, each cell once, in an order of that image's own, shifted by a row and a column offset of that image.
All inputs are finite; a program needn't handle non-finite values. No bound on the sum of `null_text` on one device may be relied on, other than what follows from the above.
Results may differ from a plain program's by a relative error of at most 0.023.
Values may be sent and summed in bfloat16 or wider, within the bound.
A program may use at most 384 MiB of HBM per device.

v0:
```python
import math

import jax
import jax.numpy as jnp
from jax import lax
from jax.sharding import PartitionSpec as P

HEADS = 16
HEAD_DIM = 88
FREQ = 256


EPSILON = 1e-06
HIGHEST = lax.Precision.HIGHEST


def normalize(values):
    center = values - jnp.mean(values, axis=-1, keepdims=True)
    variance = jnp.mean(center * center, axis=-1, keepdims=True)
    return center * lax.rsqrt(variance + EPSILON)


def scaled_norm(values, gain_row):
    return normalize(values) * gain_row


def rotate(values, pos_rows, pos_cols):
    quarter = values.shape[-1] // 4
    frequency = 10000.0 ** (-jnp.arange(quarter, dtype=jnp.float32) / quarter)

    def turn(halfpart, position):
        angles = position[:, None] * frequency[None, :]
        cosine = jnp.cos(angles)[:, None, :]
        sine_part = jnp.sin(angles)[:, None, :]
        former = halfpart[..., :quarter]
        latter = halfpart[..., quarter:]
        return jnp.concatenate(
            [former * cosine - latter * sine_part, former * sine_part + latter * cosine], -1
        )

    return jnp.concatenate(
        [turn(values[..., : 2 * quarter], pos_rows), turn(values[..., 2 * quarter :], pos_cols)], -1
    )


def time_features(step_ids):
    half_count = FREQ // 2
    frequency = jnp.exp(-math.log(10000.0) * jnp.arange(half_count, dtype=jnp.float32) / half_count)
    angles = step_ids.astype(jnp.float32)[:, None] * frequency[None, :]
    return jnp.concatenate([jnp.cos(angles), jnp.sin(angles)], -1)


def project(left, right):
    return jnp.einsum("tc,cd->td", left, right, preferred_element_type=jnp.float32)


def project_back(grad_low, right):
    return jnp.einsum("td,cd->tc", grad_low, right, preferred_element_type=jnp.float32)


def weight_grad(left, grad_low):
    return jnp.einsum("tc,td->cd", left, grad_low, preferred_element_type=jnp.float32)


def body(
    hidden_in,
    skip_in,
    clip_text,
    mt5_text,
    time_ids,
    null_text,
    loss_weight,
    patch_pos,
    out_cot,
    skip_weight,
    time_first,
    time_second,
    attn_qkv,
    attn_out,
    cross_qproj,
    cross_kvproj,
    cross_out,
    text_proj,
    mlp_up,
    mlp_down,
    norm_gains,
    head_gains,
):
    images, local, width = hidden_in.shape
    groups = lax.axis_size("seq")
    heads_here = HEADS // groups
    narrow = width // groups
    tokens = images * local
    full_len = local * groups
    clip_len = clip_text.shape[1]
    text_len = clip_len + mt5_text.shape[1]
    score_scale = HEAD_DIM ** (-0.5)
    pos_rows = patch_pos[0].reshape(tokens).astype(jnp.float32)
    pos_cols = patch_pos[1].reshape(tokens).astype(jnp.float32)
    col_full = (
        lax.all_gather(skip_weight, "seq", axis=1, tiled=True),
        lax.all_gather(time_first, "seq", axis=1, tiled=True),
        lax.all_gather(time_second, "seq", axis=1, tiled=True),
        lax.all_gather(attn_qkv, "seq", axis=1, tiled=True),
        lax.all_gather(attn_out, "seq", axis=1, tiled=True),
        lax.all_gather(cross_qproj, "seq", axis=1, tiled=True),
        lax.all_gather(cross_kvproj, "seq", axis=1, tiled=True),
        lax.all_gather(cross_out, "seq", axis=1, tiled=True),
        lax.all_gather(text_proj, "seq", axis=1, tiled=True),
        lax.all_gather(mlp_up, "seq", axis=1, tiled=True),
        lax.all_gather(mlp_down, "seq", axis=1, tiled=True),
    )
    weight_set = (
        lax.all_gather(col_full[0], "dp", axis=0, tiled=True),
        lax.all_gather(col_full[1], "dp", axis=0, tiled=True),
        lax.all_gather(col_full[2], "dp", axis=0, tiled=True),
        lax.all_gather(col_full[3], "dp", axis=0, tiled=True),
        lax.all_gather(col_full[4], "dp", axis=0, tiled=True),
        lax.all_gather(col_full[5], "dp", axis=0, tiled=True),
        lax.all_gather(col_full[6], "dp", axis=0, tiled=True),
        lax.all_gather(col_full[7], "dp", axis=0, tiled=True),
        lax.all_gather(col_full[8], "dp", axis=0, tiled=True),
        lax.all_gather(col_full[9], "dp", axis=0, tiled=True),
        lax.all_gather(col_full[10], "dp", axis=0, tiled=True),
    )
    w_skip, w_first, w_second, w_qkv, w_aout, w_cq, w_ckv, w_cout, w_text, w_up, w_down = weight_set
    joined = jnp.concatenate([hidden_in, skip_in], -1).reshape(tokens, 2 * width)
    merged = project(joined, w_skip)
    resid0 = scaled_norm(merged, norm_gains[0])
    feats = time_features(time_ids).astype(jnp.bfloat16)
    before = project(feats, w_first)
    lifted = jax.nn.silu(before).astype(jnp.bfloat16)
    shift = project(lifted, w_second)
    shift_tok = jnp.repeat(shift, local, axis=0)
    normed1 = (scaled_norm(resid0, norm_gains[1]) + shift_tok).astype(jnp.bfloat16)
    packed = project(normed1, w_qkv).reshape(tokens, 3, HEADS, HEAD_DIM)

    def query_prep(values, gain_row):
        return rotate(scaled_norm(values, gain_row), pos_rows, pos_cols)

    self_q = query_prep(packed[:, 0], head_gains[0]).astype(jnp.bfloat16)
    self_k = query_prep(packed[:, 1], head_gains[1]).astype(jnp.bfloat16)
    self_v = packed[:, 2].astype(jnp.bfloat16)
    stacked = jnp.stack([self_q, self_k, self_v], 1).reshape(images, local, 3, width)

    def self_block(operand):
        queries, keyset, valueset = operand
        scores = (
            jnp.einsum("qd,kd->qk", queries, keyset, preferred_element_type=jnp.float32)
            * score_scale
        )
        top_score = jnp.max(scores, axis=-1, keepdims=True)
        exponent = jnp.exp(scores - top_score)
        totals = jnp.sum(exponent, axis=-1, keepdims=True)
        mixed_out = jnp.einsum(
            "qk,kd->qd",
            (exponent / totals).astype(jnp.bfloat16),
            valueset,
            preferred_element_type=jnp.float32,
        )
        return (mixed_out.astype(jnp.bfloat16), (top_score + jnp.log(totals))[:, 0])

    pieces = lax.all_to_all(stacked, "seq", split_axis=3, concat_axis=1, tiled=True)
    item_count = pieces.shape[0]
    length = pieces.shape[1]
    split_heads = pieces.reshape(item_count, length, 3, heads_here, HEAD_DIM)
    triple_set = jnp.transpose(split_heads, (2, 0, 3, 1, 4)).reshape(
        3, item_count * heads_here, length, HEAD_DIM
    )
    mixed_out, logsum = lax.map(self_block, (triple_set[0], triple_set[1], triple_set[2]))
    joined_heads = jnp.transpose(
        mixed_out.reshape(item_count, heads_here, length, HEAD_DIM), (0, 2, 1, 3)
    ).reshape(item_count, length, narrow)
    returned = lax.all_to_all(joined_heads, "seq", split_axis=1, concat_axis=2, tiled=True)
    self_logsum = logsum.reshape(item_count, heads_here, length)
    attn_flat = returned.reshape(tokens, width)
    resid1 = resid0 + project(attn_flat, w_aout)
    normed2 = scaled_norm(resid1, norm_gains[2]).astype(jnp.bfloat16)
    cross_pre = project(normed2, w_cq).reshape(tokens, HEADS, HEAD_DIM)
    cross_q = (
        scaled_norm(cross_pre, head_gains[2])
        .astype(jnp.bfloat16)
        .reshape(images, local, HEADS, HEAD_DIM)
    )
    keep_text = (1 - null_text).astype(jnp.bfloat16)
    projected = jnp.einsum(
        "btc,cd->btd", mt5_text, w_text, preferred_element_type=jnp.float32
    ).astype(jnp.bfloat16)
    context = jnp.concatenate([clip_text, projected], 1) * keep_text[:, None, None]
    text_kv = jnp.einsum("btc,cd->btd", context, w_ckv, preferred_element_type=jnp.float32).reshape(
        images, text_len, 2, HEADS, HEAD_DIM
    )
    cross_k = scaled_norm(text_kv[:, :, 0], head_gains[3]).astype(jnp.bfloat16)
    cross_v = text_kv[:, :, 1].astype(jnp.bfloat16)
    cross_scores = (
        jnp.einsum("bqhd,bkhd->bhqk", cross_q, cross_k, preferred_element_type=jnp.float32)
        * score_scale
    )
    cross_top = jnp.max(cross_scores, axis=-1, keepdims=True)
    cross_exp = jnp.exp(cross_scores - cross_top)
    cross_total = jnp.sum(cross_exp, axis=-1, keepdims=True)
    cross_logsum = cross_top + jnp.log(cross_total)
    cross_mix = jnp.einsum(
        "bhqk,bkhd->bqhd",
        (cross_exp / cross_total).astype(jnp.bfloat16),
        cross_v,
        preferred_element_type=jnp.float32,
    ).astype(jnp.bfloat16)
    cross_flat = cross_mix.reshape(tokens, width)
    resid2 = resid1 + project(cross_flat, w_cout)
    normed3 = scaled_norm(resid2, norm_gains[3]).astype(jnp.bfloat16)
    upper = project(normed3, w_up)
    active = jax.nn.gelu(upper, approximate=True).astype(jnp.bfloat16)
    final = resid2 + project(active, w_down)
    block_out = final.astype(jnp.bfloat16).reshape(images, local, width)
    again_full = (
        lax.all_gather(skip_weight, "seq", axis=1, tiled=True),
        lax.all_gather(time_first, "seq", axis=1, tiled=True),
        lax.all_gather(time_second, "seq", axis=1, tiled=True),
        lax.all_gather(attn_qkv, "seq", axis=1, tiled=True),
        lax.all_gather(attn_out, "seq", axis=1, tiled=True),
        lax.all_gather(cross_qproj, "seq", axis=1, tiled=True),
        lax.all_gather(cross_kvproj, "seq", axis=1, tiled=True),
        lax.all_gather(cross_out, "seq", axis=1, tiled=True),
        lax.all_gather(text_proj, "seq", axis=1, tiled=True),
        lax.all_gather(mlp_up, "seq", axis=1, tiled=True),
        lax.all_gather(mlp_down, "seq", axis=1, tiled=True),
    )
    weight_set = (
        lax.all_gather(again_full[0], "dp", axis=0, tiled=True),
        lax.all_gather(again_full[1], "dp", axis=0, tiled=True),
        lax.all_gather(again_full[2], "dp", axis=0, tiled=True),
        lax.all_gather(again_full[3], "dp", axis=0, tiled=True),
        lax.all_gather(again_full[4], "dp", axis=0, tiled=True),
        lax.all_gather(again_full[5], "dp", axis=0, tiled=True),
        lax.all_gather(again_full[6], "dp", axis=0, tiled=True),
        lax.all_gather(again_full[7], "dp", axis=0, tiled=True),
        lax.all_gather(again_full[8], "dp", axis=0, tiled=True),
        lax.all_gather(again_full[9], "dp", axis=0, tiled=True),
        lax.all_gather(again_full[10], "dp", axis=0, tiled=True),
    )
    w_skip, w_first, w_second, w_qkv, w_aout, w_cq, w_ckv, w_cout, w_text, w_up, w_down = weight_set
    scaled_cot = (out_cot.astype(jnp.float32) * loss_weight[:, None, None]).reshape(tokens, width)
    grad_low = scaled_cot.astype(jnp.bfloat16)
    g_down = weight_grad(active, grad_low)
    d_active = project_back(grad_low, w_down)
    upper_vals, gelu_back = jax.vjp(lambda values: jax.nn.gelu(values, approximate=True), upper)
    d_upper = gelu_back(d_active)[0].astype(jnp.bfloat16)
    g_up = weight_grad(normed3, d_upper)
    d_normed3 = project_back(d_upper, w_up)
    norm_vals, norm_back = jax.vjp(scaled_norm, resid2, norm_gains[3])
    d_resid, d_gain3 = norm_back(d_normed3)
    resid_grad = scaled_cot + d_resid
    grad_low = resid_grad.astype(jnp.bfloat16)
    g_cout = weight_grad(cross_flat, grad_low)
    d_cmix = (
        project_back(grad_low, w_cout).astype(jnp.bfloat16).reshape(images, local, HEADS, HEAD_DIM)
    )
    cross_weights = jnp.exp(cross_scores - cross_logsum)
    d_cweights = jnp.einsum("bqhd,bkhd->bhqk", d_cmix, cross_v, preferred_element_type=jnp.float32)
    row_dot = jnp.sum(cross_weights * d_cweights, axis=-1, keepdims=True)
    d_cscores = (cross_weights * (d_cweights - row_dot)).astype(jnp.bfloat16)
    d_cquery = (
        jnp.einsum("bhqk,bkhd->bqhd", d_cscores, cross_k, preferred_element_type=jnp.float32)
        * score_scale
    ).astype(jnp.bfloat16)
    d_ckey = (
        jnp.einsum("bhqk,bqhd->bkhd", d_cscores, cross_q, preferred_element_type=jnp.float32)
        * score_scale
    )
    d_cval = jnp.einsum(
        "bhqk,bqhd->bkhd",
        cross_weights.astype(jnp.bfloat16),
        d_cmix,
        preferred_element_type=jnp.float32,
    )
    cq_vals, cq_back = jax.vjp(scaled_norm, cross_pre, head_gains[2])
    d_cpre, d_hgain2 = cq_back(d_cquery.astype(jnp.float32).reshape(tokens, HEADS, HEAD_DIM))
    d_cpre_low = d_cpre.reshape(tokens, width).astype(jnp.bfloat16)
    g_cquery = weight_grad(normed2, d_cpre_low)
    d_normed2 = project_back(d_cpre_low, w_cq)
    norm_vals, norm_back = jax.vjp(scaled_norm, resid1, norm_gains[2])
    d_resid, d_gain2 = norm_back(d_normed2)
    resid_grad = resid_grad + d_resid
    ck_vals, ck_back = jax.vjp(scaled_norm, text_kv[:, :, 0], head_gains[3])
    d_kpre, d_hgain3 = ck_back(d_ckey)
    d_textkv = (
        jnp.stack([d_kpre, d_cval], 2).reshape(images, text_len, 2 * width).astype(jnp.bfloat16)
    )
    g_ckv = jnp.einsum("btc,btd->cd", context, d_textkv, preferred_element_type=jnp.float32)
    d_context = jnp.einsum("btd,cd->btc", d_textkv, w_ckv, preferred_element_type=jnp.float32)
    d_proj = (d_context[:, clip_len:] * keep_text.astype(jnp.float32)[:, None, None]).astype(
        jnp.bfloat16
    )
    g_tproj = jnp.einsum("btc,btd->cd", mt5_text, d_proj, preferred_element_type=jnp.float32)
    grad_low = resid_grad.astype(jnp.bfloat16)
    g_aout = weight_grad(attn_flat, grad_low)
    d_attn = project_back(grad_low, w_aout).astype(jnp.bfloat16).reshape(images, local, width)
    d_heads = lax.all_to_all(d_attn, "seq", split_axis=2, concat_axis=1, tiled=True)

    def self_back(operand):
        queries, keyset, valueset, d_mixed, logsum = operand
        scores = (
            jnp.einsum("qd,kd->qk", queries, keyset, preferred_element_type=jnp.float32)
            * score_scale
        )
        weights = jnp.exp(scores - logsum[:, None])
        d_weights = jnp.einsum("qd,kd->qk", d_mixed, valueset, preferred_element_type=jnp.float32)
        row_sum = jnp.sum(weights * d_weights, axis=-1, keepdims=True)
        d_scores = (weights * (d_weights - row_sum)).astype(jnp.bfloat16)
        d_query = (
            jnp.einsum("qk,kd->qd", d_scores, keyset, preferred_element_type=jnp.float32)
            * score_scale
        )
        d_key = (
            jnp.einsum("qk,qd->kd", d_scores, queries, preferred_element_type=jnp.float32)
            * score_scale
        )
        d_value = jnp.einsum(
            "qk,qd->kd", weights.astype(jnp.bfloat16), d_mixed, preferred_element_type=jnp.float32
        )
        return (
            d_query.astype(jnp.bfloat16),
            d_key.astype(jnp.bfloat16),
            d_value.astype(jnp.bfloat16),
        )

    head_split = pieces.reshape(images, full_len, 3, heads_here, HEAD_DIM)
    triple_set = jnp.transpose(head_split, (2, 0, 3, 1, 4)).reshape(
        3, images * heads_here, full_len, HEAD_DIM
    )
    d_split = jnp.transpose(
        d_heads.reshape(images, full_len, heads_here, HEAD_DIM), (0, 2, 1, 3)
    ).reshape(images * heads_here, full_len, HEAD_DIM)
    d_query, d_key, d_value = lax.map(
        self_back,
        (
            triple_set[0],
            triple_set[1],
            triple_set[2],
            d_split,
            self_logsum.reshape(images * heads_here, full_len),
        ),
    )
    d_triple = jnp.stack([d_query, d_key, d_value], 0).reshape(
        3, images, heads_here, full_len, HEAD_DIM
    )
    d_triple = jnp.transpose(d_triple, (1, 3, 0, 2, 4)).reshape(images, full_len, 3, narrow)
    d_stacked = lax.all_to_all(d_triple, "seq", split_axis=1, concat_axis=3, tiled=True)
    d_packed_in = d_stacked.reshape(tokens, 3, HEADS, HEAD_DIM).astype(jnp.float32)
    q_vals, q_back = jax.vjp(query_prep, packed[:, 0], head_gains[0])
    d_qpre, d_hgain0 = q_back(d_packed_in[:, 0])
    k_vals, k_back = jax.vjp(query_prep, packed[:, 1], head_gains[1])
    d_kself, d_hgain1 = k_back(d_packed_in[:, 1])
    d_packed = (
        jnp.stack([d_qpre, d_kself, d_packed_in[:, 2]], 1)
        .reshape(tokens, 3 * width)
        .astype(jnp.bfloat16)
    )
    g_qkv = weight_grad(normed1, d_packed)
    d_normed1 = project_back(d_packed, w_qkv)
    d_shift = jnp.sum(d_normed1.reshape(images, local, width), axis=1)
    norm_vals, norm_back = jax.vjp(scaled_norm, resid0, norm_gains[1])
    d_resid, d_gain1 = norm_back(d_normed1)
    resid_grad = resid_grad + d_resid
    g_tsecond = jnp.einsum("bc,bd->cd", lifted.astype(jnp.float32), d_shift, precision=HIGHEST)
    d_lifted = jnp.einsum("bd,cd->bc", d_shift, w_second.astype(jnp.float32), precision=HIGHEST)
    silu_vals, silu_back = jax.vjp(jax.nn.silu, before)
    d_before = silu_back(d_lifted)[0]
    g_tfirst = jnp.einsum("bc,bd->cd", feats.astype(jnp.float32), d_before, precision=HIGHEST)
    norm_vals, norm_back = jax.vjp(scaled_norm, merged, norm_gains[0])
    d_merged, d_gain0 = norm_back(resid_grad)
    d_merged_low = d_merged.astype(jnp.bfloat16)
    g_skipw = weight_grad(joined, d_merged_low)
    d_joined = project_back(d_merged_low, w_skip)
    hidden_grad = d_joined[:, :width].reshape(images, local, width)
    skip_grad = d_joined[:, width:].reshape(images, local, width)
    row_sums = (
        lax.psum_scatter(
            g_skipw.astype(jnp.bfloat16), "dp", scatter_dimension=0, tiled=True
        ).astype(jnp.float32),
        lax.psum_scatter(
            g_tfirst.astype(jnp.bfloat16), "dp", scatter_dimension=0, tiled=True
        ).astype(jnp.float32),
        lax.psum_scatter(
            g_tsecond.astype(jnp.bfloat16), "dp", scatter_dimension=0, tiled=True
        ).astype(jnp.float32),
        lax.psum_scatter(g_qkv.astype(jnp.bfloat16), "dp", scatter_dimension=0, tiled=True).astype(
            jnp.float32
        ),
        lax.psum_scatter(g_aout.astype(jnp.bfloat16), "dp", scatter_dimension=0, tiled=True).astype(
            jnp.float32
        ),
        lax.psum_scatter(
            g_cquery.astype(jnp.bfloat16), "dp", scatter_dimension=0, tiled=True
        ).astype(jnp.float32),
        lax.psum_scatter(g_ckv.astype(jnp.bfloat16), "dp", scatter_dimension=0, tiled=True).astype(
            jnp.float32
        ),
        lax.psum_scatter(g_cout.astype(jnp.bfloat16), "dp", scatter_dimension=0, tiled=True).astype(
            jnp.float32
        ),
        lax.psum_scatter(
            g_tproj.astype(jnp.bfloat16), "dp", scatter_dimension=0, tiled=True
        ).astype(jnp.float32),
        lax.psum_scatter(g_up.astype(jnp.bfloat16), "dp", scatter_dimension=0, tiled=True).astype(
            jnp.float32
        ),
        lax.psum_scatter(g_down.astype(jnp.bfloat16), "dp", scatter_dimension=0, tiled=True).astype(
            jnp.float32
        ),
    )
    owned = (
        lax.psum_scatter(
            row_sums[0].astype(jnp.bfloat16), "seq", scatter_dimension=1, tiled=True
        ).astype(jnp.float32),
        lax.psum_scatter(
            row_sums[1].astype(jnp.bfloat16), "seq", scatter_dimension=1, tiled=True
        ).astype(jnp.float32),
        lax.psum_scatter(
            row_sums[2].astype(jnp.bfloat16), "seq", scatter_dimension=1, tiled=True
        ).astype(jnp.float32),
        lax.psum_scatter(
            row_sums[3].astype(jnp.bfloat16), "seq", scatter_dimension=1, tiled=True
        ).astype(jnp.float32),
        lax.psum_scatter(
            row_sums[4].astype(jnp.bfloat16), "seq", scatter_dimension=1, tiled=True
        ).astype(jnp.float32),
        lax.psum_scatter(
            row_sums[5].astype(jnp.bfloat16), "seq", scatter_dimension=1, tiled=True
        ).astype(jnp.float32),
        lax.psum_scatter(
            row_sums[6].astype(jnp.bfloat16), "seq", scatter_dimension=1, tiled=True
        ).astype(jnp.float32),
        lax.psum_scatter(
            row_sums[7].astype(jnp.bfloat16), "seq", scatter_dimension=1, tiled=True
        ).astype(jnp.float32),
        lax.psum_scatter(
            row_sums[8].astype(jnp.bfloat16), "seq", scatter_dimension=1, tiled=True
        ).astype(jnp.float32),
        lax.psum_scatter(
            row_sums[9].astype(jnp.bfloat16), "seq", scatter_dimension=1, tiled=True
        ).astype(jnp.float32),
        lax.psum_scatter(
            row_sums[10].astype(jnp.bfloat16), "seq", scatter_dimension=1, tiled=True
        ).astype(jnp.float32),
    )
    gain_totals = lax.psum(
        (
            jnp.stack([d_gain0, d_gain1, d_gain2, d_gain3], 0),
            jnp.stack([d_hgain0, d_hgain1, d_hgain2, d_hgain3], 0),
        ),
        ("dp", "seq"),
    )
    return (
        block_out,
        hidden_grad,
        skip_grad,
        owned[0],
        owned[1],
        owned[2],
        owned[3],
        owned[4],
        owned[5],
        owned[6],
        owned[7],
        owned[8],
        owned[9],
        owned[10],
        gain_totals[0],
        gain_totals[1],
    )


def solution(mesh):
    placed = (
        P("dp", "seq", None),
        P("dp", "seq", None),
        P("dp", None, None),
        P("dp", None, None),
        P("dp"),
        P("dp"),
        P("dp"),
        P(None, "dp", "seq"),
        P("dp", "seq", None),
        P("dp", "seq"),
        P("dp", "seq"),
        P("dp", "seq"),
        P("dp", "seq"),
        P("dp", "seq"),
        P("dp", "seq"),
        P("dp", "seq"),
        P("dp", "seq"),
        P("dp", "seq"),
        P("dp", "seq"),
        P("dp", "seq"),
        P(),
        P(),
    )
    return jax.shard_map(
        body,
        mesh=mesh,
        in_specs=placed,
        out_specs=(
            P("dp", "seq", None),
            P("dp", "seq", None),
            P("dp", "seq", None),
            P("dp", "seq"),
            P("dp", "seq"),
            P("dp", "seq"),
            P("dp", "seq"),
            P("dp", "seq"),
            P("dp", "seq"),
            P("dp", "seq"),
            P("dp", "seq"),
            P("dp", "seq"),
            P("dp", "seq"),
            P("dp", "seq"),
            P(),
            P(),
        ),
        check_vma=False,
    )
```

profile of v0, /device:TPU:0, one launch (start us, length us, event | category | flops | bytes accessed | tf_op | source)
XLA Modules:
  0.0 2478.4 jit_solution(2763180883298254115)
XLA Ops:
  104.7 26.3 %all_gather.87 = bf16[256,1408]{1,0:T(8,128)(2,1)S(1)} all-gather(bf16[16,1408]{1,0:T(8,128)(2,1)S(1)} %bitcast.589), channel_id=1, replica_groups=mesh['dp'=16,'seq'=2] {'dp'}, dimensions={0}, use_global_device_ids=true | all-gather | bytes 765952 | tf_op jit(solution)/shard_map/all_gather | solution.py:115
  136.4 70.7 %all-gather.23.cloned.1.call-done = bf16[2816,1408]{1,0:T(8,128)(2,1)} async-done(((bf16[176,1408]{1,0:T(8,128)(2,1)}), bf16[2816,1408]{1,0:T(8,128)(2,1)}) %all-gather.23.cloned.1.call-update) | async-done | bytes 7929872 | tf_op jit(solution)/shard_map/all_gather | solution.py:114
  218.4 86.2 %all-gather.27.cloned.1.call-done = bf16[1408,4224]{1,0:T(8,128)(2,1)} async-done(((bf16[88,4224]{1,0:T(8,128)(2,1)}), bf16[1408,4224]{1,0:T(8,128)(2,1)}) %all-gather.27.cloned.1.call-update) | async-done | bytes 11894800 | tf_op jit(solution)/shard_map/all_gather | solution.py:117
  365.0 50.3 %all-gather.33.cloned.1.call-done = bf16[1024,2816]{1,0:T(8,128)(2,1)} async-done(((bf16[64,2816]{1,0:T(8,128)(2,1)}), bf16[1024,2816]{1,0:T(8,128)(2,1)}) %all-gather.33.cloned.1.call-update) | async-done | bytes 5767184 | tf_op jit(solution)/shard_map/all_gather | solution.py:120
  473.2 51.7 %while.26 = (s32[]{:T(128)}, bf16[8,1024,88]{1,2,0:T(8,128)(2,1)}, f32[8,1024]{1,0:T(8,128)}, bf16[8,1024,88]{2,1,0:T(8,128)(2,1)S(1)}, bf16[8,1024,88]{2,1,0:T(...) while((s32[]{:T(128)}, bf16[8,1024,88]{1,2,0:T(8,128)(2,1)}, f32[8,1024]{1,0:T(8,128)}, ...), condition=%wide.region_11.12_spmd, body=%wide.region_8.11_spmd.sunk | while | flops 378625024 | bytes 13592673 | solution.py:170
  639.2 24.2 all-gather.45.cloned.1.call-done
  679.0 81.4 %all-gather.39.cloned.1.call-done = bf16[1408,6336]{1,0:T(8,128)(2,1)} async-done(((bf16[88,6336]{1,0:T(8,128)(2,1)}), bf16[1408,6336]{1,0:T(8,128)(2,1)}) %all-gather.39.cloned.1.call-update) | async-done | bytes 17842192 | tf_op jit(solution)/shard_map/all_gather | solution.py:123
  778.6 23.9 fusion.62
  912.2 22.1 all_to_all.54
  949.1 93.6 %while.27 = (s32[]{:T(128)}, bf16[8,1024,88]{1,2,0:T(8,128)(2,1)}, bf16[8,1024,88]{1,2,0:T(8,128)(2,1)}, bf16[8,1024,88]{1,2,0:T(8,128)(2,1)}, bf16[8,1024,88]{2...) while((s32[]{:T(128)}, bf16[8,1024,88]{1,2,0:T(8,128)(2,1)}, ...), condition=%wide.region_31.32_spmd, body=%wide.region_29.31_spmd.sunk | while | flops 935779328 | bytes 33703024 | solution.py:335
  1056.7 79.2 %all_to_all.55 = bf16[1,1024,3,704]{3,2,0,1:T(4,128)(2,1)} all-to-all(bf16[1,1024,3,704]{3,2,0,1:T(4,128)(2,1)} %copy.188), channel_id=1, replica_groups=mesh['dp'=16,'seq'=2] {'seq'}, dimensions={1} | all-to-all | bytes 8650752 | tf_op jit(solution)/shard_map/all_to_all | solution.py:349
  1320.3 198.1 %fusion = bf16[400,1408]{1,0:T(8,128)(2,1)S(1)} fusion(bf16[6336,1408]{1,0:T(8,128)(2,1)} %convolution_convert_fusion.1), kind=kCustom, calls=%all-reduce-scatter | all-reduce-scatter fusion | flops 9011201 | bytes 18969088
  1518.4 20.1 collective-permute-start
  1552.6 23.3 reduce-scatter.96.cloned.1.call-done
  1577.8 74.0 %reduce-scatter.82.cloned.1.call-done = bf16[128,1024]{1,0:T(8,128)(2,1)} async-done(((bf16[2048,1024]{1,0:T(8,128)(2,1)}), bf16[128,1024]{1,0:T(8,128)(2,1)}) %reduce-scatter.82.cloned.1.call-update) | async-done | bytes 262160
  1653.7 83.9 %reduce-scatter.88.cloned.1.call-done = bf16[88,1408]{1,0:T(8,128)(2,1)} async-done(((bf16[1408,1408]{1,0:T(8,128)(2,1)}), bf16[88,1408]{1,0:T(8,128)(2,1)}) %reduce-scatter.88.cloned.1.call-update) | async-done | bytes 247824
  1739.5 82.9 %reduce-scatter.60.cloned.1.call-done = bf16[64,2816]{1,0:T(8,128)(2,1)} async-done(((bf16[1024,2816]{1,0:T(8,128)(2,1)}), bf16[64,2816]{1,0:T(8,128)(2,1)}) %reduce-scatter.60.cloned.1.call-update) | async-done | bytes 360464 | tf_op jit(solution)/shard_map/reduce_scatter | solution.py:397
  1824.6 104.5 %reduce-scatter.56.cloned.1.call-done = bf16[176,1408]{1,0:T(8,128)(2,1)} async-done(((bf16[2816,1408]{1,0:T(8,128)(2,1)}), bf16[176,1408]{1,0:T(8,128)(2,1)}) %reduce-scatter.56.cloned.1.call-update) | async-done | bytes 495632 | tf_op jit(solution)/shard_map/reduce_scatter | solution.py:379
  1931.3 132.1 %reduce-scatter.90.cloned.1.call-done = bf16[88,4224]{1,0:T(8,128)(2,1)} async-done(((bf16[1408,4224]{1,0:T(8,128)(2,1)}), bf16[88,4224]{1,0:T(8,128)(2,1)}) %reduce-scatter.90.cloned.1.call-update) | async-done | bytes 743440
  2065.7 194.3 %reduce-scatter.64.cloned.1.call-done = bf16[88,6336]{1,0:T(8,128)(2,1)} async-done(((bf16[1408,6336]{1,0:T(8,128)(2,1)}), bf16[88,6336]{1,0:T(8,128)(2,1)}) %reduce-scatter.64.cloned.1.call-update) | async-done | bytes 1115152 | tf_op jit(solution)/shard_map/reduce_scatter | solution.py:406
  2262.7 20.4 fusion.75
  2289.2 40.1 %all-reduce.19 = (f32[4,1408]{1,0:T(4,128)}, f32[4,88]{1,0:T(4,128)}) all-reduce(f32[4,1408]{1,0:T(4,128)S(1)} %pad_maximum_fusion.6, f32[4,88]{1,0:T(4,128)S(1)} %pad_maximum_fusion.7), channel_id=1, replica_groups=mesh['dp'=16,'seq'=2] {'dp','seq'}, use_global_device_ids=true, to_apply=%region_69.70 | all-reduce | flops 5984 | bytes 47872 | tf_op jit(solution)/shard_map/psum | solution.py:448
  2418.4 21.6 reduce-scatter.72.cloned.1.call-done
  2442.2 26.5 %reduce-scatter.84.cloned.1.call-done = bf16[3168,88]{1,0:T(8,128)(2,1)} async-done(((bf16[6336,88]{1,0:T(8,128)(2,1)}), bf16[3168,88]{1,0:T(8,128)(2,1)}) %reduce-scatter.84.cloned.1.call-update) | async-done | bytes 557584
  (743 shorter events, 972.3 us)
Async XLA Ops:
  66.0 517.5 %all-gather.29.cloned.1.call-start = ((), (), s32[]{:S(2)}) async-start(), calls=%async_computation.28 | async-start | bytes 4212736 | tf_op jit(solution)/shard_map/all_gather | solution.py:118
  75.8 516.5 %all-gather.35.cloned.1.call-start = ((), (), s32[]{:S(2)}) async-start(), calls=%async_computation.31 | async-start | bytes 4212736 | tf_op jit(solution)/shard_map/all_gather | solution.py:119
  83.4 547.1 %all-gather.37.cloned.1.call-start = ((), (), s32[]{:S(2)}) async-start(), calls=%async_computation.32 | async-start | bytes 4212736 | tf_op jit(solution)/shard_map/all_gather | solution.py:121
  90.4 573.0 %all-gather.45.cloned.1.call-start = ((), (), s32[]{:S(2)}) async-start(), calls=%async_computation.41 | async-start | bytes 19148800 | tf_op jit(solution)/shard_map/all_gather | solution.py:124
  94.7 665.7 %all-gather.39.cloned.1.call-start = ((), (), s32[]{:S(2)}) async-start(), calls=%async_computation.33 | async-start | bytes 19148800 | tf_op jit(solution)/shard_map/all_gather | solution.py:123
  554.2 992.7 %reduce-scatter.58.cloned.1.call-start = ((), (), s32[]{:S(2)}) async-start(), calls=%async_computation.35 | async-start | bytes 765952 | tf_op jit(solution)/shard_map/reduce_scatter | solution.py:382
  1208.2 367.7 %reduce-scatter.96.cloned.1.call-start = ((), (), s32[]{:S(2)}) async-start(), calls=%async_computation.57 | async-start | bytes 4212736
  1215.2 436.6 %reduce-scatter.82.cloned.1.call-start = ((), (), s32[]{:S(2)}) async-start(), calls=%async_computation.50 | async-start | bytes 4456448
  1241.9 495.7 %reduce-scatter.88.cloned.1.call-start = ((), (), s32[]{:S(2)}) async-start(), calls=%async_computation.53 | async-start | bytes 4212736
  1245.1 577.3 %reduce-scatter.60.cloned.1.call-start = ((), (), s32[]{:S(2)}) async-start(), calls=%async_computation.36 | async-start | bytes 6127616 | tf_op jit(solution)/shard_map/reduce_scatter | solution.py:397
  1253.0 676.0 %reduce-scatter.56.cloned.1.call-start = ((), (), s32[]{:S(2)}) async-start(), calls=%async_computation.34 | async-start | bytes 8425472 | tf_op jit(solution)/shard_map/reduce_scatter | solution.py:379
  1267.8 795.5 %reduce-scatter.90.cloned.1.call-start = ((), (), s32[]{:S(2)}) async-start(), calls=%async_computation.54 | async-start | bytes 12638208
  1282.4 977.6 %reduce-scatter.64.cloned.1.call-start = ((), (), s32[]{:S(2)}) async-start(), calls=%async_computation.38 | async-start | bytes 19148800 | tf_op jit(solution)/shard_map/reduce_scatter | solution.py:406
  1300.5 986.2 %reduce-scatter.86.cloned.1.call-start = ((), (), s32[]{:S(2)}) async-start(), calls=%async_computation.52 | async-start | bytes 2162688
  1546.8 793.8 %reduce-scatter.68.cloned.1.call-start = ((), (), s32[]{:S(2)}) async-start(), calls=%async_computation.43 | async-start | bytes 540672
  1548.6 793.7 %reduce-scatter.74.cloned.1.call-start = ((), (), s32[]{:S(2)}) async-start(), calls=%async_computation.46 | async-start | bytes 540672
  1550.6 793.5 %reduce-scatter.76.cloned.1.call-start = ((), (), s32[]{:S(2)}) async-start(), calls=%async_computation.47 | async-start | bytes 540672
  1552.5 795.1 %reduce-scatter.80.cloned.1.call-start = ((), (), s32[]{:S(2)}) async-start(), calls=%async_computation.49 | async-start | bytes 540672
  1577.8 784.5 %reduce-scatter.62.cloned.1.call-start = ((), (), s32[]{:S(2)}) async-start(), calls=%async_computation.37 | async-start | bytes 393216 | tf_op jit(solution)/shard_map/reduce_scatter | solution.py:438
  1653.7 724.2 %reduce-scatter.70.cloned.1.call-start = ((), (), s32[]{:S(2)}) async-start(), calls=%async_computation.44 | async-start | bytes 540672
  1739.4 657.3 %reduce-scatter.78.cloned.1.call-start = ((), (), s32[]{:S(2)}) async-start(), calls=%async_computation.48 | async-start | bytes 1081344
  1824.5 591.9 %reduce-scatter.66.cloned.1.call-start = ((), (), s32[]{:S(2)}) async-start(), calls=%async_computation.42 | async-start | bytes 1081344
  1931.2 508.8 %reduce-scatter.72.cloned.1.call-start = ((), (), s32[]{:S(2)}) async-start(), calls=%async_computation.45 | async-start | bytes 1622016
  2065.7 403.1 %reduce-scatter.84.cloned.1.call-start = ((), (), s32[]{:S(2)}) async-start(), calls=%async_computation.51 | async-start | bytes 2433024
  (164 other events, 9710.3 us)
Sparse Core Ops, SparseCore 0:
  9.6 34.2 all-gather.42
  45.4 29.4 all-gather.40
  77.7 55.8 all-gather.24
  136.2 70.8 all-gather.22
  209.6 94.8 all-gather.26
  306.5 48.8 all-gather.30
  357.7 57.5 all-gather.32
  418.0 47.5 all-gather.28
  468.4 48.0 all-gather.34
  519.1 47.9 all-gather.36
  569.3 94.0 all-gather.44
  665.4 94.9 all-gather.38
  1194.4 53.9 reduce-scatter.57
  1252.6 83.2 reduce-scatter.91
  1340.0 139.1 reduce-scatter.93
  1483.4 92.4 reduce-scatter.95
  1580.1 71.6 reduce-scatter.81
  1655.5 81.9 reduce-scatter.87
  1741.5 80.8 reduce-scatter.59
  1826.2 102.7 reduce-scatter.55
  1933.7 129.5 reduce-scatter.89
  2067.4 192.6 reduce-scatter.63
  2262.9 23.7 reduce-scatter.85
  2442.1 26.6 reduce-scatter.83
  (9 shorter events, 129.5 us)
where the time goes:
time: 2490 us; the launch traced here: 2480 us
  waiting for transfers between devices  1140 us (46%)
  blocking collectives  443 us (18%)
  matrix products  404 us (16%)
  local copies, waits for them, and re-layouts  310 us (12%)
  other arithmetic  129 us (5%)
  starting transfers between devices  32.1 us (1%)
    unnamed x50, waiting for transfers between devices  417 us
    unnamed x1, blocking collectives  198 us
    reduce_scatter x1, waiting for transfers between devices, body(): lax.psum_scatter(g_up.astype(jnp.bfloat16), 'dp', scatter_dimension=0, ti...  194 us
    unnamed x348, local copies, waits for them, and re-layouts  121 us
    reduce_scatter x1, waiting for transfers between devices, body(): lax.psum_scatter(g_skipw.astype(jnp.bfloat16), 'dp', scatter_dimension=0,...  104 us
    dot_general x9, matrix products, project(): jnp.einsum('tc,cd->td', left, right, preferred_element_type=jnp.float32)  88 us
    all_gather x1, waiting for transfers between devices, body(): lax.all_gather(col_full[3], 'dp', axis=0, tiled=True)  86.2 us
    reduce_scatter x1, waiting for transfers between devices, body(): lax.psum_scatter(g_ckv.astype(jnp.bfloat16), 'dp', scatter_dimension=0, t...  82.9 us
  transfers between devices with their start and end apart: 36, of which 22 were waited for; matrix products, arithmetic and copies ran while one was open for 28% of the time, Pallas kernels for 0%

commit v1 on v0

--- a/solution.py
+++ b/solution.py
@@ -472,6 +472,692 @@
     )
 
 
+BOTH = ("dp", "seq")
+FLIP = [(0, 1), (1, 0)]
+LOG2E = 1.4426950408889634
+LANES = 128
+
+
+def swap(value, bit):
+    return lax.ppermute(value, "dp", [(i, i ^ bit) for i in range(16)])
+
+
+def swap_seq(value):
+    return lax.ppermute(value, "seq", FLIP)
+
+
+def core_holds(dp_index, seq_index):
+    return dp_index % 2 == dp_index // 8
+
+
+def seq_holds(dp_index, seq_index):
+    return seq_index == dp_index // 8
+
+
+def hop_pairs(holds, outward):
+    pairs = []
+    for i in range(16):
+        for s in range(2):
+            if holds(i, s):
+                there = ((i ^ 8) * 2 + s, i * 2 + s)
+                pairs.append(there[::-1] if outward else there)
+    return pairs
+
+
+def corner_pairs(outward):
+    first, second = [], []
+    for i in range(16):
+        h = i // 8
+        base = i - i % 2
+        if i % 2 == 0:
+            for core in range(2):
+                source = (base + core) * 2 + h
+                first.append((source, (base + 1 - core) * 2 + core))
+            core = 1 - h
+            second.append(((base + core) * 2 + h, (base + core) * 2 + 1 - h))
+    if not outward:
+        return [p[::-1] for p in first], [p[::-1] for p in second]
+    return first, second
+
+
+def pair(flag, own, other, axis=0):
+    return jnp.where(
+        flag == 0,
+        jnp.concatenate([own, other], axis),
+        jnp.concatenate([other, own], axis),
+    )
+
+
+def pick(flag, first, second):
+    return jnp.where(flag == 0, first, second)
+
+
+class Spot:
+    def __init__(self):
+        self.d = lax.axis_index("dp")
+        self.y = lax.axis_index("seq")
+        self.z = self.d // 4
+        self.x = (self.d // 2) % 2
+        self.c = self.d % 2
+        self.b = self.z % 2
+        self.h = self.z // 2
+
+
+class Flow:
+    def __init__(self):
+        self.chains = {}
+        self.done = {}
+
+    def add(self, name, chain):
+        self.chains[name] = [chain, None, next(chain)]
+
+    def step(self, values, names):
+        for name in names:
+            entry = self.chains[name]
+            if entry[1] is not None:
+                try:
+                    entry[1:] = [None, entry[0].send(entry[1])]
+                except StopIteration as end:
+                    self.done[name] = end.value
+                    del self.chains[name]
+        moving = [name for name in names if name in self.chains]
+        arrays = [[array for _, array in self.chains[name][2]] for name in moving]
+        ended = [self.done[name] for name in names if name in self.done]
+        values, arrays, ended = lax.optimization_barrier((list(values), arrays, ended))
+        for name, value in zip([n for n in names if n in self.done], ended):
+            self.done[name] = value
+        for name, given in zip(moving, arrays):
+            entry = self.chains[name]
+            entry[1] = [route(array) for (route, _), array in zip(entry[2], given)]
+        return values
+
+    def finish(self, name):
+        while name in self.chains:
+            self.step([], [name])
+        return self.done[name]
+
+
+def by_core(value):
+    return swap(value, 1)
+
+
+def by_x(value):
+    return swap(value, 2)
+
+
+def by_z(value):
+    return swap(value, 4)
+
+
+def by_routes(pairs):
+    return lambda value: lax.ppermute(value, BOTH, pairs)
+
+
+def join(parts):
+    if len(parts) == 1:
+        return parts[0].astype(jnp.bfloat16)
+    return jnp.concatenate([part.astype(jnp.float32) for part in parts], axis=1).astype(
+        jnp.bfloat16
+    )
+
+
+def assemble(spot, sources, spans, over_seq, x_first):
+    count = len(sources) // 2
+
+    def piece(level, i, j):
+        near = sources[level * count : (level + 1) * count]
+        if not over_seq:
+            return choose(choose(near[0], 0, i), 0, j)
+        if x_first:
+            parts = [choose(choose(source, 0, i), 0, j) for source in near]
+        else:
+            both = jnp.where(i == 0, choose(near[0], 1, j), choose(near[1], 1, j))
+            parts = [both[0], both[1]]
+        return pair(spot.y, parts[0], parts[1], 1)
+
+    blocks = []
+    for f in range(2):
+        for j in range(2):
+            for i in range(2):
+                place = i ^ spot.x, j ^ spot.b
+                blocks.append(jnp.where(spot.c == f, piece(0, *place), piece(1, *place)))
+    outs, at = [], 0
+    for span in spans:
+        outs.append(jnp.concatenate([block[at : at + span] for block in blocks], 0))
+        at += span
+    return outs
+
+
+def assemble_columns(spot, own, other):
+    whole = pair(spot.c, own, other, 2)
+    return pair(spot.b, whole[0], whole[1], 0)
+
+
+def gather_rows(spot, shards):
+    mates = yield [(by_core, shard) for shard in shards]
+    blocks = [pair(spot.c, s, m) for s, m in zip(shards, mates)]
+    hop = by_routes(hop_pairs(core_holds, True))
+    fars = yield [(hop, block) for block in blocks]
+    blocks = [jnp.where(spot.c == spot.h, block, far) for block, far in zip(blocks, fars)]
+    nears = yield [(by_z, block) for block in blocks]
+    lines = [jnp.stack([block, near]) for block, near in zip(blocks, nears)]
+    sides = yield [(by_x, line) for line in lines]
+    owns = [jnp.stack([line, side]) for line, side in zip(lines, sides)]
+    fars = yield [(by_core, own) for own in owns]
+    return [
+        assemble(spot, [own, far], [own.shape[2]], False, True)[0] for own, far in zip(owns, fars)
+    ]
+
+
+def gather_both(spot, shards, x_first):
+    mates = yield [(by_core, jnp.concatenate(shards, 0))]
+    at, blocks = 0, []
+    for shard in shards:
+        rows = shard.shape[0]
+        blocks.append(pair(spot.c, shard, mates[0][at : at + rows]))
+        at += rows
+    block = jnp.concatenate(blocks, 0)
+    (far,) = yield [(by_routes(hop_pairs(core_holds, True)), block)]
+    block = jnp.where(spot.c == spot.h, block, far)
+    (near,) = yield [(by_z, block)]
+    line = jnp.stack([block, near])
+    (side,) = yield [(by_x if x_first else swap_seq, line)]
+    own = jnp.stack([line, side])
+    (other,) = yield [(swap_seq if x_first else by_x, own)]
+    fars = yield [(by_core, own), (by_core, other)]
+    return assemble(spot, [own, other, *fars], [b.shape[0] for b in blocks], True, x_first)
+
+
+def gather_down(spot, shard):
+    first, second = corner_pairs(False)
+    crossed, across = yield [(by_routes(first), shard), (by_routes(second), shard)]
+    mine = jnp.where(spot.c == spot.y, shard, across)
+    block = pair(spot.c, mine, crossed)
+    (far,) = yield [(by_routes(hop_pairs(seq_holds, True)), block)]
+    block = jnp.where(spot.y == spot.h, block, far)
+    (near,) = yield [(by_z, block)]
+    line = jnp.stack([block, near])
+    (side,) = yield [(by_x, line)]
+    own = pair(spot.x, line, side, 1)
+    (other,) = yield [(by_core, own)]
+    return assemble_columns(spot, own, other)
+
+
+def narrow(value):
+    return value.astype(jnp.bfloat16)
+
+
+def wide(value):
+    return value.astype(jnp.float32)
+
+
+def choose(value, axis, index):
+    return lax.dynamic_index_in_dim(value, index, axis, keepdims=False)
+
+
+def dot_rows(left, right):
+    return jnp.einsum("tc,td->cd", left, right, preferred_element_type=jnp.float32)
+
+
+def settle_x(spot, part):
+    (given,) = yield [(by_x, choose(part, 1, 1 - spot.x))]
+    return narrow(wide(choose(part, 1, spot.x)) + wide(given))
+
+
+def settle_z(spot, part, holds):
+    (given,) = yield [(by_z, choose(part, 0, 1 - spot.b))]
+    block = wide(choose(part, 0, spot.b)) + wide(given)
+    (given,) = yield [(by_routes(hop_pairs(holds, False)), narrow(block))]
+    return block + wide(given)
+
+
+def split_rows(spot, block):
+    pieces = block.reshape(2, block.shape[0] // 2, block.shape[1])
+    (given,) = yield [(by_core, narrow(choose(pieces, 0, 1 - spot.c)))]
+    return jnp.where(spot.c == spot.h, choose(pieces, 0, spot.c), wide(given))
+
+
+def quarters(own):
+    rows, cols = own.shape
+    return own.reshape(2, 2, rows // 4, cols)
+
+
+def reduce_both(spot, halves, grads):
+    mine = pick(spot.c, halves[0], halves[1])
+    theirs = pick(spot.c, halves[1], halves[0])
+    grad_own = pick(spot.y, grads[0], grads[1])
+    grad_other = pick(spot.y, grads[1], grads[0])
+    given = yield [(by_core, narrow(dot_rows(theirs, g))) for g in (grad_own, grad_other)]
+    own = dot_rows(mine, grad_own) + wide(given[0])
+    other = dot_rows(mine, grad_other) + wide(given[1])
+    (given,) = yield [(swap_seq, narrow(other))]
+    part = quarters(narrow(own + wide(given)))
+    part = yield from settle_x(spot, part)
+    block = yield from settle_z(spot, part, core_holds)
+    return (yield from split_rows(spot, block))
+
+
+def reduce_rows(spot, halves, grad):
+    mine = pick(spot.c, halves[0], halves[1])
+    theirs = pick(spot.c, halves[1], halves[0])
+    (given,) = yield [(by_core, narrow(dot_rows(theirs, grad)))]
+    part = quarters(narrow(dot_rows(mine, grad) + wide(given)))
+    part = yield from settle_x(spot, part)
+    block = yield from settle_z(spot, part, core_holds)
+    return (yield from split_rows(spot, block))
+
+
+def reduce_down(spot, left, grads):
+    mine = pick(spot.c, grads[0], grads[1])
+    theirs = pick(spot.c, grads[1], grads[0])
+    (given,) = yield [(by_core, narrow(dot_rows(left, theirs)))]
+    part = quarters(narrow(dot_rows(left, mine) + wide(given)))
+    part = yield from settle_x(spot, part)
+    block = yield from settle_z(spot, part, seq_holds)
+    pieces = block.reshape(2, block.shape[0] // 2, block.shape[1])
+    same, cross = choose(pieces, 0, spot.c), choose(pieces, 0, 1 - spot.c)
+    first, second = corner_pairs(True)
+    crossed, across = yield [(by_routes(first), narrow(cross)), (by_routes(second), narrow(same))]
+    inner = jnp.where(spot.y == spot.h, same, wide(across))
+    return jnp.where(spot.c == spot.y, inner, wide(crossed))
+
+
+def total_over_all(value):
+    for bit in (1, 2, 4, 8):
+        value = value + swap(value, bit)
+    return value + swap_seq(value)
+
+
+def gather_images(spot, value):
+    for bit, flag in ((1, spot.c), (2, spot.x), (4, spot.b), (8, spot.h)):
+        value = pair(flag, value, swap(value, bit))
+    return value
+
+
+def partner(lane):
+    quarter = HEAD_DIM // 4
+    return jnp.where((lane // quarter) % 2 == 0, lane + quarter, lane - quarter)
+
+
+def attend(q_src, kv_src, gains, cosine, sine, heads, q_at, k_at, v_at, keys):
+    width = heads * HEAD_DIM
+
+    def heads_of(source, at):
+        return source[:, at : at + width].reshape(source.shape[0], heads, HEAD_DIM)
+
+    def prepared(source, at, which):
+        v = normalize(heads_of(source, at)) * gains[which]
+        if cosine is not None:
+            other = v[..., partner(jnp.arange(HEAD_DIM))]
+            v = v * cosine[:, None, :HEAD_DIM] + other * sine[:, None, :HEAD_DIM]
+        return v.astype(jnp.bfloat16)
+
+    q, k = prepared(q_src, q_at, 0), prepared(kv_src, k_at, 1)
+    v = heads_of(kv_src, v_at).astype(jnp.bfloat16)
+    s = jnp.einsum("qhd,khd->hqk", q, k, preferred_element_type=jnp.float32) * HEAD_DIM**-0.5
+    s = jnp.where(jnp.arange(kv_src.shape[0]) < keys, s, -1e9)
+    p = jax.nn.softmax(s, axis=-1).astype(jnp.bfloat16)
+    o = jnp.einsum("hqk,khd->qhd", p, v, preferred_element_type=jnp.float32)
+    return o.reshape(q_src.shape[0], width)
+
+
+def attend_forward(
+    q_src, kv_src, cosine, sine, gains, helpers, heads, q_at, k_at, v_at, keys
+):
+    q32, kv32 = q_src.astype(jnp.float32), kv_src.astype(jnp.float32)
+    o, back = jax.vjp(
+        lambda a, b, g: attend(a, b, g, cosine, sine, heads, q_at, k_at, v_at, keys),
+        q32,
+        kv32,
+        gains[:2, :HEAD_DIM],
+    )
+    return narrow(o), back, None, None
+
+
+def attend_backward(
+    q_src, kv_src, cosine, sine, gains, helpers, back, kn, vn, out, grad_out, heads, q_at, k_at, v_at
+):
+    dq, dk, dg = back(grad_out.astype(jnp.float32))
+    dg = jnp.pad(dg * gains[:2, :HEAD_DIM], ((0, 0), (0, LANES - HEAD_DIM)))
+    if q_src is kv_src:
+        return narrow(dq + dk), dg
+    return narrow(dq), narrow(dk), dg
+
+
+def rope_tables(pos_rows, pos_cols):
+    quarter = HEAD_DIM // 4
+    frequency = 10000.0 ** (-jnp.arange(quarter, dtype=jnp.float32) / quarter)
+    row_angles = pos_rows[:, None] * frequency[None, :]
+    col_angles = pos_cols[:, None] * frequency[None, :]
+    angles = jnp.concatenate([row_angles, row_angles, col_angles, col_angles], -1)
+    sign = jnp.where((jnp.arange(HEAD_DIM) // quarter) % 2 == 0, -1.0, 1.0)
+    wide = ((0, 0), (0, LANES - HEAD_DIM))
+    return jnp.pad(jnp.cos(angles), wide), jnp.pad(jnp.sin(angles) * sign[None, :], wide)
+
+
+def gain_rows(gains):
+    lane = jnp.arange(HEAD_DIM)
+    return jnp.pad(
+        jnp.concatenate([gains, gains[:, partner(lane)]], 0), ((0, 0), (0, LANES - HEAD_DIM))
+    )
+
+
+def gelu(values):
+    return jax.nn.gelu(values, approximate=True)
+
+
+def halves_of(value):
+    mid = value.shape[1] // 2
+    return value[:, :mid], value[:, mid:]
+
+
+def norm_parts(values):
+    center = values - jnp.mean(values, axis=-1, keepdims=True)
+    scale = lax.rsqrt(jnp.mean(center * center, axis=-1, keepdims=True) + EPSILON)
+    return center * scale, scale
+
+
+def norm_grad(grad, values, gain):
+    normal, scale = norm_parts(values)
+    gain_grad = jnp.sum(grad * normal, axis=0)
+    grad = grad * gain
+    mean = jnp.mean(grad, axis=-1, keepdims=True)
+    mean_product = jnp.mean(grad * normal, axis=-1, keepdims=True)
+    return scale * (grad - mean - normal * mean_product), gain_grad
+
+
+def fast_body(
+    hidden_in,
+    skip_in,
+    clip_text,
+    mt5_text,
+    time_ids,
+    null_text,
+    loss_weight,
+    patch_pos,
+    out_cot,
+    skip_weight,
+    time_first,
+    time_second,
+    attn_qkv,
+    attn_out,
+    cross_qproj,
+    cross_kvproj,
+    cross_out,
+    text_proj,
+    mlp_up,
+    mlp_down,
+    norm_gains,
+    head_gains,
+):
+    spot = Spot()
+    _, local, width = hidden_in.shape
+    narrow_width = width // 2
+    heads_here = HEADS // 2
+    clip_len = clip_text.shape[1]
+    text_len = clip_len + mt5_text.shape[1]
+    text_pad = -(-text_len // LANES) * LANES
+    y = spot.y
+    bf16 = jnp.bfloat16
+
+    time_rows = lax.all_gather(jnp.concatenate([time_first, time_second], 0), "dp")
+    time_cut = time_first.shape[0]
+    time_weights = [
+        rows.reshape(-1, narrow_width) for rows in (time_rows[:, :time_cut], time_rows[:, time_cut:])
+    ]
+    flow = Flow()
+    hidden = hidden_in[0]
+    skip = skip_in[0]
+    scaled_cot = out_cot[0].astype(jnp.float32) * loss_weight[0]
+    cot_low = narrow(scaled_cot)
+    pos = patch_pos[:, 0].astype(jnp.float32)
+    pos_far = swap_seq(pos)
+
+    def both_halves(value, axis=1):
+        return pair(y, value, swap_seq(value), axis)
+
+    a, m, e = (attn_qkv[:, i * narrow_width : (i + 1) * narrow_width] for i in range(3))
+    moved = swap_seq(m)
+    qkv_shard = jnp.concatenate([pick(y, a, moved), pick(y, e, a), pick(y, moved, e)], 1)
+
+    flow.add("skip", gather_both(spot, [skip_weight], False))
+    flow.add("qkv", gather_rows(spot, [qkv_shard]))
+    flow.add("text", gather_rows(spot, [text_proj, cross_kvproj]))
+    flow.add("outs", gather_both(spot, [attn_out, cross_qproj, cross_out], False))
+    flow.add("up", gather_rows(spot, [mlp_up]))
+    flow.add("down", gather_down(spot, mlp_down))
+    flow.step([], ["skip", "qkv", "text", "outs", "up", "down"])
+    flow.step([], ["skip"])
+    flow.step([], ["skip", "qkv"])
+    flow.step([], ["skip", "qkv", "text"])
+    cot_far = swap_seq(cot_low)
+    flow.step([], ["skip", "text", "outs"])
+    flow.step([], ["skip", "qkv", "outs", "up"])
+
+    feats = time_features(time_ids).astype(bf16)
+    before = both_halves(project(feats, time_weights[0]))
+    lifted = jax.nn.silu(before).astype(bf16)
+    shift = both_halves(project(lifted, time_weights[1]))
+
+    cosine, sine = rope_tables(*jnp.concatenate([pos, pos_far], 1))
+    helpers = []
+    hidden, skip, cot_far = flow.step([hidden, skip, cot_far], ["skip", "qkv", "text", "outs"])
+    (w_skip,) = flow.done["skip"]
+    w_hidden, w_far = w_skip[:width], w_skip[width:]
+    merged = project(hidden, w_hidden) + project(skip, w_far)
+    resid0 = scaled_norm(merged, norm_gains[0])
+    normed1 = narrow(scaled_norm(resid0, norm_gains[1]) + shift)
+    (normed1,) = flow.step([normed1], ["qkv", "text", "up", "down"])
+    (w_qkv,) = flow.done["qkv"]
+
+    normed1_both = jnp.concatenate([normed1, swap_seq(normed1)], 0)
+    packed = narrow(project(normed1_both, w_qkv))
+    self_gains = gain_rows(head_gains[0:2])
+    (packed,) = flow.step([packed], ["outs", "down", "text"])
+    self_o, self_q, self_k, self_v = attend_forward(
+        packed,
+        packed,
+        cosine,
+        sine,
+        self_gains,
+        helpers,
+        heads_here,
+        0,
+        narrow_width,
+        2 * narrow_width,
+        2 * local,
+    )
+    (self_o,) = flow.step([self_o], ["outs", "up", "down"])
+    far_o = swap_seq(self_o[local:])
+
+    w_text, w_ckv = flow.done["text"]
+    keep_text = (1 - null_text[0]).astype(bf16)
+    projected = both_halves(narrow(project(mt5_text[0], w_text)))
+    context = jnp.concatenate([clip_text[0], projected], 0) * keep_text
+    context = jnp.pad(context, ((0, text_pad - text_len), (0, 0)))
+    text_kv = both_halves(narrow(project(context, w_ckv)))
+    text_kv, own_o, far_o = flow.step([text_kv, self_o[:local], far_o], ["outs", "up", "down"])
+
+    w_aout, w_cq, w_cout = flow.done["outs"]
+    attn_halves = pick(y, own_o, far_o), pick(y, far_o, own_o)
+    attn_flat = jnp.concatenate(attn_halves, 1)
+    resid1 = resid0 + project(attn_flat, w_aout)
+    normed2 = narrow(scaled_norm(resid1, norm_gains[2]))
+    cross_pre = narrow(project(normed2, w_cq))
+    cross_gains = gain_rows(head_gains[2:4])
+    cross_o, cross_q, cross_k, cross_v = attend_forward(
+        cross_pre, text_kv, None, None, cross_gains, helpers, HEADS, 0, 0, width, text_len
+    )
+    resid2 = resid1 + project(cross_o, w_cout)
+    normed3 = narrow(scaled_norm(resid2, norm_gains[3]))
+    (normed3,) = flow.step([normed3], ["up", "down"])
+    w_up, w_down = flow.finish("up")[0], flow.finish("down")
+
+    normed3_both = jnp.concatenate([normed3, swap_seq(normed3)], 0)
+    upper = narrow(project(normed3_both, w_up))
+    active = narrow(gelu(upper.astype(jnp.float32)))
+    mixed = project(active, w_down)
+    final = resid2 + mixed[:local] + wide(swap_seq(narrow(mixed[local:])))
+    block_out = narrow(lax.optimization_barrier(final))[None]
+
+    cot_both = jnp.concatenate([cot_low, cot_far], 0)
+    d_active = project_back(cot_both, w_down)
+    _, gelu_back = jax.vjp(gelu, upper.astype(jnp.float32))
+    d_upper = narrow(gelu_back(d_active)[0])
+    flow.add("g_down", reduce_down(spot, active, halves_of(cot_both)))
+    (d_upper,) = flow.step([d_upper], ["g_down"])
+    d_both = project_back(d_upper, w_up)
+    d_far = swap_seq(narrow(d_both[local:]))
+    flow.add("g_up", reduce_rows(spot, halves_of(normed3_both), d_upper))
+    d_own, d_far = flow.step([d_both[:local], d_far], ["g_down", "g_up"])
+    d_normed3 = d_own + wide(d_far)
+    d_resid, d_gain3 = norm_grad(d_normed3, resid2, norm_gains[3])
+    resid_grad = scaled_cot + d_resid
+
+    grad_low = narrow(resid_grad)
+    d_cmix = narrow(project_back(grad_low, w_cout))
+    flow.add("g_cout", reduce_both(spot, halves_of(cross_o), halves_of(grad_low)))
+    (d_cmix,) = flow.step([d_cmix], ["g_cout"])
+    d_cpre, d_textkv, d_cross_gains = attend_backward(
+        cross_pre,
+        text_kv,
+        None,
+        None,
+        cross_gains,
+        helpers,
+        cross_q,
+        cross_k,
+        cross_v,
+        cross_o,
+        d_cmix,
+        HEADS,
+        0,
+        0,
+        width,
+    )
+    flow.add("g_cquery", reduce_both(spot, halves_of(normed2), halves_of(d_cpre)))
+    d_cpre, d_textkv = flow.step([d_cpre, d_textkv], ["g_down", "g_up", "g_cout", "g_cquery"])
+    d_text = halves_of(d_textkv)
+    d_text_far = swap_seq(pick(y, d_text[1], d_text[0]))
+    d_normed2 = project_back(d_cpre, w_cq)
+    d_resid, d_gain2 = norm_grad(d_normed2, resid1, norm_gains[2])
+    resid_grad = resid_grad + d_resid
+    grad_low = narrow(resid_grad)
+    d_attn = halves_of(narrow(project_back(grad_low, w_aout)))
+    d_far = swap_seq(pick(y, d_attn[1], d_attn[0]))
+    d_text = narrow(wide(pick(y, d_text[0], d_text[1])) + wide(d_text_far))
+    flow.add("g_aout", reduce_both(spot, attn_halves, halves_of(grad_low)))
+    flow.add("g_ckv", reduce_rows(spot, halves_of(context), d_text))
+    d_context = halves_of(project_back(d_text[clip_len:text_len], w_ckv))
+    d_context_far = swap_seq(narrow(pick(y, d_context[1], d_context[0])))
+    d_proj = pick(y, d_context[0], d_context[1]) + wide(d_context_far)
+    d_proj = narrow(d_proj * keep_text.astype(jnp.float32))
+    flow.add("g_tproj", reduce_rows(spot, halves_of(mt5_text[0]), d_proj))
+
+    d_heads = jnp.concatenate([pick(y, d_attn[0], d_attn[1]), d_far], 0)
+    (d_heads,) = flow.step(
+        [d_heads], ["g_down", "g_cout", "g_cquery", "g_aout", "g_ckv", "g_tproj"]
+    )
+    d_packed, d_self_gains = attend_backward(
+        packed,
+        packed,
+        cosine,
+        sine,
+        self_gains,
+        helpers,
+        self_q,
+        self_k,
+        self_v,
+        self_o,
+        d_heads,
+        heads_here,
+        0,
+        narrow_width,
+        2 * narrow_width,
+    )
+    (d_packed,) = flow.step(
+        [d_packed], ["g_down", "g_up", "g_cout", "g_cquery", "g_aout", "g_ckv", "g_tproj"]
+    )
+    d_both = project_back(d_packed, w_qkv)
+    d_far = swap_seq(narrow(d_both[local:]))
+    flow.add("g_qkv", reduce_rows(spot, halves_of(normed1_both), d_packed))
+    d_own, d_far = flow.step(
+        [d_both[:local], d_far],
+        ["g_up", "g_cout", "g_cquery", "g_aout", "g_ckv", "g_tproj", "g_qkv"],
+    )
+    d_normed1 = d_own + wide(d_far)
+
+    d_shift = jnp.sum(d_normed1, axis=0)
+    d_resid, d_gain1 = norm_grad(d_normed1, resid0, norm_gains[1])
+    resid_grad = resid_grad + d_resid
+    d_merged, d_gain0 = norm_grad(resid_grad, merged, norm_gains[0])
+    d_merged = narrow(d_merged)
+    flow.add("g_skip", reduce_both(spot, (hidden, skip), halves_of(d_merged)))
+    (d_merged,) = flow.step(
+        [d_merged],
+        ["g_skip", "g_up", "g_cout", "g_cquery", "g_aout", "g_ckv", "g_tproj", "g_qkv"],
+    )
+    hidden_grad = project_back(d_merged, w_hidden)[None]
+    skip_grad = project_back(d_merged, w_far)[None]
+
+    d_shift = d_shift + swap_seq(d_shift)
+    features = jnp.pad(feats.astype(jnp.float32), ((0, 0), (0, width - FREQ)))
+    rows = gather_images(spot, jnp.stack([before[0], features[0], d_shift], 0)[None])
+    before_all, features_all, d_shift_all = rows[:, 0], rows[:, 1, :FREQ], rows[:, 2]
+    silu_all, silu_back = jax.vjp(jax.nn.silu, before_all)
+    lifted_all = wide(narrow(silu_all))
+    d_shift_cols = pick(y, *halves_of(d_shift_all))
+    d_lifted = jnp.einsum(
+        "bd,cd->bc", d_shift_cols, time_weights[1].astype(jnp.float32), precision=HIGHEST
+    )
+    d_before = silu_back(d_lifted + swap_seq(d_lifted))[0]
+
+    def block(left, cols, left_rows):
+        mine = lax.dynamic_slice_in_dim(left, spot.d * left_rows, left_rows, 1)
+        return jnp.einsum("bc,bd->cd", mine, cols, precision=HIGHEST)
+
+    g_tsecond = block(lifted_all, d_shift_cols, time_second.shape[0])
+    g_tfirst = block(features_all, pick(y, *halves_of(d_before)), time_first.shape[0])
+
+    d_head_gains = jnp.concatenate([d_self_gains, d_cross_gains], 0)[:, :HEAD_DIM] / head_gains
+    d_norm_gains = jnp.stack([d_gain0, d_gain1, d_gain2, d_gain3], 0)
+    totals = total_over_all(
+        jnp.concatenate([d_norm_gains.reshape(-1), d_head_gains.reshape(-1)])
+    )
+    norm_total = totals[: 4 * width].reshape(4, width)
+    head_total = totals[4 * width :].reshape(4, HEAD_DIM)
+
+    while flow.chains:
+        flow.step([], list(flow.chains))
+    names = ["skip", "qkv", "aout", "cquery", "ckv", "cout", "tproj", "up", "down"]
+    g_skipw, g_qkv, g_aout, g_cquery, g_ckv, g_cout, g_tproj, g_up, g_down = (
+        flow.done["g_" + name] for name in names
+    )
+    q_cols, k_cols, v_cols = (
+        g_qkv[:, i * narrow_width : (i + 1) * narrow_width] for i in range(3)
+    )
+    moved = wide(swap_seq(narrow(pick(y, v_cols, q_cols))))
+    g_qkv = jnp.concatenate([pick(y, q_cols, k_cols), moved, pick(y, k_cols, v_cols)], 1)
+    return (
+        block_out,
+        hidden_grad,
+        skip_grad,
+        g_skipw,
+        g_tfirst,
+        g_tsecond,
+        g_qkv,
+        g_aout,
+        g_cquery,
+        g_ckv,
+        g_cout,
+        g_tproj,
+        g_up,
+        g_down,
+        norm_total,
+        head_total,
+    )
+
+
 def solution(mesh):
     placed = (
         P("dp", "seq", None),
@@ -497,8 +1183,9 @@
         P(),
         P(),
     )
+    split = mesh.shape["dp"] == 16 and mesh.shape["seq"] == 2
     return jax.shard_map(
-        body,
+        fast_body if split else body,
         mesh=mesh,
         in_specs=placed,
         out_specs=(

time: 2490 us -> 1720 us (0.69)
  waiting for transfers between devices: 1140 us -> 602 us
  blocking collectives: 443 us -> 0 us
  other arithmetic: 129 us -> 379 us
  starting transfers between devices: 32.1 us -> 158 us
  local copies, waits for them, and re-layouts: 310 us -> 185 us
  matrix products: 404 us -> 363 us
    ppermute x0 -> x122, waiting for transfers between devices: none -> 602 us  [the longest x76 329 us: swap(): return lax.ppermute(value, 'dp', [(i, i ^ bit) for i in range(16)])]
    unnamed x50 -> x1, waiting for transfers between devices: 417 us -> 0.02 us
    reduce_scatter x5 -> x0, waiting for transfers between devices: 395 us -> none  [the longest x1 194 us: body(): lax.psum_scatter(g_up.astype(jnp.bfloat16), 'dp', scatter_dimension=0, ti...]
    all_gather x12 -> x1, waiting for transfers between devices: 313 us -> 0.01 us  [fast_body(): lax.all_gather(jnp.concatenate([time_first, time_second], 0), 'dp')]
    unnamed x1 -> x0, blocking collectives: 198 us -> none
    ppermute x0 -> x122, starting transfers between devices: none -> 158 us  [the longest x76 83.7 us: swap(): return lax.ppermute(value, 'dp', [(i, i ^ bit) for i in range(16)])]
    all_gather x10 -> x0, blocking collectives: 104 us -> none  [the longest x1 26.3 us: body(): lax.all_gather(col_full[1], 'dp', axis=0, tiled=True)]
    all_to_all x2 -> x0, blocking collectives: 101 us -> none  [the longest x1 79.2 us: body(): lax.all_to_all(d_triple, 'seq', split_axis=1, concat_axis=3, tiled=True)]
  transfers between devices with their start and end apart: 36 -> 123, of which waited for: 22 -> 49; matrix products, arithmetic and copies ran while one was open for 28% -> 42% of each run, Pallas kernels for 0% -> 0%
where the time goes in v1:
time: 1720 us; the launch traced here: 1710 us
  waiting for transfers between devices  602 us (35%)
  other arithmetic  379 us (22%)
  matrix products  363 us (21%)
  local copies, waits for them, and re-layouts  185 us (11%)
  starting transfers between devices  158 us (9%)
  between operations  20.6 us (1%)
    ppermute x76, waiting for transfers between devices, swap(): return lax.ppermute(value, 'dp', [(i, i ^ bit) for i in range(16)])  329 us
    ppermute x26, waiting for transfers between devices, swap_seq(): return lax.ppermute(value, 'seq', FLIP)  188 us
    dot_general x26, matrix products, dot_rows(): jnp.einsum('tc,td->cd', left, right, preferred_element_type=jnp.float32)  105 us
    ppermute x20, waiting for transfers between devices, by_routes(): return lambda value: lax.ppermute(value, BOTH, pairs)  85.6 us
    ppermute x76, starting transfers between devices, swap(): return lax.ppermute(value, 'dp', [(i, i ^ bit) for i in range(16)])  83.7 us
    dot_general x9, matrix products, project_back(): jnp.einsum('td,cd->tc', grad_low, right, preferred_element_type=jnp.float32)  76.6 us
    dot_general x12, matrix products, project(): jnp.einsum('tc,cd->td', left, right, preferred_element_type=jnp.float32)  70.4 us
    unnamed x554, local copies, waits for them, and re-layouts  51.2 us
  transfers between devices with their start and end apart: 123, of which 49 were waited for; matrix products, arithmetic and copies ran while one was open for 42% of the time, Pallas kernels for 0%

profile of v1, /device:TPU:0, one launch (start us, length us, event | category | flops | bytes accessed | tf_op | source)
XLA Modules:
  0.0 1708.3 jit_solution(1088539531480475333)
XLA Ops:
  165.5 25.4 %collective-permute-done.20 = bf16[528,704]{1,0:T(8,128)(2,1)S(1)} collective-permute-done((bf16[528,704]{1,0:T(8,128)(2,1)}, bf16[528,704]{1,0:T(8,128)(2,1)S(1)}, u32[]{:S(2)}, u32[]{:S(2)}) %collective-permute-start.20) | collective-permute-done | bytes 743456 | tf_op jit(solution)/shard_map/ppermute | solution.py:482
  262.7 25.5 %collective-permute-done.33 = bf16[792,704]{1,0:T(8,128)(2,1)S(1)} collective-permute-done((bf16[792,704]{1,0:T(8,128)(2,1)S(1)}, bf16[792,704]{1,0:T(8,128)(2,1)S(1)}, u32[]{:S(2)}, u32[]{:S(2)}) %collective-permute-start.33) | collective-permute-done | bytes 1115168 | tf_op jit(solution)/shard_map/ppermute | solution.py:593
  289.4 21.8 %collective-permute-done.40 = bf16[176,3168]{1,0:T(8,128)(2,1)S(1)} collective-permute-done((bf16[176,3168]{1,0:T(8,128)(2,1)S(1)}, bf16[176,3168]{1,0:T(8,128)(2,1)S(1)}, u32[]{:S(2)}, u32[]{:S(2)}) %collective-permute-start.40) | collective-permute-done | bytes 1115168 | tf_op jit(solution)/shard_map/ppermute | solution.py:482
  374.2 23.7 %fusion.248 = (f32[8,1024]{1,0:T(8,128)S(1)}, f32[8,1024,1024]{1,2,0:T(8,128)}) fusion(pred[1024]{0:T(1024)(128)(4,1)} %iota_compare_fusion, bf16[1024,8,88]{0,1,2:T(8,128)(2,1)} %get-tuple-element.421, bf16[1024,8,88]{0,1,2:T(8,128)(2,1)} %get-tuple-element.420), kind=kOutput, calls=%fused_computation.789 | convolution fusion | flops 1509950464 | bytes 36471808 | tf_op jit(solution)/shard_map/jvp()/sub | solution.py:799
  455.1 32.8 %collective-permute-done.43 = bf16[2,176,3168]{2,1,0:T(8,128)(2,1)} collective-permute-done((bf16[2,176,3168]{2,1,0:T(8,128)(2,1)}, bf16[2,176,3168]{2,1,0:T(8,128)(2,1)}, u32[]{:S(2)}, u32[]{:S(2)}) %collective-permute-start.43) | collective-permute-done | bytes 2230304 | tf_op jit(solution)/shard_map/ppermute | solution.py:482
  492.0 45.7 %collective-permute-done.44 = bf16[2,792,704]{2,1,0:T(8,128)(2,1)S(1)} collective-permute-done((bf16[2,792,704]{2,1,0:T(8,128)(2,1)}, bf16[2,792,704]{2,1,0:T(8,128)(2,1)S(1)}, u32[]{:S(2)}, u32[]{:S(2)}) %collective-permute-start.44) | collective-permute-done | bytes 2230304 | tf_op jit(solution)/shard_map/ppermute | solution.py:482
  654.3 14.6 maximum_select_fusion
  675.3 16.2 maximum_select_fusion.1
  716.2 25.7 %collective-permute-done.49 = bf16[512,1408]{1,0:T(8,128)(2,1)S(1)} collective-permute-done((bf16[512,1408]{1,0:T(8,128)(2,1)}, bf16[512,1408]{1,0:T(8,128)(2,1)S(1)}, u32[]{:S(2)}, u32[]{:S(2)}) %collective-permute-start.49) | collective-permute-done | bytes 1441824 | tf_op jit(solution)/shard_map/ppermute | solution.py:486
  742.2 21.6 %convolution_convert_fusion.1 = bf16[1024,3168]{0,1:T(8,128)(2,1)} fusion(bf16[1024,1408]{1,0:T(8,128)(2,1)S(1)} %constant_dynamic-update-slice_fusion.2, bf16[1408,3168]{1,0:T(8,128)(2,1)} %copy-done.184), kind=kOutput, calls=%fused_computation.54 | convolution fusion | flops 9138438144 | bytes 18292736 | tf_op jit(solution)/shard_map/tc,cd->td/dot_general | solution.py:54
  776.0 21.8 %fusion.15 = bf16[1024,3168]{0,1:T(8,128)(2,1)} fusion(bf16[1024,3168]{0,1:T(8,128)(2,1)} %convolution_convert_fusion.1, bf16[3168,1408]{1,0:T(8,128)(2,1)S(1)} %bitcast.602, bf16[512,1408]{1,0:T(8,128)(2,1)S(1)} %copy-done.247, bf16[512,1408]{1,0:T(8,128)(2,1)S(1)} %copy-done.113), kind=kOutput, calls=%fused_computation.31 | convolution fusion | flops 9209085952 | bytes 24780800 | tf_op jit(solution)/shard_map/td,cd->tc/dot_general | solution.py:58
  797.8 16.1 fusion.262
  846.7 21.2 %collective-permute-done.50 = bf16[512,1408]{1,0:T(8,128)(2,1)S(1)} collective-permute-done((bf16[512,1408]{1,0:T(8,128)(2,1)S(1)}, bf16[512,1408]{1,0:T(8,128)(2,1)S(1)}, u32[]{:S(2)}, u32[]{:S(2)}) %collective-permute-start.50) | collective-permute-done | bytes 1441824 | tf_op jit(solution)/shard_map/ppermute | solution.py:486
  964.7 27.3 %collective-permute-done.53 = bf16[2,792,704]{2,1,0:T(8,128)(2,1)} collective-permute-done((bf16[2,792,704]{2,1,0:T(8,128)(2,1)}, bf16[2,792,704]{2,1,0:T(8,128)(2,1)}, u32[]{:S(2)}, u32[]{:S(2)}) %collective-permute-start.53) | collective-permute-done | bytes 2230304 | tf_op jit(solution)/shard_map/ppermute | solution.py:482
  1052.4 17.6 %collective-permute-done.59 = bf16[704,704]{1,0:T(8,128)(2,1)} collective-permute-done((bf16[704,704]{1,0:T(8,128)(2,1)}, bf16[704,704]{1,0:T(8,128)(2,1)}, u32[]{:S(2)}, u32[]{:S(2)}) %collective-permute-start.59) | collective-permute-done | bytes 991264 | tf_op jit(solution)/shard_map/ppermute | solution.py:486
  1075.5 15.5 collective-permute-done.61
  1104.9 17.9 %fusion.7 = (f32[8,1024]{1,0:T(8,128)S(1)}, bf16[8,1024,1024]{1,2,0:T(8,128)(2,1)}) fusion(f32[8,1024,1024]{1,2,0:T(8,128)} %get-tuple-element.455, f32[8,1024]{1,0:T(8,128)S(1)} %copy-done.130, bf16[8,88,1024]{2,1,0:T(8,128)(2,1)S(1)} %bitcast.589, bf16[1024,8,88]{0,2,1:T(8,128)(2,1)S(1)} %bitcast.588), kind=kOutput, calls=%fused_computation.13 | convolution fusion | flops 1518329856 | bytes 53280768 | tf_op jit(solution)/shard_map/transpose(jvp(hqk,khd->qhd))/dot_general | solution.py:800
  1122.8 23.5 %fusion.5 = bf16[8,1024,1024]{1,2,0:T(8,128)(2,1)} fusion(f32[8,1024,1024]{1,2,0:T(8,128)} %get-tuple-element.455, bf16[8,1024,1024]{1,2,0:T(8,128)(2,1)} %get-tuple-element.470, f32[8,1024]{1,0:T(8,128)S(1)} %neg.49, f32[8,1024]{1,0:T(8,128)S(1)} %copy-done.177, pred[1024]{0:T(1024)(128)(4,1)S(1)} %copy-done.237), kind=kLoop, calls=%fused_computation.11 | loop fusion | flops 58720256 | bytes 67175424 | tf_op jit(solution)/shard_map/transpose(jvp())/mul | solution.py:797
  1175.9 15.6 scatter_fusion
  1202.0 15.1 scatter_fusion.1
  1272.3 16.3 collective-permute-done.63
  1325.6 24.1 %collective-permute-done.78 = bf16[2,256,512]{2,1,0:T(8,128)(2,1)S(1)} collective-permute-done((bf16[2,256,512]{2,1,0:T(8,128)(2,1)S(1)}, bf16[2,256,512]{2,1,0:T(8,128)(2,1)S(1)}, u32[]{:S(2)}, u32[]{:S(2)}) %collective-permute-start.78) | collective-permute-done | bytes 524320 | tf_op jit(solution)/shard_map/ppermute | solution.py:482
  1357.5 48.0 %collective-permute-done.76 = bf16[704,704]{1,0:T(8,128)(2,1)S(1)} collective-permute-done((bf16[704,704]{1,0:T(8,128)(2,1)S(1)}, bf16[704,704]{1,0:T(8,128)(2,1)S(1)}, u32[]{:S(2)}, u32[]{:S(2)}) %collective-permute-start.76) | collective-permute-done | bytes 991264 | tf_op jit(solution)/shard_map/ppermute | solution.py:486
  1561.8 16.0 collective-permute-done.99
  (1205 shorter events, 1138.8 us)
Async XLA Ops:
  7.2 116.5 %all-gather.3.cloned.1.call-start = ((), (), s32[]{:S(2)}) async-start(), calls=%async_computation | async-start | bytes 2715648 | tf_op jit(solution)/shard_map/all_gather | solution.py:903
  27.0 58.2 %collective-permute-start.16 = (bf16[88,3168]{1,0:T(8,128)(2,1)S(1)}, bf16[88,3168]{1,0:T(8,128)(2,1)S(1)}, u32[]{:S(2)}, u32[]{:S(2)}) collective-permute-start(bf16[88,3168]{1,0:T(8,128)(2,1)S(1)} %copy-done.153), channel_id=1, source_target_pairs={{0,2},{2,0},{4,6},{6,4},{8,10},{10,8},{12,14},{14,12},{16,18},{18,... | collective-permute-start | bytes 1672712 | tf_op jit(solution)/shard_map/ppermute | solution.py:482
  28.4 81.6 %collective-permute-start.29 = (bf16[396,704]{1,0:T(8,128)(2,1)S(1)}, bf16[396,704]{1,0:T(8,128)(2,1)S(1)}, u32[]{:S(2)}, u32[]{:S(2)}) collective-permute-start(bf16[396,704]{1,0:T(8,128)(2,1)S(1)} %copy-done.152), channel_id=1, source_target_pairs={{2,0},{1,2},{6,4},{5,6},{10,8},{9,10},{14,12},{13,14},{18,17},{17,... | collective-permute-start | bytes 1672712 | tf_op jit(solution)/shard_map/ppermute | solution.py:593
  35.1 74.8 %collective-permute-start.28 = (bf16[396,704]{1,0:T(8,128)(2,1)S(1)}, bf16[396,704]{1,0:T(8,128)(2,1)S(1)}, u32[]{:S(2)}, u32[]{:S(2)}) collective-permute-start(bf16[396,704]{1,0:T(8,128)(2,1)S(1)} %copy-done.152), channel_id=1, source_target_pairs={{3,2},{7,6},{11,10},{15,14},{16,17},{20,21},{24,25},{28,29}} | collective-permute-start | bytes 1672712 | tf_op jit(solution)/shard_map/ppermute | solution.py:593
  261.1 59.4 %collective-permute-start.35 = (bf16[2,2,128,1408]{3,2,1,0:T(8,128)(2,1)S(1)}, bf16[2,2,128,1408]{3,2,1,0:T(8,128)(2,1)S(1)}, u32[]{:S(2)}, u32[]{:S(2)}) collective-permute-start(bf16[2,2,128,1408]{3,2,1,0:T(8,128)(2,1)S(1)} %pad_maximum_fusion.10), channel_id=1, source_target_pairs={{0,2},{2,0},{4,6},{6,4},{8,10},{10,8},{12,14},{14,12},{16,18},{18,... | collective-permute-start | bytes 4325384 | tf_op jit(solution)/shard_map/ppermute | solution.py:482
  328.4 83.5 %collective-permute-start.36 = (bf16[256,512]{0,1:T(8,128)(2,1)}, bf16[256,512]{0,1:T(8,128)(2,1)}, u32[]{:S(2)}, u32[]{:S(2)}) collective-permute-start(bf16[256,512]{0,1:T(8,128)(2,1)} %fusion.112), channel_id=1, source_target_pairs={{0,1},{1,0},{2,3},{3,2},{4,5},{5,4},{6,7},{7,6},{8,9},{9,8},{10,11... | collective-permute-start | bytes 786440 | tf_op jit(solution)/shard_map/ppermute | solution.py:486
  363.5 72.2 %collective-permute-start.39 = (bf16[2,2,528,704]{3,2,1,0:T(8,128)(2,1)}, bf16[2,2,528,704]{3,2,1,0:T(8,128)(2,1)}, u32[]{:S(2)}, u32[]{:S(2)}) collective-permute-start(bf16[2,2,528,704]{3,2,1,0:T(8,128)(2,1)} %pad_maximum_fusion.2), channel_id=1, source_target_pairs={{0,4},{2,6},{4,0},{6,2},{8,12},{10,14},{12,8},{14,10},{16,20},{18,... | collective-permute-start | bytes 8921096 | tf_op jit(solution)/shard_map/ppermute | solution.py:482
  364.0 56.3 %collective-permute-start.41 = (bf16[792,704]{1,0:T(8,128)(2,1)S(1)}, bf16[792,704]{1,0:T(8,128)(2,1)}, u32[]{:S(2)}, u32[]{:S(2)}) collective-permute-start(bf16[792,704]{1,0:T(8,128)(2,1)S(1)} %copy-done.42), channel_id=1, source_target_pairs={{0,8},{2,10},{4,12},{6,14},{8,0},{10,2},{12,4},{14,6},{16,24},{18,... | collective-permute-start | bytes 3345416 | tf_op jit(solution)/shard_map/ppermute | solution.py:482
  448.8 114.6 %collective-permute-start.42 = (bf16[512,704]{0,1:T(8,128)(2,1)S(1)}, bf16[512,704]{0,1:T(8,128)(2,1)}, u32[]{:S(2)}, u32[]{:S(2)}) collective-permute-start(bf16[512,704]{0,1:T(8,128)(2,1)S(1)} %slice.535), channel_id=1, source_target_pairs={{0,1},{1,0},{2,3},{3,2},{4,5},{5,4},{6,7},{7,6},{8,9},{9,8},{10,11... | collective-permute-start | bytes 2162696 | tf_op jit(solution)/shard_map/ppermute | solution.py:486
  449.1 88.6 %collective-permute-start.44 = (bf16[2,792,704]{2,1,0:T(8,128)(2,1)}, bf16[2,792,704]{2,1,0:T(8,128)(2,1)S(1)}, u32[]{:S(2)}, u32[]{:S(2)}) collective-permute-start(bf16[2,792,704]{2,1,0:T(8,128)(2,1)} %pad_maximum_fusion.8), channel_id=1, source_target_pairs={{0,4},{2,6},{4,0},{6,2},{8,12},{10,14},{12,8},{14,10},{16,20},{18,... | collective-permute-start | bytes 6690824 | tf_op jit(solution)/shard_map/ppermute | solution.py:482
  450.6 92.5 %collective-permute-start.46 = (bf16[2,2,528,704]{3,2,1,0:T(8,128)(2,1)}, bf16[2,2,528,704]{3,2,1,0:T(8,128)(2,1)S(1)}, u32[]{:S(2)}, u32[]{:S(2)}) collective-permute-start(bf16[2,2,528,704]{3,2,1,0:T(8,128)(2,1)} %collective-permute-done.39), channel_id=1, source_target_pairs={{0,2},{2,0},{4,6},{6,4},{8,10},{10,8},{12,14},{14,12},{16,18},{18,... | collective-permute-start | bytes 8921096 | tf_op jit(solution)/shard_map/ppermute | solution.py:482
  450.6 92.5 %collective-permute-start.45 = (bf16[2,2,528,704]{3,2,1,0:T(8,128)(2,1)}, bf16[2,2,528,704]{3,2,1,0:T(8,128)(2,1)S(1)}, u32[]{:S(2)}, u32[]{:S(2)}) collective-permute-start(bf16[2,2,528,704]{3,2,1,0:T(8,128)(2,1)} %pad_maximum_fusion.2), channel_id=1, source_target_pairs={{0,2},{2,0},{4,6},{6,4},{8,10},{10,8},{12,14},{14,12},{16,18},{18,... | collective-permute-start | bytes 8921096 | tf_op jit(solution)/shard_map/ppermute | solution.py:482
  605.2 86.3 %collective-permute-start.47 = (bf16[2,2,176,3168]{3,2,1,0:T(8,128)(2,1)}, bf16[2,2,176,3168]{3,2,1,0:T(8,128)(2,1)}, u32[]{:S(2)}, u32[]{:S(2)}) collective-permute-start(bf16[2,2,176,3168]{3,2,1,0:T(8,128)(2,1)} %pad_maximum_fusion), channel_id=1, source_target_pairs={{0,2},{2,0},{4,6},{6,4},{8,10},{10,8},{12,14},{14,12},{16,18},{18,... | collective-permute-start | bytes 13381640 | tf_op jit(solution)/shard_map/ppermute | solution.py:482
  834.1 64.4 %collective-permute-start.51 = (bf16[512,1408]{1,0:T(8,128)(2,1)}, bf16[512,1408]{1,0:T(8,128)(2,1)}, u32[]{:S(2)}, u32[]{:S(2)}) collective-permute-start(bf16[512,1408]{1,0:T(8,128)(2,1)} %slice.1028), channel_id=1, source_target_pairs={{0,1},{1,0},{2,3},{3,2},{4,5},{5,4},{6,7},{7,6},{8,9},{9,8},{10,11... | collective-permute-start | bytes 4325384 | tf_op jit(solution)/shard_map/ppermute | solution.py:486
  937.1 54.8 %collective-permute-start.53 = (bf16[2,792,704]{2,1,0:T(8,128)(2,1)}, bf16[2,792,704]{2,1,0:T(8,128)(2,1)}, u32[]{:S(2)}, u32[]{:S(2)}) collective-permute-start(bf16[2,792,704]{2,1,0:T(8,128)(2,1)} %dynamic-slice_bitcast_fusion), channel_id=1, source_target_pairs={{0,4},{2,6},{4,0},{6,2},{8,12},{10,14},{12,8},{14,10},{16,20},{18,... | collective-permute-start | bytes 6690824 | tf_op jit(solution)/shard_map/ppermute | solution.py:482
  937.7 59.2 %collective-permute-start.54 = (bf16[704,3168]{1,0:T(8,128)(2,1)}, bf16[704,3168]{1,0:T(8,128)(2,1)}, u32[]{:S(2)}, u32[]{:S(2)}) collective-permute-start(bf16[704,3168]{1,0:T(8,128)(2,1)} %convolution_convert_fusion.2), channel_id=1, source_target_pairs={{0,2},{2,0},{4,6},{6,4},{8,10},{10,8},{12,14},{14,12},{16,18},{18,... | collective-permute-start | bytes 13381640 | tf_op jit(solution)/shard_map/ppermute | solution.py:482
  958.5 93.5 %collective-permute-start.58 = (bf16[704,704]{1,0:T(8,128)(2,1)}, bf16[704,704]{1,0:T(8,128)(2,1)}, u32[]{:S(2)}, u32[]{:S(2)}) collective-permute-start(bf16[704,704]{1,0:T(8,128)(2,1)} %convolution_convert_fusion.27), channel_id=1, source_target_pairs={{0,2},{2,0},{4,6},{6,4},{8,10},{10,8},{12,14},{14,12},{16,18},{18,... | collective-permute-start | bytes 2973704 | tf_op jit(solution)/shard_map/ppermute | solution.py:482
  1032.5 58.5 %collective-permute-start.61 = (bf16[384,1408]{0,1:T(8,128)(2,1)}, bf16[384,1408]{0,1:T(8,128)(2,1)}, u32[]{:S(2)}, u32[]{:S(2)}) collective-permute-start(bf16[384,1408]{0,1:T(8,128)(2,1)} %broadcast_select_fusion.20), channel_id=1, source_target_pairs={{0,1},{1,0},{2,3},{3,2},{4,5},{5,4},{6,7},{7,6},{8,9},{9,8},{10,11... | collective-permute-start | bytes 3244040 | tf_op jit(solution)/shard_map/ppermute | solution.py:486
  1052.0 207.2 %collective-permute-start.64 = (bf16[2,176,3168]{2,1,0:T(8,128)(2,1)}, bf16[2,176,3168]{2,1,0:T(8,128)(2,1)}, u32[]{:S(2)}, u32[]{:S(2)}) collective-permute-start(bf16[2,176,3168]{2,1,0:T(8,128)(2,1)} %dynamic-slice_bitcast_fusion.1), channel_id=1, source_target_pairs={{0,4},{2,6},{4,0},{6,2},{8,12},{10,14},{12,8},{14,10},{16,20},{18,... | collective-permute-start | bytes 6690824 | tf_op jit(solution)/shard_map/ppermute | solution.py:482
  1070.0 193.9 %collective-permute-start.66 = (bf16[704,704]{1,0:T(8,128)(2,1)}, bf16[704,704]{1,0:T(8,128)(2,1)}, u32[]{:S(2)}, u32[]{:S(2)}) collective-permute-start(bf16[704,704]{1,0:T(8,128)(2,1)} %convolution_convert_fusion.25), channel_id=1, source_target_pairs={{0,2},{2,0},{4,6},{6,4},{8,10},{10,8},{12,14},{14,12},{16,18},{18,... | collective-permute-start | bytes 2973704 | tf_op jit(solution)/shard_map/ppermute | solution.py:482
  1264.1 93.4 %collective-permute-start.75 = (bf16[704,704]{1,0:T(8,128)(2,1)}, bf16[704,704]{1,0:T(8,128)(2,1)}, u32[]{:S(2)}, u32[]{:S(2)}) collective-permute-start(bf16[704,704]{1,0:T(8,128)(2,1)} %convolution_convert_fusion.23), channel_id=1, source_target_pairs={{0,2},{2,0},{4,6},{6,4},{8,10},{10,8},{12,14},{14,12},{16,18},{18,... | collective-permute-start | bytes 2973704 | tf_op jit(solution)/shard_map/ppermute | solution.py:482
  1349.7 59.6 %collective-permute-start.71 = (bf16[512,1408]{1,0:T(8,128)(2,1)S(1)}, bf16[512,1408]{1,0:T(8,128)(2,1)S(1)}, u32[]{:S(2)}, u32[]{:S(2)}) collective-permute-start(bf16[512,1408]{1,0:T(8,128)(2,1)S(1)} %slice.1027), channel_id=1, source_target_pairs={{0,1},{1,0},{2,3},{3,2},{4,5},{5,4},{6,7},{7,6},{8,9},{9,8},{10,11... | collective-permute-start | bytes 4325384 | tf_op jit(solution)/shard_map/ppermute | solution.py:486
  1350.6 57.3 %collective-permute-start.72 = (bf16[176,3168]{1,0:T(8,128)(2,1)S(1)}, bf16[176,3168]{1,0:T(8,128)(2,1)S(1)}, u32[]{:S(2)}, u32[]{:S(2)}) collective-permute-start(bf16[176,3168]{1,0:T(8,128)(2,1)S(1)} %copy-done.119), channel_id=1, source_target_pairs={{0,8},{2,10},{4,12},{6,14},{8,0},{10,2},{12,4},{14,6},{16,24},{18,... | collective-permute-start | bytes 3345416 | tf_op jit(solution)/shard_map/ppermute | solution.py:482
  1548.2 66.9 %collective-permute-start.115 = (f32[16,1408]{1,0:T(8,128)}, f32[16,1408]{1,0:T(8,128)}, u32[]{:S(2)}, u32[]{:S(2)}) collective-permute-start(f32[16,1408]{1,0:T(8,128)} %fusion.198), channel_id=1, source_target_pairs={{0,1},{1,0},{2,3},{3,2},{4,5},{5,4},{6,7},{7,6},{8,9},{9,8},{10,11... | collective-permute-start | bytes 270344 | tf_op jit(solution)/shard_map/ppermute | solution.py:486
  (367 other events, 7601.2 us)
Sparse Core Ops, SparseCore 0:
  10.8 48.2 all-gather.2

commit v2 on v1

--- a/solution.py
+++ b/solution.py
@@ -5,6 +5,8 @@
 from jax import lax
 from jax.sharding import PartitionSpec as P
 
+DP = "dp"
+SEQ = "seq"
 HEADS = 16
 HEAD_DIM = 88
 FREQ = 256
@@ -62,7 +64,7 @@
     return jnp.einsum("tc,td->cd", left, grad_low, preferred_element_type=jnp.float32)
 
 
-def body(
+def whole_body(
     hidden_in,
     skip_in,
     clip_text,
@@ -87,7 +89,7 @@
     head_gains,
 ):
     images, local, width = hidden_in.shape
-    groups = lax.axis_size("seq")
+    groups = lax.axis_size(SEQ)
     heads_here = HEADS // groups
     narrow = width // groups
     tokens = images * local
@@ -98,30 +100,30 @@
     pos_rows = patch_pos[0].reshape(tokens).astype(jnp.float32)
     pos_cols = patch_pos[1].reshape(tokens).astype(jnp.float32)
     col_full = (
-        lax.all_gather(skip_weight, "seq", axis=1, tiled=True),
-        lax.all_gather(time_first, "seq", axis=1, tiled=True),
-        lax.all_gather(time_second, "seq", axis=1, tiled=True),
-        lax.all_gather(attn_qkv, "seq", axis=1, tiled=True),
-        lax.all_gather(attn_out, "seq", axis=1, tiled=True),
-        lax.all_gather(cross_qproj, "seq", axis=1, tiled=True),
-        lax.all_gather(cross_kvproj, "seq", axis=1, tiled=True),
-        lax.all_gather(cross_out, "seq", axis=1, tiled=True),
-        lax.all_gather(text_proj, "seq", axis=1, tiled=True),
-        lax.all_gather(mlp_up, "seq", axis=1, tiled=True),
-        lax.all_gather(mlp_down, "seq", axis=1, tiled=True),
+        lax.all_gather(skip_weight, SEQ, axis=1, tiled=True),
+        lax.all_gather(time_first, SEQ, axis=1, tiled=True),
+        lax.all_gather(time_second, SEQ, axis=1, tiled=True),
+        lax.all_gather(attn_qkv, SEQ, axis=1, tiled=True),
+        lax.all_gather(attn_out, SEQ, axis=1, tiled=True),
+        lax.all_gather(cross_qproj, SEQ, axis=1, tiled=True),
+        lax.all_gather(cross_kvproj, SEQ, axis=1, tiled=True),
+        lax.all_gather(cross_out, SEQ, axis=1, tiled=True),
+        lax.all_gather(text_proj, SEQ, axis=1, tiled=True),
+        lax.all_gather(mlp_up, SEQ, axis=1, tiled=True),
+        lax.all_gather(mlp_down, SEQ, axis=1, tiled=True),
     )
     weight_set = (
-        lax.all_gather(col_full[0], "dp", axis=0, tiled=True),
-        lax.all_gather(col_full[1], "dp", axis=0, tiled=True),
-        lax.all_gather(col_full[2], "dp", axis=0, tiled=True),
-        lax.all_gather(col_full[3], "dp", axis=0, tiled=True),
-        lax.all_gather(col_full[4], "dp", axis=0, tiled=True),
-        lax.all_gather(col_full[5], "dp", axis=0, tiled=True),
-        lax.all_gather(col_full[6], "dp", axis=0, tiled=True),
-        lax.all_gather(col_full[7], "dp", axis=0, tiled=True),
-        lax.all_gather(col_full[8], "dp", axis=0, tiled=True),
-        lax.all_gather(col_full[9], "dp", axis=0, tiled=True),
-        lax.all_gather(col_full[10], "dp", axis=0, tiled=True),
+        lax.all_gather(col_full[0], DP, axis=0, tiled=True),
+        lax.all_gather(col_full[1], DP, axis=0, tiled=True),
+        lax.all_gather(col_full[2], DP, axis=0, tiled=True),
+        lax.all_gather(col_full[3], DP, axis=0, tiled=True),
+        lax.all_gather(col_full[4], DP, axis=0, tiled=True),
+        lax.all_gather(col_full[5], DP, axis=0, tiled=True),
+        lax.all_gather(col_full[6], DP, axis=0, tiled=True),
+        lax.all_gather(col_full[7], DP, axis=0, tiled=True),
+        lax.all_gather(col_full[8], DP, axis=0, tiled=True),
+        lax.all_gather(col_full[9], DP, axis=0, tiled=True),
+        lax.all_gather(col_full[10], DP, axis=0, tiled=True),
     )
     w_skip, w_first, w_second, w_qkv, w_aout, w_cq, w_ckv, w_cout, w_text, w_up, w_down = weight_set
     joined = jnp.concatenate([hidden_in, skip_in], -1).reshape(tokens, 2 * width)
@@ -160,7 +162,7 @@
         )
         return (mixed_out.astype(jnp.bfloat16), (top_score + jnp.log(totals))[:, 0])
 
-    pieces = lax.all_to_all(stacked, "seq", split_axis=3, concat_axis=1, tiled=True)
+    pieces = lax.all_to_all(stacked, SEQ, split_axis=3, concat_axis=1, tiled=True)
     item_count = pieces.shape[0]
     length = pieces.shape[1]
     split_heads = pieces.reshape(item_count, length, 3, heads_here, HEAD_DIM)
@@ -171,7 +173,7 @@
     joined_heads = jnp.transpose(
         mixed_out.reshape(item_count, heads_here, length, HEAD_DIM), (0, 2, 1, 3)
     ).reshape(item_count, length, narrow)
-    returned = lax.all_to_all(joined_heads, "seq", split_axis=1, concat_axis=2, tiled=True)
+    returned = lax.all_to_all(joined_heads, SEQ, split_axis=1, concat_axis=2, tiled=True)
     self_logsum = logsum.reshape(item_count, heads_here, length)
     attn_flat = returned.reshape(tokens, width)
     resid1 = resid0 + project(attn_flat, w_aout)
@@ -214,30 +216,30 @@
     final = resid2 + project(active, w_down)
     block_out = final.astype(jnp.bfloat16).reshape(images, local, width)
     again_full = (
-        lax.all_gather(skip_weight, "seq", axis=1, tiled=True),
-        lax.all_gather(time_first, "seq", axis=1, tiled=True),
-        lax.all_gather(time_second, "seq", axis=1, tiled=True),
-        lax.all_gather(attn_qkv, "seq", axis=1, tiled=True),
-        lax.all_gather(attn_out, "seq", axis=1, tiled=True),
-        lax.all_gather(cross_qproj, "seq", axis=1, tiled=True),
-        lax.all_gather(cross_kvproj, "seq", axis=1, tiled=True),
-        lax.all_gather(cross_out, "seq", axis=1, tiled=True),
-        lax.all_gather(text_proj, "seq", axis=1, tiled=True),
-        lax.all_gather(mlp_up, "seq", axis=1, tiled=True),
-        lax.all_gather(mlp_down, "seq", axis=1, tiled=True),
+        lax.all_gather(skip_weight, SEQ, axis=1, tiled=True),
+        lax.all_gather(time_first, SEQ, axis=1, tiled=True),
+        lax.all_gather(time_second, SEQ, axis=1, tiled=True),
+        lax.all_gather(attn_qkv, SEQ, axis=1, tiled=True),
+        lax.all_gather(attn_out, SEQ, axis=1, tiled=True),
+        lax.all_gather(cross_qproj, SEQ, axis=1, tiled=True),
+        lax.all_gather(cross_kvproj, SEQ, axis=1, tiled=True),
+        lax.all_gather(cross_out, SEQ, axis=1, tiled=True),
+        lax.all_gather(text_proj, SEQ, axis=1, tiled=True),
+        lax.all_gather(mlp_up, SEQ, axis=1, tiled=True),
+        lax.all_gather(mlp_down, SEQ, axis=1, tiled=True),
     )
     weight_set = (
-        lax.all_gather(again_full[0], "dp", axis=0, tiled=True),
-        lax.all_gather(again_full[1], "dp", axis=0, tiled=True),
-        lax.all_gather(again_full[2], "dp", axis=0, tiled=True),
-        lax.all_gather(again_full[3], "dp", axis=0, tiled=True),
-        lax.all_gather(again_full[4], "dp", axis=0, tiled=True),
-        lax.all_gather(again_full[5], "dp", axis=0, tiled=True),
-        lax.all_gather(again_full[6], "dp", axis=0, tiled=True),
-        lax.all_gather(again_full[7], "dp", axis=0, tiled=True),
-        lax.all_gather(again_full[8], "dp", axis=0, tiled=True),
-        lax.all_gather(again_full[9], "dp", axis=0, tiled=True),
-        lax.all_gather(again_full[10], "dp", axis=0, tiled=True),
+        lax.all_gather(again_full[0], DP, axis=0, tiled=True),
+        lax.all_gather(again_full[1], DP, axis=0, tiled=True),
+        lax.all_gather(again_full[2], DP, axis=0, tiled=True),
+        lax.all_gather(again_full[3], DP, axis=0, tiled=True),
+        lax.all_gather(again_full[4], DP, axis=0, tiled=True),
+        lax.all_gather(again_full[5], DP, axis=0, tiled=True),
+        lax.all_gather(again_full[6], DP, axis=0, tiled=True),
+        lax.all_gather(again_full[7], DP, axis=0, tiled=True),
+        lax.all_gather(again_full[8], DP, axis=0, tiled=True),
+        lax.all_gather(again_full[9], DP, axis=0, tiled=True),
+        lax.all_gather(again_full[10], DP, axis=0, tiled=True),
     )
     w_skip, w_first, w_second, w_qkv, w_aout, w_cq, w_ckv, w_cout, w_text, w_up, w_down = weight_set
     scaled_cot = (out_cot.astype(jnp.float32) * loss_weight[:, None, None]).reshape(tokens, width)
@@ -296,7 +298,7 @@
     grad_low = resid_grad.astype(jnp.bfloat16)
     g_aout = weight_grad(attn_flat, grad_low)
     d_attn = project_back(grad_low, w_aout).astype(jnp.bfloat16).reshape(images, local, width)
-    d_heads = lax.all_to_all(d_attn, "seq", split_axis=2, concat_axis=1, tiled=True)
+    d_heads = lax.all_to_all(d_attn, SEQ, split_axis=2, concat_axis=1, tiled=True)
 
     def self_back(operand):
         queries, keyset, valueset, d_mixed, logsum = operand
@@ -346,7 +348,7 @@
         3, images, heads_here, full_len, HEAD_DIM
     )
     d_triple = jnp.transpose(d_triple, (1, 3, 0, 2, 4)).reshape(images, full_len, 3, narrow)
-    d_stacked = lax.all_to_all(d_triple, "seq", split_axis=1, concat_axis=3, tiled=True)
+    d_stacked = lax.all_to_all(d_triple, SEQ, split_axis=1, concat_axis=3, tiled=True)
     d_packed_in = d_stacked.reshape(tokens, 3, HEADS, HEAD_DIM).astype(jnp.float32)
     q_vals, q_back = jax.vjp(query_prep, packed[:, 0], head_gains[0])
     d_qpre, d_hgain0 = q_back(d_packed_in[:, 0])
@@ -377,72 +379,72 @@
     skip_grad = d_joined[:, width:].reshape(images, local, width)
     row_sums = (
         lax.psum_scatter(
-            g_skipw.astype(jnp.bfloat16), "dp", scatter_dimension=0, tiled=True
-        ).astype(jnp.float32),
-        lax.psum_scatter(
-            g_tfirst.astype(jnp.bfloat16), "dp", scatter_dimension=0, tiled=True
-        ).astype(jnp.float32),
-        lax.psum_scatter(
-            g_tsecond.astype(jnp.bfloat16), "dp", scatter_dimension=0, tiled=True
-        ).astype(jnp.float32),
-        lax.psum_scatter(g_qkv.astype(jnp.bfloat16), "dp", scatter_dimension=0, tiled=True).astype(
+            g_skipw.astype(jnp.bfloat16), DP, scatter_dimension=0, tiled=True
+        ).astype(jnp.float32),
+        lax.psum_scatter(
+            g_tfirst.astype(jnp.bfloat16), DP, scatter_dimension=0, tiled=True
+        ).astype(jnp.float32),
+        lax.psum_scatter(
+            g_tsecond.astype(jnp.bfloat16), DP, scatter_dimension=0, tiled=True
+        ).astype(jnp.float32),
+        lax.psum_scatter(g_qkv.astype(jnp.bfloat16), DP, scatter_dimension=0, tiled=True).astype(
             jnp.float32
         ),
-        lax.psum_scatter(g_aout.astype(jnp.bfloat16), "dp", scatter_dimension=0, tiled=True).astype(
+        lax.psum_scatter(g_aout.astype(jnp.bfloat16), DP, scatter_dimension=0, tiled=True).astype(
             jnp.float32
         ),
         lax.psum_scatter(
-            g_cquery.astype(jnp.bfloat16), "dp", scatter_dimension=0, tiled=True
-        ).astype(jnp.float32),
-        lax.psum_scatter(g_ckv.astype(jnp.bfloat16), "dp", scatter_dimension=0, tiled=True).astype(
+            g_cquery.astype(jnp.bfloat16), DP, scatter_dimension=0, tiled=True
+        ).astype(jnp.float32),
+        lax.psum_scatter(g_ckv.astype(jnp.bfloat16), DP, scatter_dimension=0, tiled=True).astype(
             jnp.float32
         ),
-        lax.psum_scatter(g_cout.astype(jnp.bfloat16), "dp", scatter_dimension=0, tiled=True).astype(
+        lax.psum_scatter(g_cout.astype(jnp.bfloat16), DP, scatter_dimension=0, tiled=True).astype(
             jnp.float32
         ),
         lax.psum_scatter(
-            g_tproj.astype(jnp.bfloat16), "dp", scatter_dimension=0, tiled=True
-        ).astype(jnp.float32),
-        lax.psum_scatter(g_up.astype(jnp.bfloat16), "dp", scatter_dimension=0, tiled=True).astype(
+            g_tproj.astype(jnp.bfloat16), DP, scatter_dimension=0, tiled=True
+        ).astype(jnp.float32),
+        lax.psum_scatter(g_up.astype(jnp.bfloat16), DP, scatter_dimension=0, tiled=True).astype(
             jnp.float32
         ),
-        lax.psum_scatter(g_down.astype(jnp.bfloat16), "dp", scatter_dimension=0, tiled=True).astype(
+        lax.psum_scatter(g_down.astype(jnp.bfloat16), DP, scatter_dimension=0, tiled=True).astype(
             jnp.float32
         ),
     )
     owned = (
         lax.psum_scatter(
-            row_sums[0].astype(jnp.bfloat16), "seq", scatter_dimension=1, tiled=True
-        ).astype(jnp.float32),
-        lax.psum_scatter(
-            row_sums[1].astype(jnp.bfloat16), "seq", scatter_dimension=1, tiled=True
-        ).astype(jnp.float32),
-        lax.psum_scatter(
-            row_sums[2].astype(jnp.bfloat16), "seq", scatter_dimension=1, tiled=True
-        ).astype(jnp.float32),
-        lax.psum_scatter(
-            row_sums[3].astype(jnp.bfloat16), "seq", scatter_dimension=1, tiled=True
-        ).astype(jnp.float32),
-        lax.psum_scatter(
-            row_sums[4].astype(jnp.bfloat16), "seq", scatter_dimension=1, tiled=True
-        ).astype(jnp.float32),
-        lax.psum_scatter(
-            row_sums[5].astype(jnp.bfloat16), "seq", scatter_dimension=1, tiled=True
-        ).astype(jnp.float32),
-        lax.psum_scatter(
-            row_sums[6].astype(jnp.bfloat16), "seq", scatter_dimension=1, tiled=True
-        ).astype(jnp.float32),
-        lax.psum_scatter(
-            row_sums[7].astype(jnp.bfloat16), "seq", scatter_dimension=1, tiled=True
-        ).astype(jnp.float32),
-        lax.psum_scatter(
-            row_sums[8].astype(jnp.bfloat16), "seq", scatter_dimension=1, tiled=True
-        ).astype(jnp.float32),
-        lax.psum_scatter(
-            row_sums[9].astype(jnp.bfloat16), "seq", scatter_dimension=1, tiled=True
-        ).astype(jnp.float32),
-        lax.psum_scatter(
-            row_sums[10].astype(jnp.bfloat16), "seq", scatter_dimension=1, tiled=True
+            row_sums[0].astype(jnp.bfloat16), SEQ, scatter_dimension=1, tiled=True
+        ).astype(jnp.float32),
+        lax.psum_scatter(
+            row_sums[1].astype(jnp.bfloat16), SEQ, scatter_dimension=1, tiled=True
+        ).astype(jnp.float32),
+        lax.psum_scatter(
+            row_sums[2].astype(jnp.bfloat16), SEQ, scatter_dimension=1, tiled=True
+        ).astype(jnp.float32),
+        lax.psum_scatter(
+            row_sums[3].astype(jnp.bfloat16), SEQ, scatter_dimension=1, tiled=True
+        ).astype(jnp.float32),
+        lax.psum_scatter(
+            row_sums[4].astype(jnp.bfloat16), SEQ, scatter_dimension=1, tiled=True
+        ).astype(jnp.float32),
+        lax.psum_scatter(
+            row_sums[5].astype(jnp.bfloat16), SEQ, scatter_dimension=1, tiled=True
+        ).astype(jnp.float32),
+        lax.psum_scatter(
+            row_sums[6].astype(jnp.bfloat16), SEQ, scatter_dimension=1, tiled=True
+        ).astype(jnp.float32),
+        lax.psum_scatter(
+            row_sums[7].astype(jnp.bfloat16), SEQ, scatter_dimension=1, tiled=True
+        ).astype(jnp.float32),
+        lax.psum_scatter(
+            row_sums[8].astype(jnp.bfloat16), SEQ, scatter_dimension=1, tiled=True
+        ).astype(jnp.float32),
+        lax.psum_scatter(
+            row_sums[9].astype(jnp.bfloat16), SEQ, scatter_dimension=1, tiled=True
+        ).astype(jnp.float32),
+        lax.psum_scatter(
+            row_sums[10].astype(jnp.bfloat16), SEQ, scatter_dimension=1, tiled=True
         ).astype(jnp.float32),
     )
     gain_totals = lax.psum(
@@ -450,7 +452,7 @@
             jnp.stack([d_gain0, d_gain1, d_gain2, d_gain3], 0),
             jnp.stack([d_hgain0, d_hgain1, d_hgain2, d_hgain3], 0),
         ),
-        ("dp", "seq"),
+        (DP, SEQ),
     )
     return (
         block_out,
@@ -472,18 +474,18 @@
     )
 
 
-BOTH = ("dp", "seq")
+BOTH = (DP, SEQ)
 FLIP = [(0, 1), (1, 0)]
 LOG2E = 1.4426950408889634
 LANES = 128
 
 
 def swap(value, bit):
-    return lax.ppermute(value, "dp", [(i, i ^ bit) for i in range(16)])
+    return lax.ppermute(value, DP, [(i, i ^ bit) for i in range(16)])
 
 
 def swap_seq(value):
-    return lax.ppermute(value, "seq", FLIP)
+    return lax.ppermute(value, SEQ, FLIP)
 
 
 def core_holds(dp_index, seq_index):
@@ -534,8 +536,8 @@
 
 class Spot:
     def __init__(self):
-        self.d = lax.axis_index("dp")
-        self.y = lax.axis_index("seq")
+        self.d = lax.axis_index(DP)
+        self.y = lax.axis_index(SEQ)
         self.z = self.d // 4
         self.x = (self.d // 2) % 2
         self.c = self.d % 2
@@ -593,96 +595,6 @@
     return lambda value: lax.ppermute(value, BOTH, pairs)
 
 
-def join(parts):
-    if len(parts) == 1:
-        return parts[0].astype(jnp.bfloat16)
-    return jnp.concatenate([part.astype(jnp.float32) for part in parts], axis=1).astype(
-        jnp.bfloat16
-    )
-
-
-def assemble(spot, sources, spans, over_seq, x_first):
-    count = len(sources) // 2
-
-    def piece(level, i, j):
-        near = sources[level * count : (level + 1) * count]
-        if not over_seq:
-            return choose(choose(near[0], 0, i), 0, j)
-        if x_first:
-            parts = [choose(choose(source, 0, i), 0, j) for source in near]
-        else:
-            both = jnp.where(i == 0, choose(near[0], 1, j), choose(near[1], 1, j))
-            parts = [both[0], both[1]]
-        return pair(spot.y, parts[0], parts[1], 1)
-
-    blocks = []
-    for f in range(2):
-        for j in range(2):
-            for i in range(2):
-                place = i ^ spot.x, j ^ spot.b
-                blocks.append(jnp.where(spot.c == f, piece(0, *place), piece(1, *place)))
-    outs, at = [], 0
-    for span in spans:
-        outs.append(jnp.concatenate([block[at : at + span] for block in blocks], 0))
-        at += span
-    return outs
-
-
-def assemble_columns(spot, own, other):
-    whole = pair(spot.c, own, other, 2)
-    return pair(spot.b, whole[0], whole[1], 0)
-
-
-def gather_rows(spot, shards):
-    mates = yield [(by_core, shard) for shard in shards]
-    blocks = [pair(spot.c, s, m) for s, m in zip(shards, mates)]
-    hop = by_routes(hop_pairs(core_holds, True))
-    fars = yield [(hop, block) for block in blocks]
-    blocks = [jnp.where(spot.c == spot.h, block, far) for block, far in zip(blocks, fars)]
-    nears = yield [(by_z, block) for block in blocks]
-    lines = [jnp.stack([block, near]) for block, near in zip(blocks, nears)]
-    sides = yield [(by_x, line) for line in lines]
-    owns = [jnp.stack([line, side]) for line, side in zip(lines, sides)]
-    fars = yield [(by_core, own) for own in owns]
-    return [
-        assemble(spot, [own, far], [own.shape[2]], False, True)[0] for own, far in zip(owns, fars)
-    ]
-
-
-def gather_both(spot, shards, x_first):
-    mates = yield [(by_core, jnp.concatenate(shards, 0))]
-    at, blocks = 0, []
-    for shard in shards:
-        rows = shard.shape[0]
-        blocks.append(pair(spot.c, shard, mates[0][at : at + rows]))
-        at += rows
-    block = jnp.concatenate(blocks, 0)
-    (far,) = yield [(by_routes(hop_pairs(core_holds, True)), block)]
-    block = jnp.where(spot.c == spot.h, block, far)
-    (near,) = yield [(by_z, block)]
-    line = jnp.stack([block, near])
-    (side,) = yield [(by_x if x_first else swap_seq, line)]
-    own = jnp.stack([line, side])
-    (other,) = yield [(swap_seq if x_first else by_x, own)]
-    fars = yield [(by_core, own), (by_core, other)]
-    return assemble(spot, [own, other, *fars], [b.shape[0] for b in blocks], True, x_first)
-
-
-def gather_down(spot, shard):
-    first, second = corner_pairs(False)
-    crossed, across = yield [(by_routes(first), shard), (by_routes(second), shard)]
-    mine = jnp.where(spot.c == spot.y, shard, across)
-    block = pair(spot.c, mine, crossed)
-    (far,) = yield [(by_routes(hop_pairs(seq_holds, True)), block)]
-    block = jnp.where(spot.y == spot.h, block, far)
-    (near,) = yield [(by_z, block)]
-    line = jnp.stack([block, near])
-    (side,) = yield [(by_x, line)]
-    own = pair(spot.x, line, side, 1)
-    (other,) = yield [(by_core, own)]
-    return assemble_columns(spot, own, other)
-
-
 def narrow(value):
     return value.astype(jnp.bfloat16)
 
@@ -774,11 +686,6 @@
     return value
 
 
-def partner(lane):
-    quarter = HEAD_DIM // 4
-    return jnp.where((lane // quarter) % 2 == 0, lane + quarter, lane - quarter)
-
-
 def attend(q_src, kv_src, gains, cosine, sine, heads, q_at, k_at, v_at, keys):
     width = heads * HEAD_DIM
 
@@ -788,7 +695,8 @@
     def prepared(source, at, which):
         v = normalize(heads_of(source, at)) * gains[which]
         if cosine is not None:
-            other = v[..., partner(jnp.arange(HEAD_DIM))]
+            q1, q2, q3, q4 = jnp.split(v, 4, axis=-1)
+            other = jnp.concatenate([q2, q1, q4, q3], -1)
             v = v * cosine[:, None, :HEAD_DIM] + other * sine[:, None, :HEAD_DIM]
         return v.astype(jnp.bfloat16)
 
@@ -836,10 +744,7 @@
 
 
 def gain_rows(gains):
-    lane = jnp.arange(HEAD_DIM)
-    return jnp.pad(
-        jnp.concatenate([gains, gains[:, partner(lane)]], 0), ((0, 0), (0, LANES - HEAD_DIM))
-    )
+    return jnp.pad(gains, ((0, 0), (0, LANES - HEAD_DIM)))
 
 
 def gelu(values):
@@ -900,7 +805,7 @@
     y = spot.y
     bf16 = jnp.bfloat16
 
-    time_rows = lax.all_gather(jnp.concatenate([time_first, time_second], 0), "dp")
+    time_rows = lax.all_gather(jnp.concatenate([time_first, time_second], 0), DP)
     time_cut = time_first.shape[0]
     time_weights = [
         rows.reshape(-1, narrow_width) for rows in (time_rows[:, :time_cut], time_rows[:, time_cut:])
@@ -920,19 +825,35 @@
     moved = swap_seq(m)
     qkv_shard = jnp.concatenate([pick(y, a, moved), pick(y, e, a), pick(y, moved, e)], 1)
 
-    flow.add("skip", gather_both(spot, [skip_weight], False))
-    flow.add("qkv", gather_rows(spot, [qkv_shard]))
-    flow.add("text", gather_rows(spot, [text_proj, cross_kvproj]))
-    flow.add("outs", gather_both(spot, [attn_out, cross_qproj, cross_out], False))
-    flow.add("up", gather_rows(spot, [mlp_up]))
-    flow.add("down", gather_down(spot, mlp_down))
-    flow.step([], ["skip", "qkv", "text", "outs", "up", "down"])
-    flow.step([], ["skip"])
-    flow.step([], ["skip", "qkv"])
-    flow.step([], ["skip", "qkv", "text"])
+    def gather(shard):
+        return lax.all_gather(shard, DP, axis=0, tiled=True)
+
+    def with_far(own):
+        return own, swap_seq(own)
+
+    def times(value, sides):
+        return pair(y, project(value, sides[0]), project(value, sides[1]), 1)
+
+    def times_back(grad, sides):
+        first, second = halves_of(grad)
+        own, far = pick(y, first, second), pick(y, second, first)
+        return project_back(own, sides[0]) + project_back(far, sides[1])
+
+    w_skip = with_far(gather(skip_weight))
+    w_qkv = gather(qkv_shard)
+    w_text = gather(text_proj)
+    w_ckv = gather(cross_kvproj)
+    out_rows = lax.all_gather(jnp.concatenate([attn_out, cross_qproj, cross_out], 0), DP)
+    out_sides = with_far(out_rows.reshape(out_rows.shape[0], 3, -1, narrow_width))
+    w_aout, w_cq, w_cout = (
+        tuple(side[:, k].reshape(-1, narrow_width) for side in out_sides) for k in range(3)
+    )
+    w_up = gather(mlp_up)
+    down_rows = gather(mlp_down)
+    half_rows = down_rows.shape[0] // 2
+    upper_rows, lower_rows = down_rows[:half_rows], down_rows[half_rows:]
+    w_down = pick(y, upper_rows, lower_rows), swap_seq(pick(y, lower_rows, upper_rows))
     cot_far = swap_seq(cot_low)
-    flow.step([], ["skip", "text", "outs"])
-    flow.step([], ["skip", "qkv", "outs", "up"])
 
     feats = time_features(time_ids).astype(bf16)
     before = both_halves(project(feats, time_weights[0]))
@@ -941,19 +862,13 @@
 
     cosine, sine = rope_tables(*jnp.concatenate([pos, pos_far], 1))
     helpers = []
-    hidden, skip, cot_far = flow.step([hidden, skip, cot_far], ["skip", "qkv", "text", "outs"])
-    (w_skip,) = flow.done["skip"]
-    w_hidden, w_far = w_skip[:width], w_skip[width:]
-    merged = project(hidden, w_hidden) + project(skip, w_far)
+    merged = times(jnp.concatenate([hidden, skip], -1), w_skip)
     resid0 = scaled_norm(merged, norm_gains[0])
     normed1 = narrow(scaled_norm(resid0, norm_gains[1]) + shift)
-    (normed1,) = flow.step([normed1], ["qkv", "text", "up", "down"])
-    (w_qkv,) = flow.done["qkv"]
 
     normed1_both = jnp.concatenate([normed1, swap_seq(normed1)], 0)
     packed = narrow(project(normed1_both, w_qkv))
     self_gains = gain_rows(head_gains[0:2])
-    (packed,) = flow.step([packed], ["outs", "down", "text"])
     self_o, self_q, self_k, self_v = attend_forward(
         packed,
         packed,
@@ -967,57 +882,52 @@
         2 * narrow_width,
         2 * local,
     )
-    (self_o,) = flow.step([self_o], ["outs", "up", "down"])
     far_o = swap_seq(self_o[local:])
 
-    w_text, w_ckv = flow.done["text"]
     keep_text = (1 - null_text[0]).astype(bf16)
     projected = both_halves(narrow(project(mt5_text[0], w_text)))
     context = jnp.concatenate([clip_text[0], projected], 0) * keep_text
     context = jnp.pad(context, ((0, text_pad - text_len), (0, 0)))
     text_kv = both_halves(narrow(project(context, w_ckv)))
-    text_kv, own_o, far_o = flow.step([text_kv, self_o[:local], far_o], ["outs", "up", "down"])
-
-    w_aout, w_cq, w_cout = flow.done["outs"]
+    own_o = self_o[:local]
+
     attn_halves = pick(y, own_o, far_o), pick(y, far_o, own_o)
     attn_flat = jnp.concatenate(attn_halves, 1)
-    resid1 = resid0 + project(attn_flat, w_aout)
+    resid1 = resid0 + times(attn_flat, w_aout)
     normed2 = narrow(scaled_norm(resid1, norm_gains[2]))
-    cross_pre = narrow(project(normed2, w_cq))
+    cross_pre = narrow(times(normed2, w_cq))
     cross_gains = gain_rows(head_gains[2:4])
     cross_o, cross_q, cross_k, cross_v = attend_forward(
         cross_pre, text_kv, None, None, cross_gains, helpers, HEADS, 0, 0, width, text_len
     )
-    resid2 = resid1 + project(cross_o, w_cout)
+    resid2 = resid1 + times(cross_o, w_cout)
     normed3 = narrow(scaled_norm(resid2, norm_gains[3]))
-    (normed3,) = flow.step([normed3], ["up", "down"])
-    w_up, w_down = flow.finish("up")[0], flow.finish("down")
 
     normed3_both = jnp.concatenate([normed3, swap_seq(normed3)], 0)
     upper = narrow(project(normed3_both, w_up))
     active = narrow(gelu(upper.astype(jnp.float32)))
-    mixed = project(active, w_down)
+    mixed = times(active, w_down)
     final = resid2 + mixed[:local] + wide(swap_seq(narrow(mixed[local:])))
-    block_out = narrow(lax.optimization_barrier(final))[None]
+    block_out = narrow(final)[None]
 
     cot_both = jnp.concatenate([cot_low, cot_far], 0)
-    d_active = project_back(cot_both, w_down)
+    d_active = times_back(cot_both, w_down)
     _, gelu_back = jax.vjp(gelu, upper.astype(jnp.float32))
     d_upper = narrow(gelu_back(d_active)[0])
-    flow.add("g_down", reduce_down(spot, active, halves_of(cot_both)))
-    (d_upper,) = flow.step([d_upper], ["g_down"])
+    flow.add(8, reduce_down(spot, active, halves_of(cot_both)))
+    (d_upper,) = flow.step([d_upper], [8])
     d_both = project_back(d_upper, w_up)
     d_far = swap_seq(narrow(d_both[local:]))
-    flow.add("g_up", reduce_rows(spot, halves_of(normed3_both), d_upper))
-    d_own, d_far = flow.step([d_both[:local], d_far], ["g_down", "g_up"])
+    flow.add(7, reduce_rows(spot, halves_of(normed3_both), d_upper))
+    d_own, d_far = flow.step([d_both[:local], d_far], [8, 7])
     d_normed3 = d_own + wide(d_far)
     d_resid, d_gain3 = norm_grad(d_normed3, resid2, norm_gains[3])
     resid_grad = scaled_cot + d_resid
 
     grad_low = narrow(resid_grad)
-    d_cmix = narrow(project_back(grad_low, w_cout))
-    flow.add("g_cout", reduce_both(spot, halves_of(cross_o), halves_of(grad_low)))
-    (d_cmix,) = flow.step([d_cmix], ["g_cout"])
+    d_cmix = narrow(times_back(grad_low, w_cout))
+    flow.add(5, reduce_both(spot, halves_of(cross_o), halves_of(grad_low)))
+    (d_cmix,) = flow.step([d_cmix], [5])
     d_cpre, d_textkv, d_cross_gains = attend_backward(
         cross_pre,
         text_kv,
@@ -1035,28 +945,28 @@
         0,
         width,
     )
-    flow.add("g_cquery", reduce_both(spot, halves_of(normed2), halves_of(d_cpre)))
-    d_cpre, d_textkv = flow.step([d_cpre, d_textkv], ["g_down", "g_up", "g_cout", "g_cquery"])
+    flow.add(3, reduce_both(spot, halves_of(normed2), halves_of(d_cpre)))
+    d_cpre, d_textkv = flow.step([d_cpre, d_textkv], [8, 7, 5, 3])
     d_text = halves_of(d_textkv)
     d_text_far = swap_seq(pick(y, d_text[1], d_text[0]))
-    d_normed2 = project_back(d_cpre, w_cq)
+    d_normed2 = times_back(d_cpre, w_cq)
     d_resid, d_gain2 = norm_grad(d_normed2, resid1, norm_gains[2])
     resid_grad = resid_grad + d_resid
     grad_low = narrow(resid_grad)
-    d_attn = halves_of(narrow(project_back(grad_low, w_aout)))
+    d_attn = halves_of(narrow(times_back(grad_low, w_aout)))
     d_far = swap_seq(pick(y, d_attn[1], d_attn[0]))
     d_text = narrow(wide(pick(y, d_text[0], d_text[1])) + wide(d_text_far))
-    flow.add("g_aout", reduce_both(spot, attn_halves, halves_of(grad_low)))
-    flow.add("g_ckv", reduce_rows(spot, halves_of(context), d_text))
+    flow.add(2, reduce_both(spot, attn_halves, halves_of(grad_low)))
+    flow.add(4, reduce_rows(spot, halves_of(context), d_text))
     d_context = halves_of(project_back(d_text[clip_len:text_len], w_ckv))
     d_context_far = swap_seq(narrow(pick(y, d_context[1], d_context[0])))
     d_proj = pick(y, d_context[0], d_context[1]) + wide(d_context_far)
     d_proj = narrow(d_proj * keep_text.astype(jnp.float32))
-    flow.add("g_tproj", reduce_rows(spot, halves_of(mt5_text[0]), d_proj))
+    flow.add(6, reduce_rows(spot, halves_of(mt5_text[0]), d_proj))
 
     d_heads = jnp.concatenate([pick(y, d_attn[0], d_attn[1]), d_far], 0)
     (d_heads,) = flow.step(
-        [d_heads], ["g_down", "g_cout", "g_cquery", "g_aout", "g_ckv", "g_tproj"]
+        [d_heads], [8, 5, 3, 2, 4, 6]
     )
     d_packed, d_self_gains = attend_backward(
         packed,
@@ -1076,14 +986,14 @@
         2 * narrow_width,
     )
     (d_packed,) = flow.step(
-        [d_packed], ["g_down", "g_up", "g_cout", "g_cquery", "g_aout", "g_ckv", "g_tproj"]
+        [d_packed], [8, 7, 5, 3, 2, 4, 6]
     )
     d_both = project_back(d_packed, w_qkv)
     d_far = swap_seq(narrow(d_both[local:]))
-    flow.add("g_qkv", reduce_rows(spot, halves_of(normed1_both), d_packed))
+    flow.add(1, reduce_rows(spot, halves_of(normed1_both), d_packed))
     d_own, d_far = flow.step(
         [d_both[:local], d_far],
-        ["g_up", "g_cout", "g_cquery", "g_aout", "g_ckv", "g_tproj", "g_qkv"],
+        [7, 5, 3, 2, 4, 6, 1],
     )
     d_normed1 = d_own + wide(d_far)
 
@@ -1092,13 +1002,13 @@
     resid_grad = resid_grad + d_resid
     d_merged, d_gain0 = norm_grad(resid_grad, merged, norm_gains[0])
     d_merged = narrow(d_merged)
-    flow.add("g_skip", reduce_both(spot, (hidden, skip), halves_of(d_merged)))
+    flow.add(0, reduce_both(spot, (hidden, skip), halves_of(d_merged)))
     (d_merged,) = flow.step(
         [d_merged],
-        ["g_skip", "g_up", "g_cout", "g_cquery", "g_aout", "g_ckv", "g_tproj", "g_qkv"],
-    )
-    hidden_grad = project_back(d_merged, w_hidden)[None]
-    skip_grad = project_back(d_merged, w_far)[None]
+        [0, 7, 5, 3, 2, 4, 6, 1],
+    )
+    d_joined = times_back(d_merged, w_skip)
+    hidden_grad, skip_grad = d_joined[:, :width][None], d_joined[:, width:][None]
 
     d_shift = d_shift + swap_seq(d_shift)
     features = jnp.pad(feats.astype(jnp.float32), ((0, 0), (0, width - FREQ)))
@@ -1129,9 +1039,8 @@
 
     while flow.chains:
         flow.step([], list(flow.chains))
-    names = ["skip", "qkv", "aout", "cquery", "ckv", "cout", "tproj", "up", "down"]
     g_skipw, g_qkv, g_aout, g_cquery, g_ckv, g_cout, g_tproj, g_up, g_down = (
-        flow.done["g_" + name] for name in names
+        flow.done[name] for name in range(9)
     )
     q_cols, k_cols, v_cols = (
         g_qkv[:, i * narrow_width : (i + 1) * narrow_width] for i in range(3)
@@ -1160,49 +1069,49 @@
 
 def solution(mesh):
     placed = (
-        P("dp", "seq", None),
-        P("dp", "seq", None),
-        P("dp", None, None),
-        P("dp", None, None),
-        P("dp"),
-        P("dp"),
-        P("dp"),
-        P(None, "dp", "seq"),
-        P("dp", "seq", None),
-        P("dp", "seq"),
-        P("dp", "seq"),
-        P("dp", "seq"),
-        P("dp", "seq"),
-        P("dp", "seq"),
-        P("dp", "seq"),
-        P("dp", "seq"),
-        P("dp", "seq"),
-        P("dp", "seq"),
-        P("dp", "seq"),
-        P("dp", "seq"),
+        P(DP, SEQ, None),
+        P(DP, SEQ, None),
+        P(DP, None, None),
+        P(DP, None, None),
+        P(DP),
+        P(DP),
+        P(DP),
+        P(None, DP, SEQ),
+        P(DP, SEQ, None),
+        P(DP, SEQ),
+        P(DP, SEQ),
+        P(DP, SEQ),
+        P(DP, SEQ),
+        P(DP, SEQ),
+        P(DP, SEQ),
+        P(DP, SEQ),
+        P(DP, SEQ),
+        P(DP, SEQ),
+        P(DP, SEQ),
+        P(DP, SEQ),
         P(),
         P(),
     )
-    split = mesh.shape["dp"] == 16 and mesh.shape["seq"] == 2
+    split = mesh.shape[DP] == 16 and mesh.shape[SEQ] == 2
     return jax.shard_map(
-        fast_body if split else body,
+        fast_body if split else whole_body,
         mesh=mesh,
         in_specs=placed,
         out_specs=(
-            P("dp", "seq", None),
-            P("dp", "seq", None),
-            P("dp", "seq", None),
-            P("dp", "seq"),
-            P("dp", "seq"),
-            P("dp", "seq"),
-            P("dp", "seq"),
-            P("dp", "seq"),
-            P("dp", "seq"),
-            P("dp", "seq"),
-            P("dp", "seq"),
-            P("dp", "seq"),
-            P("dp", "seq"),
-            P("dp", "seq"),
+            P(DP, SEQ, None),
+            P(DP, SEQ, None),
+            P(DP, SEQ, None),
+            P(DP, SEQ),
+            P(DP, SEQ),
+            P(DP, SEQ),
+            P(DP, SEQ),
+            P(DP, SEQ),
+            P(DP, SEQ),
+            P(DP, SEQ),
+            P(DP, SEQ),
+            P(DP, SEQ),
+            P(DP, SEQ),
+            P(DP, SEQ),
             P(),
             P(),
         ),

time: 1720 us -> 1480 us (0.86)
  other arithmetic: 379 us -> 195 us
  starting transfers between devices: 158 us -> 103 us
  waiting for transfers between devices: 602 us -> 634 us
  local copies, waits for them, and re-layouts: 185 us -> 157 us
    all_gather x1 -> x8, waiting for transfers between devices: 0.01 us -> 215 us  [the longest x6 147 us: gather(): return lax.all_gather(shard, DP, axis=0, tiled=True)]
    ppermute x102 -> x74, waiting for transfers between devices: 517 us -> 373 us  [the longest x27 245 us: swap_seq(): return lax.ppermute(value, SEQ, FLIP)]
    select_n x20 -> x9, other arithmetic: 48 us -> 4.02 us  [pair(): jnp.where(flag == 0, jnp.concatenate([own, other], axis), jnp.concatenate...]
    ppermute x20 -> x11, waiting for transfers between devices: 85.6 us -> 43.8 us  [by_routes(): return lambda value: lax.ppermute(value, BOTH, pairs)]
    unnamed x42 -> x5, other arithmetic: 36.2 us -> 0.01 us
    scatter-add x2 -> x0, other arithmetic: 30.7 us -> none  [prepared(): other = v[..., partner(jnp.arange(HEAD_DIM))]]
    ppermute x102 -> x74, starting transfers between devices: 118 us -> 87.8 us  [the longest x47 51.5 us: swap(): return lax.ppermute(value, DP, [(i, i ^ bit) for i in range(16)])]
    ppermute x20 -> x11, starting transfers between devices: 40.2 us -> 14.7 us  [by_routes(): return lambda value: lax.ppermute(value, BOTH, pairs)]
  transfers between devices with their start and end apart: 123 -> 93, of which waited for: 49 -> 43; matrix products, arithmetic and copies ran while one was open for 42% -> 39% of each run, Pallas kernels for 0% -> 0%
where the time goes in v2:
time: 1480 us; the launch traced here: 1470 us
  waiting for transfers between devices  634 us (43%)
  matrix products  360 us (24%)
  other arithmetic  195 us (13%)
  local copies, waits for them, and re-layouts  157 us (11%)
  starting transfers between devices  103 us (7%)
  between operations  20.1 us (1%)
    ppermute x27, waiting for transfers between devices, swap_seq(): return lax.ppermute(value, SEQ, FLIP)  245 us
    all_gather x6, waiting for transfers between devices, gather(): return lax.all_gather(shard, DP, axis=0, tiled=True)  147 us
    ppermute x47, waiting for transfers between devices, swap(): return lax.ppermute(value, DP, [(i, i ^ bit) for i in range(16)])  128 us
    dot_general x26, matrix products, dot_rows(): jnp.einsum('tc,td->cd', left, right, preferred_element_type=jnp.float32)  93.9 us
    dot_general x13, matrix products, project_back(): jnp.einsum('td,cd->tc', grad_low, right, preferred_element_type=jnp.float32)  78.7 us
    dot_general x16, matrix products, project(): jnp.einsum('tc,cd->td', left, right, preferred_element_type=jnp.float32)  71.1 us
    ppermute x47, starting transfers between devices, swap(): return lax.ppermute(value, DP, [(i, i ^ bit) for i in range(16)])  51.5 us
    dot_general x6, matrix products, attend(): o = jnp.einsum('hqk,khd->qhd', p, v, preferred_element_type=jnp.float32)  48.3 us
  transfers between devices with their start and end apart: 93, of which 43 were waited for; matrix products, arithmetic and copies ran while one was open for 39% of the time, Pallas kernels for 0%

profile of v2, /device:TPU:0, one launch (start us, length us, event | category | flops | bytes accessed | tf_op | source)
XLA Modules:
  0.0 1468.6 jit_solution(7379056970565184148)
XLA Ops:
  28.9 35.4 %all-gather.12.cloned.1.call-done = bf16[2816,704]{1,0:T(8,128)(2,1)} async-done(((bf16[176,704]{1,0:T(8,128)(2,1)}), bf16[2816,704]{1,0:T(8,128)(2,1)}) %all-gather.12.cloned.1.call-update) | async-done | bytes 3964944 | tf_op jit(solution)/shard_map/all_gather | solution.py:829
  75.0 31.2 %all-gather.16.cloned.1.call-done = bf16[2048,512]{1,0:T(8,128)(2,1)} async-done(((bf16[128,512]{1,0:T(8,128)(2,1)}), bf16[2048,512]{1,0:T(8,128)(2,1)}) %all-gather.16.cloned.1.call-update) | async-done | bytes 2097168 | tf_op jit(solution)/shard_map/all_gather | solution.py:829
  110.8 40.0 %all-gather.22.cloned.1.call-done = bf16[1664,704]{1,0:T(8,128)(2,1)} async-done(((bf16[104,704]{1,0:T(8,128)(2,1)}), bf16[1664,704]{1,0:T(8,128)(2,1)}) %all-gather.22.cloned.1.call-update) | async-done | bytes 2342928 | tf_op jit(solution)/shard_map/all_gather | solution.py:808
  170.6 25.6 %all-gather.18.cloned.1.call-done = bf16[1024,1408]{1,0:T(8,128)(2,1)} async-done(((bf16[64,1408]{1,0:T(8,128)(2,1)}), bf16[1024,1408]{1,0:T(8,128)(2,1)}) %all-gather.18.cloned.1.call-update) | async-done | bytes 2883600 | tf_op jit(solution)/shard_map/all_gather | solution.py:829
  232.3 27.9 %all-gather.24.cloned.1.call-done = bf16[4224,704]{1,0:T(8,128)(2,1)} async-done(((bf16[264,704]{1,0:T(8,128)(2,1)}), bf16[4224,704]{1,0:T(8,128)(2,1)}) %all-gather.24.cloned.1.call-update) | async-done | bytes 5947408 | tf_op jit(solution)/shard_map/all_gather | solution.py:846
  267.6 54.6 %all-gather.14.cloned.1.call-done = bf16[1408,2112]{1,0:T(8,128)(2,1)} async-done(((bf16[88,2112]{1,0:T(8,128)(2,1)}), bf16[1408,2112]{1,0:T(8,128)(2,1)}) %all-gather.14.cloned.1.call-update) | async-done | bytes 5947408 | tf_op jit(solution)/shard_map/all_gather | solution.py:829
  352.2 31.0 %fusion.258 = (f32[8,1024]{1,0:T(8,128)S(1)}, f32[8,1024,1024]{1,2,0:T(8,128)}) fusion(pred[1024]{0:T(1024)(128)(4,1)S(1)} %iota_compare_fusion, bf16[1024,8,88]{0,2,1:T(8,128)(2,1)} %get-tuple-element.313, bf16[1024,8,88]{0,2,1:T(8,128)(2,1)} %get-tuple-element.312), kind=kOutput, calls=%fused_computation.580 | convolution fusion | flops 1509950464 | bytes 36471808 | tf_op jit(solution)/shard_map/jvp()/sub | solution.py:707
  383.3 13.4 divide_convert_fusion
  519.2 16.2 %convolution_convert_fusion.1 = bf16[1024,3168]{0,1:T(8,128)(2,1)} fusion(bf16[1408,3168]{1,0:T(8,128)(2,1)} %all-gather.20.cloned.1.call-done, bf16[512,1408]{0,1:T(8,128)(2,1)} %collective-permute-done.10, bf16[512,1408]{0,1:T(8,128)(2,1)S(1)} %multiply_convert_fusion.1), kind=kOutput, calls=%fused_computation.48 | convolution fusion | flops 9144205312 | bytes 18292736 | tf_op jit(solution)/shard_map/tc,cd->td/dot_general | solution.py:56
  552.0 61.6 %collective-permute-done.11 = bf16[3168,704]{0,1:T(8,128)(2,1)} collective-permute-done((bf16[3168,704]{0,1:T(8,128)(2,1)}, bf16[3168,704]{0,1:T(8,128)(2,1)}, u32[]{:S(2)}, u32[]{:S(2)}) %collective-permute-start.11) | collective-permute-done | bytes 4460576 | tf_op jit(solution)/shard_map/ppermute | solution.py:488
  624.1 17.7 %fusion.15 = bf16[1024,3168]{0,1:T(8,128)(2,1)} fusion(bf16[1024,3168]{0,1:T(8,128)(2,1)} %convolution_convert_fusion.1, f32[1024,3168]{0,1:T(8,128)} %fusion.94, bf16[3168,704]{1,0:T(8,128)(2,1)S(1)} %copy-done.54, bf16[1024,704]{0,1:T(8,128)(2,1)S(1)} %get-tuple-element.284, bf16[1024,704]{0,1:T(8,128)(2,1)S(1)} %copy-done.121, pred[]{:T(512)S(6)} %eq.28), kind=kOutput, calls=%fused_computation.27 | convolution fusion | flops 4639686656 | bytes 33296384 | tf_op jit(solution)/shard_map/td,cd->tc/dot_general | solution.py:60
  641.8 14.2 fusion.267
  706.7 16.3 %collective-permute-done.12 = bf16[512,1408]{0,1:T(8,128)(2,1)} collective-permute-done((bf16[512,1408]{0,1:T(8,128)(2,1)}, bf16[512,1408]{0,1:T(8,128)(2,1)}, u32[]{:S(2)}, u32[]{:S(2)}) %collective-permute-start.12) | collective-permute-done | bytes 1441824 | tf_op jit(solution)/shard_map/ppermute | solution.py:488
  790.3 24.7 %collective-permute-done.16 = bf16[2,792,704]{2,1,0:T(8,128)(2,1)} collective-permute-done((bf16[2,792,704]{2,1,0:T(8,128)(2,1)}, bf16[2,792,704]{2,1,0:T(8,128)(2,1)}, u32[]{:S(2)}, u32[]{:S(2)}) %collective-permute-start.16) | collective-permute-done | bytes 2230304 | tf_op jit(solution)/shard_map/ppermute | solution.py:484
  866.5 20.8 %collective-permute-done.22 = bf16[704,704]{1,0:T(8,128)(2,1)S(1)} collective-permute-done((bf16[704,704]{1,0:T(8,128)(2,1)}, bf16[704,704]{1,0:T(8,128)(2,1)S(1)}, u32[]{:S(2)}, u32[]{:S(2)}) %collective-permute-start.22) | collective-permute-done | bytes 991264 | tf_op jit(solution)/shard_map/ppermute | solution.py:488
  890.1 18.3 %collective-permute-done.24 = bf16[384,1408]{0,1:T(8,128)(2,1)S(1)} collective-permute-done((bf16[384,1408]{0,1:T(8,128)(2,1)S(1)}, bf16[384,1408]{0,1:T(8,128)(2,1)S(1)}, u32[]{:S(2)}, u32[]{:S(2)}) %collective-permute-start.24) | collective-permute-done | bytes 1081376 | tf_op jit(solution)/shard_map/ppermute | solution.py:488
  918.8 17.6 %fusion.7 = (f32[8,1024]{1,0:T(8,128)S(1)}, bf16[8,1024,1024]{1,2,0:T(8,128)(2,1)}) fusion(f32[8,1024,1024]{1,2,0:T(8,128)} %get-tuple-element.342, f32[8,1024]{1,0:T(8,128)S(1)} %copy-done.133, bf16[8,88,1024]{2,1,0:T(8,128)(2,1)S(1)} %bitcast.449, bf16[1024,8,88]{0,2,1:T(8,128)(2,1)S(1)} %bitcast.448), kind=kOutput, calls=%fused_computation.9 | convolution fusion | flops 1518329856 | bytes 53280768 | tf_op jit(solution)/shard_map/transpose(jvp(hqk,khd->qhd))/dot_general | solution.py:708
  936.5 23.6 %fusion.5 = bf16[8,1024,1024]{1,2,0:T(8,128)(2,1)} fusion(f32[8,1024,1024]{1,2,0:T(8,128)} %get-tuple-element.342, bf16[8,1024,1024]{1,2,0:T(8,128)(2,1)} %get-tuple-element.353, f32[8,1024]{1,0:T(8,128)S(1)} %neg.49, f32[8,1024]{1,0:T(8,128)S(1)} %copy-done.159, pred[1024]{0:T(1024)(128)(4,1)S(1)} %copy-done.203), kind=kLoop, calls=%fused_computation.7 | loop fusion | flops 58720256 | bytes 67175424 | tf_op jit(solution)/shard_map/transpose(jvp())/mul | solution.py:705
  1079.8 23.2 %collective-permute-done.41 = bf16[2,256,512]{2,1,0:T(8,128)(2,1)S(1)} collective-permute-done((bf16[2,256,512]{2,1,0:T(8,128)(2,1)S(1)}, bf16[2,256,512]{2,1,0:T(8,128)(2,1)S(1)}, u32[]{:S(2)}, u32[]{:S(2)}) %collective-permute-start.41) | collective-permute-done | bytes 524320 | tf_op jit(solution)/shard_map/ppermute | solution.py:484
  1110.0 47.9 %collective-permute-done.39 = bf16[704,704]{1,0:T(8,128)(2,1)S(1)} collective-permute-done((bf16[704,704]{1,0:T(8,128)(2,1)S(1)}, bf16[704,704]{1,0:T(8,128)(2,1)S(1)}, u32[]{:S(2)}, u32[]{:S(2)}) %collective-permute-start.39) | collective-permute-done | bytes 991264 | tf_op jit(solution)/shard_map/ppermute | solution.py:488
  1222.0 13.4 collective-permute-start.77
  1329.0 22.3 %collective-permute-done.60 = bf16[1408,704]{0,1:T(8,128)(2,1)S(1)} collective-permute-done((bf16[1408,704]{0,1:T(8,128)(2,1)S(1)}, bf16[1408,704]{0,1:T(8,128)(2,1)S(1)}, u32[]{:S(2)}, u32[]{:S(2)}) %collective-permute-start.60) | collective-permute-done | bytes 1982496 | tf_op jit(solution)/shard_map/ppermute | solution.py:488
  1398.5 13.7 collective-permute-done.66
  1439.4 13.7 collective-permute-done.71
  (953 shorter events, 824.3 us)
Async XLA Ops:
  7.2 57.1 %all-gather.12.cloned.1.call-start = ((), (), s32[]{:S(2)}) async-start(), calls=%async_computation | async-start | bytes 4595712 | tf_op jit(solution)/shard_map/all_gather | solution.py:829
  7.9 98.3 %all-gather.16.cloned.1.call-start = ((), (), s32[]{:S(2)}) async-start(), calls=%async_computation.2 | async-start | bytes 2228224 | tf_op jit(solution)/shard_map/all_gather | solution.py:829
  8.7 142.2 %all-gather.22.cloned.1.call-start = ((), (), s32[]{:S(2)}) async-start(), calls=%async_computation.5 | async-start | bytes 2715648 | tf_op jit(solution)/shard_map/all_gather | solution.py:808
  10.3 185.9 %all-gather.18.cloned.1.call-start = ((), (), s32[]{:S(2)}) async-start(), calls=%async_computation.3 | async-start | bytes 3063808 | tf_op jit(solution)/shard_map/all_gather | solution.py:829
  10.9 249.3 %all-gather.24.cloned.1.call-start = ((), (), s32[]{:S(2)}) async-start(), calls=%async_computation.6 | async-start | bytes 6893568 | tf_op jit(solution)/shard_map/all_gather | solution.py:846
  12.8 309.4 %all-gather.14.cloned.1.call-start = ((), (), s32[]{:S(2)}) async-start(), calls=%async_computation.1 | async-start | bytes 6510592 | tf_op jit(solution)/shard_map/all_gather | solution.py:829
  22.4 467.5 %all-gather.26.cloned.1.call-start = ((), (), s32[]{:S(2)}) async-start(), calls=%async_computation.7 | async-start | bytes 10444800 | tf_op jit(solution)/shard_map/all_gather | solution.py:829
  23.2 496.0 %all-gather.20.cloned.1.call-start = ((), (), s32[]{:S(2)}) async-start(), calls=%async_computation.4 | async-start | bytes 9574400 | tf_op jit(solution)/shard_map/all_gather | solution.py:829
  27.9 457.4 %collective-permute-start.13 = (bf16[512,1408]{0,1:T(8,128)(2,1)}, bf16[512,1408]{0,1:T(8,128)(2,1)}, u32[]{:S(2)}, u32[]{:S(2)}) collective-permute-start(bf16[512,1408]{0,1:T(8,128)(2,1)} %bitcast_convert_fusion), channel_id=1, source_target_pairs={{0,1},{1,0},{2,3},{3,2},{4,5},{5,4},{6,7},{7,6},{8,9},{9,8},{10,11... | collective-permute-start | bytes 4325384 | tf_op jit(solution)/shard_map/ppermute | solution.py:488
  70.6 135.0 %collective-permute-start = (bf16[2816,704]{0,1:T(8,128)(2,1)}, bf16[2816,704]{0,1:T(8,128)(2,1)}, u32[]{:S(2)}, u32[]{:S(2)}) collective-permute-start(bf16[2816,704]{0,1:T(8,128)(2,1)} %copy.128), channel_id=1, source_target_pairs={{0,1},{1,0},{2,3},{3,2},{4,5},{5,4},{6,7},{7,6},{8,9},{9,8},{10,11... | collective-permute-start | bytes 11894792 | tf_op jit(solution)/shard_map/ppermute | solution.py:488
  108.6 55.8 %collective-permute-start.8 = (bf16[256,512]{1,0:T(8,128)(2,1)S(1)}, bf16[256,512]{1,0:T(8,128)(2,1)S(1)}, u32[]{:S(2)}, u32[]{:S(2)}) collective-permute-start(bf16[256,512]{1,0:T(8,128)(2,1)S(1)} %convolution_convert_fusion.26), channel_id=1, source_target_pairs={{0,1},{1,0},{2,3},{3,2},{4,5},{5,4},{6,7},{7,6},{8,9},{9,8},{10,11... | collective-permute-start | bytes 786440 | tf_op jit(solution)/shard_map/ppermute | solution.py:488
  215.9 106.3 %collective-permute-start.3 = (bf16[512,1408]{0,1:T(8,128)(2,1)}, bf16[512,1408]{0,1:T(8,128)(2,1)}, u32[]{:S(2)}, u32[]{:S(2)}) collective-permute-start(bf16[512,1408]{0,1:T(8,128)(2,1)} %add_convert_fusion.8), channel_id=1, source_target_pairs={{0,1},{1,0},{2,3},{3,2},{4,5},{5,4},{6,7},{7,6},{8,9},{9,8},{10,11... | collective-permute-start | bytes 4325384 | tf_op jit(solution)/shard_map/ppermute | solution.py:488
  266.1 162.1 %collective-permute-start.7 = (bf16[16,3,88,704]{3,2,0,1:T(8,128)(2,1)}, bf16[16,3,88,704]{3,2,0,1:T(8,128)(2,1)}, u32[]{:S(2)}, u32[]{:S(2)}) collective-permute-start(bf16[16,3,88,704]{3,2,0,1:T(8,128)(2,1)} %copy.130), channel_id=1, source_target_pairs={{0,1},{1,0},{2,3},{3,2},{4,5},{5,4},{6,7},{7,6},{8,9},{9,8},{10,11... | collective-permute-start | bytes 17842184 | tf_op jit(solution)/shard_map/ppermute | solution.py:488
  511.8 101.7 %collective-permute-start.11 = (bf16[3168,704]{0,1:T(8,128)(2,1)}, bf16[3168,704]{0,1:T(8,128)(2,1)}, u32[]{:S(2)}, u32[]{:S(2)}) collective-permute-start(bf16[3168,704]{0,1:T(8,128)(2,1)} %copy.139), channel_id=1, source_target_pairs={{0,1},{1,0},{2,3},{3,2},{4,5},{5,4},{6,7},{7,6},{8,9},{9,8},{10,11... | collective-permute-start | bytes 13381640 | tf_op jit(solution)/shard_map/ppermute | solution.py:488
  760.1 54.8 %collective-permute-start.16 = (bf16[2,792,704]{2,1,0:T(8,128)(2,1)}, bf16[2,792,704]{2,1,0:T(8,128)(2,1)}, u32[]{:S(2)}, u32[]{:S(2)}) collective-permute-start(bf16[2,792,704]{2,1,0:T(8,128)(2,1)} %dynamic-slice_bitcast_fusion), channel_id=1, source_target_pairs={{0,4},{2,6},{4,0},{6,2},{8,12},{10,14},{12,8},{14,10},{16,20},{18,... | collective-permute-start | bytes 6690824 | tf_op jit(solution)/shard_map/ppermute | solution.py:484
  761.0 56.4 %collective-permute-start.17 = (bf16[704,3168]{1,0:T(8,128)(2,1)}, bf16[704,3168]{1,0:T(8,128)(2,1)}, u32[]{:S(2)}, u32[]{:S(2)}) collective-permute-start(bf16[704,3168]{1,0:T(8,128)(2,1)} %convolution_convert_fusion.2), channel_id=1, source_target_pairs={{0,2},{2,0},{4,6},{6,4},{8,10},{10,8},{12,14},{14,12},{16,18},{18,... | collective-permute-start | bytes 13381640 | tf_op jit(solution)/shard_map/ppermute | solution.py:484
  779.8 86.1 %collective-permute-start.21 = (bf16[704,704]{1,0:T(8,128)(2,1)}, bf16[704,704]{1,0:T(8,128)(2,1)S(1)}, u32[]{:S(2)}, u32[]{:S(2)}) collective-permute-start(bf16[704,704]{1,0:T(8,128)(2,1)} %convolution_convert_fusion.24), channel_id=1, source_target_pairs={{0,2},{2,0},{4,6},{6,4},{8,10},{10,8},{12,14},{14,12},{16,18},{18,... | collective-permute-start | bytes 2973704 | tf_op jit(solution)/shard_map/ppermute | solution.py:484
  849.0 59.3 %collective-permute-start.24 = (bf16[384,1408]{0,1:T(8,128)(2,1)S(1)}, bf16[384,1408]{0,1:T(8,128)(2,1)S(1)}, u32[]{:S(2)}, u32[]{:S(2)}) collective-permute-start(bf16[384,1408]{0,1:T(8,128)(2,1)S(1)} %broadcast_select_fusion.4), channel_id=1, source_target_pairs={{0,1},{1,0},{2,3},{3,2},{4,5},{5,4},{6,7},{7,6},{8,9},{9,8},{10,11... | collective-permute-start | bytes 3244040 | tf_op jit(solution)/shard_map/ppermute | solution.py:488
  865.9 152.7 %collective-permute-start.27 = (bf16[2,176,3168]{2,1,0:T(8,128)(2,1)}, bf16[2,176,3168]{2,1,0:T(8,128)(2,1)}, u32[]{:S(2)}, u32[]{:S(2)}) collective-permute-start(bf16[2,176,3168]{2,1,0:T(8,128)(2,1)} %dynamic-slice_bitcast_fusion.1), channel_id=1, source_target_pairs={{0,4},{2,6},{4,0},{6,2},{8,12},{10,14},{12,8},{14,10},{16,20},{18,... | collective-permute-start | bytes 6690824 | tf_op jit(solution)/shard_map/ppermute | solution.py:484
  887.4 134.9 %collective-permute-start.29 = (bf16[704,704]{1,0:T(8,128)(2,1)}, bf16[704,704]{1,0:T(8,128)(2,1)}, u32[]{:S(2)}, u32[]{:S(2)}) collective-permute-start(bf16[704,704]{1,0:T(8,128)(2,1)} %convolution_convert_fusion.22), channel_id=1, source_target_pairs={{0,2},{2,0},{4,6},{6,4},{8,10},{10,8},{12,14},{14,12},{16,18},{18,... | collective-permute-start | bytes 2973704 | tf_op jit(solution)/shard_map/ppermute | solution.py:484
  988.4 54.7 %collective-permute-start.26 = (bf16[792,704]{1,0:T(8,128)(2,1)}, bf16[792,704]{1,0:T(8,128)(2,1)}, u32[]{:S(2)}, u32[]{:S(2)}) collective-permute-start(bf16[792,704]{1,0:T(8,128)(2,1)} %fusion.66), channel_id=1, source_target_pairs={{16,0},{18,2},{20,4},{22,6},{24,8},{26,10},{28,12},{30,14},{1,17},... | collective-permute-start | bytes 3345416 | tf_op jit(solution)/shard_map/ppermute | solution.py:595
  1022.7 87.3 %collective-permute-start.38 = (bf16[704,704]{1,0:T(8,128)(2,1)}, bf16[704,704]{1,0:T(8,128)(2,1)}, u32[]{:S(2)}, u32[]{:S(2)}) collective-permute-start(bf16[704,704]{1,0:T(8,128)(2,1)} %convolution_convert_fusion.20), channel_id=1, source_target_pairs={{0,2},{2,0},{4,6},{6,4},{8,10},{10,8},{12,14},{14,12},{16,18},{18,... | collective-permute-start | bytes 2973704 | tf_op jit(solution)/shard_map/ppermute | solution.py:484
  1103.0 58.7 %collective-permute-start.34 = (bf16[512,1408]{0,1:T(8,128)(2,1)S(1)}, bf16[512,1408]{0,1:T(8,128)(2,1)S(1)}, u32[]{:S(2)}, u32[]{:S(2)}) collective-permute-start(bf16[512,1408]{0,1:T(8,128)(2,1)S(1)} %slice.720), channel_id=1, source_target_pairs={{0,1},{1,0},{2,3},{3,2},{4,5},{5,4},{6,7},{7,6},{8,9},{9,8},{10,11... | collective-permute-start | bytes 4325384 | tf_op jit(solution)/shard_map/ppermute | solution.py:488
  1104.5 55.9 %collective-permute-start.35 = (bf16[176,3168]{1,0:T(8,128)(2,1)S(1)}, bf16[176,3168]{1,0:T(8,128)(2,1)S(1)}, u32[]{:S(2)}, u32[]{:S(2)}) collective-permute-start(bf16[176,3168]{1,0:T(8,128)(2,1)S(1)} %copy-done.125), channel_id=1, source_target_pairs={{0,8},{2,10},{4,12},{6,14},{8,0},{10,2},{12,4},{14,6},{16,24},{18,... | collective-permute-start | bytes 3345416 | tf_op jit(solution)/shard_map/ppermute | solution.py:484
  (292 other events, 6851.7 us)
Sparse Core Ops, SparseCore 0:
  10.3 53.9 all-gather.11
  66.5 39.7 all-gather.15
  109.0 41.7 all-gather.21
  153.0 43.1 all-gather.17
  198.8 61.3 all-gather.23
  262.8 59.4 all-gather.13
  324.5 82.4 all-gather.25
  409.2 76.9 all-gather.19

commit v3 on v2

--- a/solution.py
+++ b/solution.py
@@ -831,6 +831,13 @@
     def with_far(own):
         return own, swap_seq(own)
 
+    def scatter_rows(grad):
+        return wide(lax.psum_scatter(narrow(grad), DP, scatter_dimension=0, tiled=True))
+
+    def scatter_both(grad):
+        first, second = halves_of(scatter_rows(grad))
+        return pick(y, first, second) + wide(swap_seq(narrow(pick(y, second, first))))
+
     def times(value, sides):
         return pair(y, project(value, sides[0]), project(value, sides[1]), 1)
 
@@ -849,10 +856,16 @@
         tuple(side[:, k].reshape(-1, narrow_width) for side in out_sides) for k in range(3)
     )
     w_up = gather(mlp_up)
-    down_rows = gather(mlp_down)
-    half_rows = down_rows.shape[0] // 2
-    upper_rows, lower_rows = down_rows[:half_rows], down_rows[half_rows:]
-    w_down = pick(y, upper_rows, lower_rows), swap_seq(pick(y, lower_rows, upper_rows))
+    down_rows = lax.all_gather(mlp_down, DP)
+    middle = down_rows.shape[0] // 2
+    upper_rows, lower_rows = down_rows[:middle], down_rows[middle:]
+    w_down = tuple(
+        side.reshape(-1, narrow_width)
+        for side in (
+            pick(y, upper_rows, lower_rows),
+            swap_seq(pick(y, lower_rows, upper_rows)),
+        )
+    )
     cot_far = swap_seq(cot_low)
 
     feats = time_features(time_ids).astype(bf16)
@@ -926,8 +939,7 @@
 
     grad_low = narrow(resid_grad)
     d_cmix = narrow(times_back(grad_low, w_cout))
-    flow.add(5, reduce_both(spot, halves_of(cross_o), halves_of(grad_low)))
-    (d_cmix,) = flow.step([d_cmix], [5])
+    g_cout = scatter_both(dot_rows(cross_o, grad_low))
     d_cpre, d_textkv, d_cross_gains = attend_backward(
         cross_pre,
         text_kv,
@@ -945,8 +957,8 @@
         0,
         width,
     )
-    flow.add(3, reduce_both(spot, halves_of(normed2), halves_of(d_cpre)))
-    d_cpre, d_textkv = flow.step([d_cpre, d_textkv], [8, 7, 5, 3])
+    g_cquery = scatter_both(dot_rows(normed2, d_cpre))
+    d_cpre, d_textkv = flow.step([d_cpre, d_textkv], [8, 7])
     d_text = halves_of(d_textkv)
     d_text_far = swap_seq(pick(y, d_text[1], d_text[0]))
     d_normed2 = times_back(d_cpre, w_cq)
@@ -956,18 +968,16 @@
     d_attn = halves_of(narrow(times_back(grad_low, w_aout)))
     d_far = swap_seq(pick(y, d_attn[1], d_attn[0]))
     d_text = narrow(wide(pick(y, d_text[0], d_text[1])) + wide(d_text_far))
-    flow.add(2, reduce_both(spot, attn_halves, halves_of(grad_low)))
-    flow.add(4, reduce_rows(spot, halves_of(context), d_text))
+    g_aout = scatter_both(dot_rows(attn_flat, grad_low))
+    g_ckv = scatter_rows(dot_rows(context, d_text))
     d_context = halves_of(project_back(d_text[clip_len:text_len], w_ckv))
     d_context_far = swap_seq(narrow(pick(y, d_context[1], d_context[0])))
     d_proj = pick(y, d_context[0], d_context[1]) + wide(d_context_far)
     d_proj = narrow(d_proj * keep_text.astype(jnp.float32))
-    flow.add(6, reduce_rows(spot, halves_of(mt5_text[0]), d_proj))
+    g_tproj = scatter_rows(dot_rows(mt5_text[0], d_proj))
 
     d_heads = jnp.concatenate([pick(y, d_attn[0], d_attn[1]), d_far], 0)
-    (d_heads,) = flow.step(
-        [d_heads], [8, 5, 3, 2, 4, 6]
-    )
+    (d_heads,) = flow.step([d_heads], [8])
     d_packed, d_self_gains = attend_backward(
         packed,
         packed,
@@ -985,15 +995,13 @@
         narrow_width,
         2 * narrow_width,
     )
-    (d_packed,) = flow.step(
-        [d_packed], [8, 7, 5, 3, 2, 4, 6]
-    )
+    (d_packed,) = flow.step([d_packed], [8, 7])
     d_both = project_back(d_packed, w_qkv)
     d_far = swap_seq(narrow(d_both[local:]))
     flow.add(1, reduce_rows(spot, halves_of(normed1_both), d_packed))
     d_own, d_far = flow.step(
         [d_both[:local], d_far],
-        [7, 5, 3, 2, 4, 6, 1],
+        [7, 1],
     )
     d_normed1 = d_own + wide(d_far)
 
@@ -1005,7 +1013,7 @@
     flow.add(0, reduce_both(spot, (hidden, skip), halves_of(d_merged)))
     (d_merged,) = flow.step(
         [d_merged],
-        [0, 7, 5, 3, 2, 4, 6, 1],
+        [0, 7, 1],
     )
     d_joined = times_back(d_merged, w_skip)
     hidden_grad, skip_grad = d_joined[:, :width][None], d_joined[:, width:][None]
@@ -1039,9 +1047,7 @@
 
     while flow.chains:
         flow.step([], list(flow.chains))
-    g_skipw, g_qkv, g_aout, g_cquery, g_ckv, g_cout, g_tproj, g_up, g_down = (
-        flow.done[name] for name in range(9)
-    )
+    g_skipw, g_qkv, g_up, g_down = (flow.done[name] for name in (0, 1, 7, 8))
     q_cols, k_cols, v_cols = (
         g_qkv[:, i * narrow_width : (i + 1) * narrow_width] for i in range(3)
     )

time: 1480 us -> 1420 us (0.959)
  waiting for transfers between devices: 634 us -> 570 us
  local copies, waits for them, and re-layouts: 157 us -> 172 us
    all_gather x6 -> x5, waiting for transfers between devices: 147 us -> 121 us  [gather(): return lax.all_gather(shard, DP, axis=0, tiled=True)]
    ppermute x27, waiting for transfers between devices: 245 us -> 222 us  [swap_seq(): return lax.ppermute(value, SEQ, FLIP)]
    dot_general x26 -> x15, matrix products: 93.9 us -> 81.7 us  [dot_rows(): jnp.einsum('tc,td->cd', left, right, preferred_element_type=jnp.float32)]
    unnamed x452 -> x401, local copies, waits for them, and re-layouts: 44.2 us -> 52.3 us
    ppermute x47 -> x24, starting transfers between devices: 51.5 us -> 43.5 us  [swap(): return lax.ppermute(value, DP, [(i, i ^ bit) for i in range(16)])]
    ppermute x11 -> x6, waiting for transfers between devices: 43.8 us -> 40.6 us  [by_routes(): return lambda value: lax.ppermute(value, BOTH, pairs)]
    convert_element_type x38 -> x25, other arithmetic: 46.8 us -> 43.8 us  [narrow(): return value.astype(jnp.bfloat16)]
    ppermute x47 -> x24, waiting for transfers between devices: 128 us -> 127 us  [swap(): return lax.ppermute(value, DP, [(i, i ^ bit) for i in range(16)])]
  transfers between devices with their start and end apart: 93 -> 70, of which waited for: 43 -> 35; matrix products, arithmetic and copies ran while one was open for 39% -> 44% of each run, Pallas kernels for 0% -> 0%
where the time goes in v3:
time: 1420 us; the launch traced here: 1410 us
  waiting for transfers between devices  570 us (40%)
  matrix products  346 us (24%)
  other arithmetic  203 us (14%)
  local copies, waits for them, and re-layouts  172 us (12%)
  starting transfers between devices  97 us (7%)
  between operations  19.4 us (1%)
    ppermute x27, waiting for transfers between devices, swap_seq(): return lax.ppermute(value, SEQ, FLIP)  222 us
    ppermute x24, waiting for transfers between devices, swap(): return lax.ppermute(value, DP, [(i, i ^ bit) for i in range(16)])  127 us
    all_gather x5, waiting for transfers between devices, gather(): return lax.all_gather(shard, DP, axis=0, tiled=True)  121 us
    dot_general x15, matrix products, dot_rows(): jnp.einsum('tc,td->cd', left, right, preferred_element_type=jnp.float32)  81.7 us
    dot_general x13, matrix products, project_back(): jnp.einsum('td,cd->tc', grad_low, right, preferred_element_type=jnp.float32)  80.6 us
    dot_general x16, matrix products, project(): jnp.einsum('tc,cd->td', left, right, preferred_element_type=jnp.float32)  72.9 us
    unnamed x401, local copies, waits for them, and re-layouts  52.3 us
    dot_general x6, matrix products, attend(): o = jnp.einsum('hqk,khd->qhd', p, v, preferred_element_type=jnp.float32)  49.4 us
  transfers between devices with their start and end apart: 70, of which 35 were waited for; matrix products, arithmetic and copies ran while one was open for 44% of the time, Pallas kernels for 0%

profile of v3, /device:TPU:0, one launch (start us, length us, event | category | flops | bytes accessed | tf_op | source)
XLA Modules:
  0.0 1406.7 jit_solution(4841760693863860043)
XLA Ops:
  27.4 36.8 %all-gather.13.cloned.1.call-done = bf16[2816,704]{1,0:T(8,128)(2,1)} async-done(((bf16[176,704]{1,0:T(8,128)(2,1)}), bf16[2816,704]{1,0:T(8,128)(2,1)}) %all-gather.13.cloned.1.call-update) | async-done | bytes 3964944 | tf_op jit(solution)/shard_map/all_gather | solution.py:829
  76.8 29.5 %all-gather.17.cloned.1.call-done = bf16[2048,512]{1,0:T(8,128)(2,1)} async-done(((bf16[128,512]{1,0:T(8,128)(2,1)}), bf16[2048,512]{1,0:T(8,128)(2,1)}) %all-gather.17.cloned.1.call-update) | async-done | bytes 2097168 | tf_op jit(solution)/shard_map/all_gather | solution.py:829
  110.2 40.6 %all-gather.23.cloned.1.call-done = bf16[1664,704]{1,0:T(8,128)(2,1)} async-done(((bf16[104,704]{1,0:T(8,128)(2,1)}), bf16[1664,704]{1,0:T(8,128)(2,1)}) %all-gather.23.cloned.1.call-update) | async-done | bytes 2342928 | tf_op jit(solution)/shard_map/all_gather | solution.py:808
  153.6 41.6 %collective-permute-done.8 = bf16[256,512]{1,0:T(8,128)(2,1)S(1)} collective-permute-done((bf16[256,512]{1,0:T(8,128)(2,1)S(1)}, bf16[256,512]{1,0:T(8,128)(2,1)S(1)}, u32[]{:S(2)}, u32[]{:S(2)}) %collective-permute-start.8) | collective-permute-done | bytes 262176 | tf_op jit(solution)/shard_map/ppermute | solution.py:488
  243.7 16.4 %all-gather.25.cloned.1.call-done = bf16[4224,704]{1,0:T(8,128)(2,1)} async-done(((bf16[264,704]{1,0:T(8,128)(2,1)}), bf16[4224,704]{1,0:T(8,128)(2,1)}) %all-gather.25.cloned.1.call-update) | async-done | bytes 5947408 | tf_op jit(solution)/shard_map/all_gather | solution.py:853
  267.6 54.5 %all-gather.15.cloned.1.call-done = bf16[1408,2112]{1,0:T(8,128)(2,1)} async-done(((bf16[88,2112]{1,0:T(8,128)(2,1)}), bf16[1408,2112]{1,0:T(8,128)(2,1)}) %all-gather.15.cloned.1.call-update) | async-done | bytes 5947408 | tf_op jit(solution)/shard_map/all_gather | solution.py:829
  357.2 19.9 %fusion.248 = (f32[8,1024]{1,0:T(8,128)S(1)}, f32[8,1024,1024]{1,2,0:T(8,128)}) fusion(pred[1024]{0:T(1024)(128)(4,1)S(1)} %iota_compare_fusion, bf16[1024,8,88]{0,2,1:T(8,128)(2,1)} %get-tuple-element.235, bf16[1024,8,88]{0,2,1:T(8,128)(2,1)} %get-tuple-element.234), kind=kOutput, calls=%fused_computation.515 | convolution fusion | flops 1509950464 | bytes 36471808 | tf_op jit(solution)/shard_map/jvp()/sub | solution.py:707
  377.2 13.8 divide_convert_fusion
  518.9 16.1 %convolution_convert_fusion.4 = bf16[1024,3168]{0,1:T(8,128)(2,1)} fusion(bf16[1408,3168]{1,0:T(8,128)(2,1)} %all-gather.21.cloned.1.call-done, bf16[512,1408]{0,1:T(8,128)(2,1)} %collective-permute-done.10, bf16[512,1408]{0,1:T(8,128)(2,1)S(1)} %multiply_convert_fusion.1), kind=kOutput, calls=%fused_computation.51 | convolution fusion | flops 9144205312 | bytes 18292736 | tf_op jit(solution)/shard_map/tc,cd->td/dot_general | solution.py:56
  552.9 68.9 %collective-permute-done.11 = bf16[8,396,704]{2,0,1:T(8,128)(2,1)} collective-permute-done((bf16[8,396,704]{2,0,1:T(8,128)(2,1)}, bf16[8,396,704]{2,0,1:T(8,128)(2,1)}, u32[]{:S(2)}, u32[]{:S(2)}) %collective-permute-start.11) | collective-permute-done | bytes 4460576 | tf_op jit(solution)/shard_map/ppermute | solution.py:488
  644.4 17.3 %fusion.15 = bf16[1024,3168]{0,1:T(8,128)(2,1)} fusion(bf16[1024,3168]{0,1:T(8,128)(2,1)} %convolution_convert_fusion.4, f32[1024,3168]{0,1:T(8,128)} %fusion.93, bf16[3168,704]{1,0:T(8,128)(2,1)S(1)} %bitcast.377, bf16[1024,704]{0,1:T(8,128)(2,1)S(1)} %copy-done.99, bf16[1024,704]{0,1:T(8,128)(2,1)} %get-tuple-element.211, pred[]{:T(512)S(6)} %eq.28), kind=kOutput, calls=%fused_computation.27 | convolution fusion | flops 4639686656 | bytes 33296384 | tf_op jit(solution)/shard_map/td,cd->tc/dot_general | solution.py:60
  661.7 14.6 %fusion.256 = f32[1024,1408]{0,1:T(8,128)S(1)} fusion(bf16[1408,3168]{1,0:T(8,128)(2,1)} %all-gather.21.cloned.1.call-done, bf16[1024,3168]{0,1:T(8,128)(2,1)} %fusion.15), kind=kOutput, calls=%fused_computation.519 | convolution fusion | flops 9135194112 | bytes 21176320 | tf_op jit(solution)/shard_map/td,cd->tc/dot_general | solution.py:60
  730.7 14.3 %collective-permute-done.12 = bf16[512,1408]{0,1:T(8,128)(2,1)} collective-permute-done((bf16[512,1408]{0,1:T(8,128)(2,1)}, bf16[512,1408]{0,1:T(8,128)(2,1)}, u32[]{:S(2)}, u32[]{:S(2)}) %collective-permute-start.12) | collective-permute-done | bytes 1441824 | tf_op jit(solution)/shard_map/ppermute | solution.py:488
  805.0 44.0 %collective-permute-done.16 = bf16[2,792,704]{2,1,0:T(8,128)(2,1)} collective-permute-done((bf16[2,792,704]{2,1,0:T(8,128)(2,1)}, bf16[2,792,704]{2,1,0:T(8,128)(2,1)}, u32[]{:S(2)}, u32[]{:S(2)}) %collective-permute-start.16) | collective-permute-done | bytes 2230304 | tf_op jit(solution)/shard_map/ppermute | solution.py:484
  864.9 23.6 %collective-permute-done.49 = bf16[384,1408]{0,1:T(8,128)(2,1)S(1)} collective-permute-done((bf16[384,1408]{0,1:T(8,128)(2,1)S(1)}, bf16[384,1408]{0,1:T(8,128)(2,1)S(1)}, u32[]{:S(2)}, u32[]{:S(2)}) %collective-permute-start.49) | collective-permute-done | bytes 1081376 | tf_op jit(solution)/shard_map/ppermute | solution.py:488
  953.7 17.7 %fusion.7 = (f32[8,1024]{1,0:T(8,128)S(1)}, bf16[8,1024,1024]{1,2,0:T(8,128)(2,1)}) fusion(f32[8,1024,1024]{1,2,0:T(8,128)} %get-tuple-element.264, f32[8,1024]{1,0:T(8,128)S(1)} %multiply_divide_fusion, bf16[8,88,1024]{2,1,0:T(8,128)(2,1)S(1)} %bitcast.360, bf16[1024,8,88]{0,2,1:T(8,128)(2,1)S(1)} %bitcast.359), kind=kOutput, calls=%fused_computation.9 | convolution fusion | flops 1518329856 | bytes 53280768 | tf_op jit(solution)/shard_map/transpose(jvp(hqk,khd->qhd))/dot_general | solution.py:708
  971.5 24.1 %fusion.5 = bf16[8,1024,1024]{1,2,0:T(8,128)(2,1)} fusion(f32[8,1024,1024]{1,2,0:T(8,128)} %get-tuple-element.264, bf16[8,1024,1024]{1,2,0:T(8,128)(2,1)} %get-tuple-element.275, f32[8,1024]{1,0:T(8,128)S(1)} %neg.49, f32[8,1024]{1,0:T(8,128)S(1)} %copy-done.132, pred[1024]{0:T(1024)(128)(4,1)S(1)} %copy-done.179), kind=kLoop, calls=%fused_computation.7 | loop fusion | flops 58720256 | bytes 67175424 | tf_op jit(solution)/shard_map/transpose(jvp())/mul | solution.py:705
  1066.2 18.7 %collective-permute-done.20 = bf16[792,704]{1,0:T(8,128)(2,1)} collective-permute-done((bf16[792,704]{1,0:T(8,128)(2,1)}, bf16[792,704]{1,0:T(8,128)(2,1)}, u32[]{:S(2)}, u32[]{:S(2)}) %collective-permute-start.20) | collective-permute-done | bytes 1115168 | tf_op jit(solution)/shard_map/ppermute | solution.py:595
  1115.1 15.8 %collective-permute-done.23 = bf16[176,3168]{1,0:T(8,128)(2,1)S(1)} collective-permute-done((bf16[176,3168]{1,0:T(8,128)(2,1)}, bf16[176,3168]{1,0:T(8,128)(2,1)S(1)}, u32[]{:S(2)}, u32[]{:S(2)}) %collective-permute-start.23) | collective-permute-done | bytes 1115168 | tf_op jit(solution)/shard_map/ppermute | solution.py:484
  1143.5 14.8 %collective-permute-start.25 = (bf16[704,2112]{1,0:T(8,128)(2,1)}, bf16[704,2112]{1,0:T(8,128)(2,1)}, u32[]{:S(2)}, u32[]{:S(2)}) collective-permute-start(bf16[704,2112]{1,0:T(8,128)(2,1)} %convolution_convert_fusion.8), channel_id=1, source_target_pairs={{0,2},{2,0},{4,6},{6,4},{8,10},{10,8},{12,14},{14,12},{16,18},{18,... | collective-permute-start | bytes 8921096 | tf_op jit(solution)/shard_map/ppermute | solution.py:484
  1186.1 16.2 %collective-permute-done.55 = f32[5984]{0:T(1024)S(1)} collective-permute-done((f32[5984]{0:T(1024)S(1)}, f32[5984]{0:T(1024)S(1)}, u32[]{:S(2)}, u32[]{:S(2)}) %collective-permute-start.55) | collective-permute-done | bytes 23968 | tf_op jit(solution)/shard_map/ppermute | solution.py:484
  1222.9 15.1 %collective-permute-done.27 = bf16[2,176,2112]{2,1,0:T(8,128)(2,1)S(1)} collective-permute-done((bf16[2,176,2112]{2,1,0:T(8,128)(2,1)S(1)}, bf16[2,176,2112]{2,1,0:T(8,128)(2,1)S(1)}, u32[]{:S(2)}, u32[]{:S(2)}) %collective-permute-start.27) | collective-permute-done | bytes 1486880 | tf_op jit(solution)/shard_map/ppermute | solution.py:484
  1273.3 16.3 %collective-permute-done.32 = bf16[1408,704]{0,1:T(8,128)(2,1)} collective-permute-done((bf16[1408,704]{0,1:T(8,128)(2,1)}, bf16[1408,704]{0,1:T(8,128)(2,1)}, u32[]{:S(2)}, u32[]{:S(2)}) %collective-permute-start.32) | collective-permute-done | bytes 1982496 | tf_op jit(solution)/shard_map/ppermute | solution.py:488
  1376.8 14.7 %collective-permute-done.38 = bf16[352,704]{1,0:T(8,128)(2,1)S(1)} collective-permute-done((bf16[352,704]{1,0:T(8,128)(2,1)S(1)}, bf16[352,704]{1,0:T(8,128)(2,1)S(1)}, u32[]{:S(2)}, u32[]{:S(2)}) %collective-permute-start.38) | collective-permute-done | bytes 495648 | tf_op jit(solution)/shard_map/ppermute | solution.py:595
  (821 shorter events, 781.9 us)
Async XLA Ops:
  7.9 98.3 %all-gather.17.cloned.1.call-start = ((), (), s32[]{:S(2)}) async-start(), calls=%async_computation.7 | async-start | bytes 2228224 | tf_op jit(solution)/shard_map/all_gather | solution.py:829
  8.7 142.2 %all-gather.23.cloned.1.call-start = ((), (), s32[]{:S(2)}) async-start(), calls=%async_computation.11 | async-start | bytes 2715648 | tf_op jit(solution)/shard_map/all_gather | solution.py:808
  10.4 193.1 %all-gather.19.cloned.1.call-start = ((), (), s32[]{:S(2)}) async-start(), calls=%async_computation.8 | async-start | bytes 3063808 | tf_op jit(solution)/shard_map/all_gather | solution.py:829
  10.9 249.2 %all-gather.25.cloned.1.call-start = ((), (), s32[]{:S(2)}) async-start(), calls=%async_computation.12 | async-start | bytes 6893568 | tf_op jit(solution)/shard_map/all_gather | solution.py:853
  12.8 309.2 %all-gather.15.cloned.1.call-start = ((), (), s32[]{:S(2)}) async-start(), calls=%async_computation.6 | async-start | bytes 6510592 | tf_op jit(solution)/shard_map/all_gather | solution.py:829
  22.5 467.1 %all-gather.27.cloned.1.call-start = ((), (), s32[]{:S(2)}) async-start(), calls=%async_computation.13 | async-start | bytes 10444800 | tf_op jit(solution)/shard_map/all_gather | solution.py:859
  23.2 484.4 %all-gather.21.cloned.1.call-start = ((), (), s32[]{:S(2)}) async-start(), calls=%async_computation.9 | async-start | bytes 9574400 | tf_op jit(solution)/shard_map/all_gather | solution.py:829
  70.6 142.7 %collective-permute-start = (bf16[2816,704]{0,1:T(8,128)(2,1)}, bf16[2816,704]{0,1:T(8,128)(2,1)}, u32[]{:S(2)}, u32[]{:S(2)}) collective-permute-start(bf16[2816,704]{0,1:T(8,128)(2,1)} %copy.132), channel_id=1, source_target_pairs={{0,1},{1,0},{2,3},{3,2},{4,5},{5,4},{6,7},{7,6},{8,9},{9,8},{10,11... | collective-permute-start | bytes 11894792 | tf_op jit(solution)/shard_map/ppermute | solution.py:488
  73.5 412.3 %collective-permute-start.13 = (bf16[512,1408]{0,1:T(8,128)(2,1)}, bf16[512,1408]{0,1:T(8,128)(2,1)}, u32[]{:S(2)}, u32[]{:S(2)}) collective-permute-start(bf16[512,1408]{0,1:T(8,128)(2,1)} %bitcast_convert_fusion), channel_id=1, source_target_pairs={{0,1},{1,0},{2,3},{3,2},{4,5},{5,4},{6,7},{7,6},{8,9},{9,8},{10,11... | collective-permute-start | bytes 4325384 | tf_op jit(solution)/shard_map/ppermute | solution.py:488
  74.1 972.1 %reduce-scatter.20.cloned.1.call-start = ((), (), s32[]{:S(2)}) async-start(), calls=%async_computation.16 | async-start | bytes 4212736
  108.6 86.6 %collective-permute-start.8 = (bf16[256,512]{1,0:T(8,128)(2,1)S(1)}, bf16[256,512]{1,0:T(8,128)(2,1)S(1)}, u32[]{:S(2)}, u32[]{:S(2)}) collective-permute-start(bf16[256,512]{1,0:T(8,128)(2,1)S(1)} %convolution_convert_fusion.23), channel_id=1, source_target_pairs={{0,1},{1,0},{2,3},{3,2},{4,5},{5,4},{6,7},{7,6},{8,9},{9,8},{10,11... | collective-permute-start | bytes 786440 | tf_op jit(solution)/shard_map/ppermute | solution.py:488
  223.9 98.2 %collective-permute-start.3 = (bf16[512,1408]{0,1:T(8,128)(2,1)}, bf16[512,1408]{0,1:T(8,128)(2,1)}, u32[]{:S(2)}, u32[]{:S(2)}) collective-permute-start(bf16[512,1408]{0,1:T(8,128)(2,1)} %add_convert_fusion.8), channel_id=1, source_target_pairs={{0,1},{1,0},{2,3},{3,2},{4,5},{5,4},{6,7},{7,6},{8,9},{9,8},{10,11... | collective-permute-start | bytes 4325384 | tf_op jit(solution)/shard_map/ppermute | solution.py:488
  266.1 161.3 %collective-permute-start.7 = (bf16[16,3,88,704]{3,2,0,1:T(8,128)(2,1)}, bf16[16,3,88,704]{3,2,0,1:T(8,128)(2,1)}, u32[]{:S(2)}, u32[]{:S(2)}) collective-permute-start(bf16[16,3,88,704]{3,2,0,1:T(8,128)(2,1)} %copy.134), channel_id=1, source_target_pairs={{0,1},{1,0},{2,3},{3,2},{4,5},{5,4},{6,7},{7,6},{8,9},{9,8},{10,11... | collective-permute-start | bytes 17842184 | tf_op jit(solution)/shard_map/ppermute | solution.py:488
  500.3 121.5 %collective-permute-start.11 = (bf16[8,396,704]{2,0,1:T(8,128)(2,1)}, bf16[8,396,704]{2,0,1:T(8,128)(2,1)}, u32[]{:S(2)}, u32[]{:S(2)}) collective-permute-start(bf16[8,396,704]{2,0,1:T(8,128)(2,1)} %copy.143), channel_id=1, source_target_pairs={{0,1},{1,0},{2,3},{3,2},{4,5},{5,4},{6,7},{7,6},{8,9},{9,8},{10,11... | collective-permute-start | bytes 13381640 | tf_op jit(solution)/shard_map/ppermute | solution.py:488
  782.7 271.2 %reduce-scatter.22.cloned.1.call-start = ((), (), s32[]{:S(2)}) async-start(), calls=%async_computation.17 | async-start | bytes 4212736
  782.8 69.8 %collective-permute-start.17 = (bf16[704,3168]{1,0:T(8,128)(2,1)}, bf16[704,3168]{1,0:T(8,128)(2,1)}, u32[]{:S(2)}, u32[]{:S(2)}) collective-permute-start(bf16[704,3168]{1,0:T(8,128)(2,1)} %convolution_convert_fusion.5), channel_id=1, source_target_pairs={{0,2},{2,0},{4,6},{6,4},{8,10},{10,8},{12,14},{14,12},{16,18},{18,... | collective-permute-start | bytes 13381640 | tf_op jit(solution)/shard_map/ppermute | solution.py:484
  782.9 66.1 %collective-permute-start.16 = (bf16[2,792,704]{2,1,0:T(8,128)(2,1)}, bf16[2,792,704]{2,1,0:T(8,128)(2,1)}, u32[]{:S(2)}, u32[]{:S(2)}) collective-permute-start(bf16[2,792,704]{2,1,0:T(8,128)(2,1)} %dynamic-slice_bitcast_fusion), channel_id=1, source_target_pairs={{0,4},{2,6},{4,0},{6,2},{8,12},{10,14},{12,8},{14,10},{16,20},{18,... | collective-permute-start | bytes 6690824 | tf_op jit(solution)/shard_map/ppermute | solution.py:484
  794.3 465.1 %reduce-scatter.16.cloned.1.call-start = ((), (), s32[]{:S(2)}) async-start(), calls=%async_computation.14 | async-start | bytes 2228224
  907.7 353.5 %reduce-scatter.14.cloned.1.call-start = ((), (), s32[]{:S(2)}) async-start(), calls=%async_computation.10 | async-start | bytes 3063808 | tf_op jit(solution)/shard_map/reduce_scatter | solution.py:835
  914.8 348.1 %reduce-scatter.18.cloned.1.call-start = ((), (), s32[]{:S(2)}) async-start(), calls=%async_computation.15 | async-start | bytes 4212736
  934.8 126.2 %collective-permute-start.21 = (bf16[2,176,3168]{2,1,0:T(8,128)(2,1)}, bf16[2,176,3168]{2,1,0:T(8,128)(2,1)}, u32[]{:S(2)}, u32[]{:S(2)}) collective-permute-start(bf16[2,176,3168]{2,1,0:T(8,128)(2,1)} %dynamic-slice_bitcast_fusion.1), channel_id=1, source_target_pairs={{0,4},{2,6},{4,0},{6,2},{8,12},{10,14},{12,8},{14,10},{16,20},{18,... | collective-permute-start | bytes 6690824 | tf_op jit(solution)/shard_map/ppermute | solution.py:484
  1027.0 57.9 %collective-permute-start.20 = (bf16[792,704]{1,0:T(8,128)(2,1)}, bf16[792,704]{1,0:T(8,128)(2,1)}, u32[]{:S(2)}, u32[]{:S(2)}) collective-permute-start(bf16[792,704]{1,0:T(8,128)(2,1)} %fusion.66), channel_id=1, source_target_pairs={{16,0},{18,2},{20,4},{22,6},{24,8},{26,10},{28,12},{30,14},{1,17},... | collective-permute-start | bytes 3345416 | tf_op jit(solution)/shard_map/ppermute | solution.py:595
  1142.1 66.1 %collective-permute-start.24 = (bf16[176,3168]{1,0:T(8,128)(2,1)}, bf16[176,3168]{1,0:T(8,128)(2,1)}, u32[]{:S(2)}, u32[]{:S(2)}) collective-permute-start(bf16[176,3168]{1,0:T(8,128)(2,1)} %fusion.72), channel_id=1, source_target_pairs={{16,0},{17,1},{20,4},{21,5},{24,8},{25,9},{28,12},{29,13},{2,18},{... | collective-permute-start | bytes 3345416 | tf_op jit(solution)/shard_map/ppermute | solution.py:595
  1143.5 66.4 %collective-permute-start.25 = (bf16[704,2112]{1,0:T(8,128)(2,1)}, bf16[704,2112]{1,0:T(8,128)(2,1)}, u32[]{:S(2)}, u32[]{:S(2)}) collective-permute-start(bf16[704,2112]{1,0:T(8,128)(2,1)} %convolution_convert_fusion.8), channel_id=1, source_target_pairs={{0,2},{2,0},{4,6},{6,4},{8,10},{10,8},{12,14},{14,12},{16,18},{18,... | collective-permute-start | bytes 8921096 | tf_op jit(solution)/shard_map/ppermute | solution.py:484
  (242 other events, 6689.3 us)
Sparse Core Ops, SparseCore 0:
  10.3 53.9 all-gather.12
  66.5 39.7 all-gather.16
  109.0 41.7 all-gather.22
  153.0 43.1 all-gather.18
  198.7 61.3 all-gather.24
  262.7 59.3 all-gather.14
  324.3 82.4 all-gather.26
  409.0 76.9 all-gather.20
  782.8 94.1 reduce-scatter.19
  880.7 94.6 reduce-scatter.21
  979.2 82.7 reduce-scatter.15
  1066.1 72.7 reduce-scatter.13
  1142.8 89.8 reduce-scatter.17

commit v4 on v3

--- a/solution.py
+++ b/solution.py
@@ -856,16 +856,9 @@
         tuple(side[:, k].reshape(-1, narrow_width) for side in out_sides) for k in range(3)
     )
     w_up = gather(mlp_up)
-    down_rows = lax.all_gather(mlp_down, DP)
+    down_rows = lax.all_gather(pair(y, mlp_down, swap_seq(mlp_down), 1), DP)
     middle = down_rows.shape[0] // 2
-    upper_rows, lower_rows = down_rows[:middle], down_rows[middle:]
-    w_down = tuple(
-        side.reshape(-1, narrow_width)
-        for side in (
-            pick(y, upper_rows, lower_rows),
-            swap_seq(pick(y, lower_rows, upper_rows)),
-        )
-    )
+    w_down = pick(y, down_rows[:middle], down_rows[middle:]).reshape(-1, width)
     cot_far = swap_seq(cot_low)
 
     feats = time_features(time_ids).astype(bf16)
@@ -919,12 +912,12 @@
     normed3_both = jnp.concatenate([normed3, swap_seq(normed3)], 0)
     upper = narrow(project(normed3_both, w_up))
     active = narrow(gelu(upper.astype(jnp.float32)))
-    mixed = times(active, w_down)
+    mixed = project(active, w_down)
     final = resid2 + mixed[:local] + wide(swap_seq(narrow(mixed[local:])))
     block_out = narrow(final)[None]
 
     cot_both = jnp.concatenate([cot_low, cot_far], 0)
-    d_active = times_back(cot_both, w_down)
+    d_active = project_back(cot_both, w_down)
     _, gelu_back = jax.vjp(gelu, upper.astype(jnp.float32))
     d_upper = narrow(gelu_back(d_active)[0])
     flow.add(8, reduce_down(spot, active, halves_of(cot_both)))

time: 1420 us -> 1360 us (0.958)
  waiting for transfers between devices: 570 us -> 529 us
  local copies, waits for them, and re-layouts: 172 us -> 151 us
    ppermute x27, waiting for transfers between devices: 222 us -> 147 us  [swap_seq(): return lax.ppermute(value, SEQ, FLIP)]
    all_gather x5, waiting for transfers between devices: 121 us -> 149 us  [gather(): return lax.all_gather(shard, DP, axis=0, tiled=True)]
    unnamed x401 -> x369, local copies, waits for them, and re-layouts: 52.3 us -> 45.4 us
    dot_general x13 -> x12, matrix products: 80.6 us -> 76.1 us  [project_back(): jnp.einsum('td,cd->tc', grad_low, right, preferred_element_type=jnp.float32)]
    dot_general x16 -> x15, matrix products: 72.9 us -> 68.6 us  [project(): jnp.einsum('tc,cd->td', left, right, preferred_element_type=jnp.float32)]
where the time goes in v4:
time: 1360 us; the launch traced here: 1350 us
  waiting for transfers between devices  529 us (39%)
  matrix products  343 us (25%)
  other arithmetic  201 us (15%)
  local copies, waits for them, and re-layouts  151 us (11%)
  starting transfers between devices  103 us (8%)
  between operations  19.3 us (1%)
    all_gather x5, waiting for transfers between devices, gather(): return lax.all_gather(shard, DP, axis=0, tiled=True)  149 us
    ppermute x27, waiting for transfers between devices, swap_seq(): return lax.ppermute(value, SEQ, FLIP)  147 us
    ppermute x24, waiting for transfers between devices, swap(): return lax.ppermute(value, DP, [(i, i ^ bit) for i in range(16)])  128 us
    dot_general x15, matrix products, dot_rows(): jnp.einsum('tc,td->cd', left, right, preferred_element_type=jnp.float32)  87.8 us
    dot_general x12, matrix products, project_back(): jnp.einsum('td,cd->tc', grad_low, right, preferred_element_type=jnp.float32)  76.1 us
    dot_general x15, matrix products, project(): jnp.einsum('tc,cd->td', left, right, preferred_element_type=jnp.float32)  68.6 us
    ppermute x24, starting transfers between devices, swap(): return lax.ppermute(value, DP, [(i, i ^ bit) for i in range(16)])  51.6 us
    dot_general x6, matrix products, attend(): o = jnp.einsum('hqk,khd->qhd', p, v, preferred_element_type=jnp.float32)  49.6 us
  transfers between devices with their start and end apart: 70, of which 35 were waited for; matrix products, arithmetic and copies ran while one was open for 44% of the time, Pallas kernels for 0%

profile of v4, /device:TPU:0, one launch (start us, length us, event | category | flops | bytes accessed | tf_op | source)
XLA Modules:
  0.0 1347.3 jit_solution(5968193766986694443)
XLA Ops:
  26.1 38.2 %all-gather.11.cloned.1.call-done = bf16[2816,704]{1,0:T(8,128)(2,1)} async-done(((bf16[176,704]{1,0:T(8,128)(2,1)}), bf16[2816,704]{1,0:T(8,128)(2,1)}) %all-gather.11.cloned.1.call-update) | async-done | bytes 3964944 | tf_op jit(solution)/shard_map/all_gather | solution.py:829
  74.3 31.9 %all-gather.15.cloned.1.call-done = bf16[2048,512]{1,0:T(8,128)(2,1)} async-done(((bf16[128,512]{1,0:T(8,128)(2,1)}), bf16[2048,512]{1,0:T(8,128)(2,1)}) %all-gather.15.cloned.1.call-update) | async-done | bytes 2097168 | tf_op jit(solution)/shard_map/all_gather | solution.py:829
  111.9 38.9 %all-gather.23.cloned.1.call-done = bf16[1664,704]{1,0:T(8,128)(2,1)} async-done(((bf16[104,704]{1,0:T(8,128)(2,1)}), bf16[1664,704]{1,0:T(8,128)(2,1)}) %all-gather.23.cloned.1.call-update) | async-done | bytes 2342928 | tf_op jit(solution)/shard_map/all_gather | solution.py:808
  171.3 24.8 %all-gather.17.cloned.1.call-done = bf16[1024,1408]{1,0:T(8,128)(2,1)} async-done(((bf16[64,1408]{1,0:T(8,128)(2,1)}), bf16[1024,1408]{1,0:T(8,128)(2,1)}) %all-gather.17.cloned.1.call-update) | async-done | bytes 2883600 | tf_op jit(solution)/shard_map/all_gather | solution.py:829
  236.0 24.1 %all-gather.25.cloned.1.call-done = bf16[4224,704]{1,0:T(8,128)(2,1)} async-done(((bf16[264,704]{1,0:T(8,128)(2,1)}), bf16[4224,704]{1,0:T(8,128)(2,1)}) %all-gather.25.cloned.1.call-update) | async-done | bytes 5947408 | tf_op jit(solution)/shard_map/all_gather | solution.py:853
  267.5 54.5 %all-gather.13.cloned.1.call-done = bf16[1408,2112]{1,0:T(8,128)(2,1)} async-done(((bf16[88,2112]{1,0:T(8,128)(2,1)}), bf16[1408,2112]{1,0:T(8,128)(2,1)}) %all-gather.13.cloned.1.call-update) | async-done | bytes 5947408 | tf_op jit(solution)/shard_map/all_gather | solution.py:829
  351.9 19.9 %fusion.248 = (f32[8,1024]{1,0:T(8,128)S(1)}, f32[8,1024,1024]{1,2,0:T(8,128)}) fusion(pred[1024]{0:T(1024)(128)(4,1)S(1)} %iota_compare_fusion, bf16[1024,8,88]{0,2,1:T(8,128)(2,1)} %get-tuple-element.231, bf16[1024,8,88]{0,2,1:T(8,128)(2,1)} %get-tuple-element.230), kind=kOutput, calls=%fused_computation.513 | convolution fusion | flops 1509950464 | bytes 36471808 | tf_op jit(solution)/shard_map/jvp()/sub | solution.py:707
  405.1 18.6 %collective-permute-done.6 = bf16[512,704]{0,1:T(8,128)(2,1)} collective-permute-done((bf16[512,704]{0,1:T(8,128)(2,1)}, bf16[512,704]{0,1:T(8,128)(2,1)}, u32[]{:S(2)}, u32[]{:S(2)}) %collective-permute-start.6) | collective-permute-done | bytes 720928 | tf_op jit(solution)/shard_map/ppermute | solution.py:488
  491.9 28.4 %collective-permute-done.10 = bf16[512,1408]{0,1:T(8,128)(2,1)} collective-permute-done((bf16[512,1408]{0,1:T(8,128)(2,1)}, bf16[512,1408]{0,1:T(8,128)(2,1)}, u32[]{:S(2)}, u32[]{:S(2)}) %collective-permute-start.10) | collective-permute-done | bytes 1441824 | tf_op jit(solution)/shard_map/ppermute | solution.py:488
  520.3 16.4 %convolution_convert_fusion.4 = bf16[1024,3168]{0,1:T(8,128)(2,1)} fusion(bf16[1408,3168]{1,0:T(8,128)(2,1)} %all-gather.19.cloned.1.call-done, bf16[512,1408]{0,1:T(8,128)(2,1)} %collective-permute-done.10, bf16[512,1408]{0,1:T(8,128)(2,1)} %multiply_convert_fusion.1), kind=kOutput, calls=%fused_computation.52 | convolution fusion | flops 9144205312 | bytes 18292736 | tf_op jit(solution)/shard_map/tc,cd->td/dot_general | solution.py:56
  579.3 23.9 %fusion.15 = bf16[1024,3168]{0,1:T(8,128)(2,1)} fusion(bf16[1024,3168]{0,1:T(8,128)(2,1)} %convolution_convert_fusion.4, bf16[3168,1408]{1,0:T(8,128)(2,1)} %reshape.766, bf16[512,1408]{0,1:T(8,128)(2,1)} %collective-permute-done.13, bf16[512,1408]{0,1:T(8,128)(2,1)} %bitcast_convert_fusion), kind=kOutput, calls=%fused_computation.27 | convolution fusion | flops 9209085952 | bytes 24780800 | tf_op jit(solution)/shard_map/td,cd->tc/dot_general | solution.py:60
  603.3 14.4 %fusion.256 = f32[1024,1408]{0,1:T(8,128)S(1)} fusion(bf16[1408,3168]{1,0:T(8,128)(2,1)} %all-gather.19.cloned.1.call-done, bf16[1024,3168]{0,1:T(8,128)(2,1)} %fusion.15), kind=kOutput, calls=%fused_computation.517 | convolution fusion | flops 9135194112 | bytes 21176320 | tf_op jit(solution)/shard_map/td,cd->tc/dot_general | solution.py:60
  622.6 14.0 %fusion.226 = f32[1024,1408]{0,1:T(8,128)} fusion(bf16[3168,1408]{1,0:T(8,128)(2,1)S(1)} %bitcast.368, bf16[1024,3168]{0,1:T(8,128)(2,1)} %convolution_convert_fusion.4), kind=kOutput, calls=%fused_computation.497 | convolution fusion | flops 9167634432 | bytes 21176320 | tf_op jit(solution)/shard_map/tc,cd->td/dot_general | solution.py:56
  746.5 44.0 %collective-permute-done.16 = bf16[2,792,704]{2,1,0:T(8,128)(2,1)} collective-permute-done((bf16[2,792,704]{2,1,0:T(8,128)(2,1)}, bf16[2,792,704]{2,1,0:T(8,128)(2,1)}, u32[]{:S(2)}, u32[]{:S(2)}) %collective-permute-start.16) | collective-permute-done | bytes 2230304 | tf_op jit(solution)/shard_map/ppermute | solution.py:484
  806.5 23.8 %collective-permute-done.49 = bf16[384,1408]{0,1:T(8,128)(2,1)S(1)} collective-permute-done((bf16[384,1408]{0,1:T(8,128)(2,1)S(1)}, bf16[384,1408]{0,1:T(8,128)(2,1)S(1)}, u32[]{:S(2)}, u32[]{:S(2)}) %collective-permute-start.49) | collective-permute-done | bytes 1081376 | tf_op jit(solution)/shard_map/ppermute | solution.py:488
  895.5 17.8 %fusion.7 = (f32[8,1024]{1,0:T(8,128)S(1)}, bf16[8,1024,1024]{1,2,0:T(8,128)(2,1)}) fusion(f32[8,1024,1024]{1,2,0:T(8,128)} %get-tuple-element.260, f32[8,1024]{1,0:T(8,128)S(1)} %multiply_divide_fusion, bf16[8,88,1024]{2,1,0:T(8,128)(2,1)S(1)} %bitcast.359, bf16[1024,8,88]{0,2,1:T(8,128)(2,1)S(1)} %bitcast.358), kind=kOutput, calls=%fused_computation.9 | convolution fusion | flops 1518329856 | bytes 53280768 | tf_op jit(solution)/shard_map/transpose(jvp(hqk,khd->qhd))/dot_general | solution.py:708
  913.3 24.1 %fusion.5 = bf16[8,1024,1024]{1,2,0:T(8,128)(2,1)} fusion(f32[8,1024,1024]{1,2,0:T(8,128)} %get-tuple-element.260, bf16[8,1024,1024]{1,2,0:T(8,128)(2,1)} %get-tuple-element.271, f32[8,1024]{1,0:T(8,128)S(1)} %neg.49, f32[8,1024]{1,0:T(8,128)S(1)} %copy-done.118, pred[1024]{0:T(1024)(128)(4,1)S(1)} %copy-done.165), kind=kLoop, calls=%fused_computation.7 | loop fusion | flops 58720256 | bytes 67175424 | tf_op jit(solution)/shard_map/transpose(jvp())/mul | solution.py:705
  1008.2 18.7 %collective-permute-done.20 = bf16[792,704]{1,0:T(8,128)(2,1)} collective-permute-done((bf16[792,704]{1,0:T(8,128)(2,1)}, bf16[792,704]{1,0:T(8,128)(2,1)}, u32[]{:S(2)}, u32[]{:S(2)}) %collective-permute-start.20) | collective-permute-done | bytes 1115168 | tf_op jit(solution)/shard_map/ppermute | solution.py:595
  1056.8 15.4 %collective-permute-done.23 = bf16[176,3168]{1,0:T(8,128)(2,1)S(1)} collective-permute-done((bf16[176,3168]{1,0:T(8,128)(2,1)}, bf16[176,3168]{1,0:T(8,128)(2,1)S(1)}, u32[]{:S(2)}, u32[]{:S(2)}) %collective-permute-start.23) | collective-permute-done | bytes 1115168 | tf_op jit(solution)/shard_map/ppermute | solution.py:484
  1084.6 14.8 %collective-permute-start.25 = (bf16[704,2112]{1,0:T(8,128)(2,1)}, bf16[704,2112]{1,0:T(8,128)(2,1)}, u32[]{:S(2)}, u32[]{:S(2)}) collective-permute-start(bf16[704,2112]{1,0:T(8,128)(2,1)} %convolution_convert_fusion.8), channel_id=1, source_target_pairs={{0,2},{2,0},{4,6},{6,4},{8,10},{10,8},{12,14},{14,12},{16,18},{18,... | collective-permute-start | bytes 8921096 | tf_op jit(solution)/shard_map/ppermute | solution.py:484
  1127.5 21.0 %collective-permute-done.55 = f32[5984]{0:T(1024)S(1)} collective-permute-done((f32[5984]{0:T(1024)S(1)}, f32[5984]{0:T(1024)S(1)}, u32[]{:S(2)}, u32[]{:S(2)}) %collective-permute-start.55) | collective-permute-done | bytes 23968 | tf_op jit(solution)/shard_map/ppermute | solution.py:484
  1164.4 15.0 %collective-permute-done.27 = bf16[2,176,2112]{2,1,0:T(8,128)(2,1)S(1)} collective-permute-done((bf16[2,176,2112]{2,1,0:T(8,128)(2,1)S(1)}, bf16[2,176,2112]{2,1,0:T(8,128)(2,1)S(1)}, u32[]{:S(2)}, u32[]{:S(2)}) %collective-permute-start.27) | collective-permute-done | bytes 1486880 | tf_op jit(solution)/shard_map/ppermute | solution.py:484
  1284.7 15.1 %collective-permute-start.36 = (bf16[352,704]{1,0:T(8,128)(2,1)S(1)}, bf16[352,704]{1,0:T(8,128)(2,1)S(1)}, u32[]{:S(2)}, u32[]{:S(2)}) collective-permute-start(bf16[352,704]{1,0:T(8,128)(2,1)S(1)} %dynamic-slice_bitcast_fusion.6), channel_id=1, source_target_pairs={{0,8},{2,10},{4,12},{6,14},{8,0},{10,2},{12,4},{14,6},{16,24},{18,... | collective-permute-start | bytes 1486856 | tf_op jit(solution)/shard_map/ppermute | solution.py:484
  1316.6 14.6 %collective-permute-done.38 = bf16[352,704]{1,0:T(8,128)(2,1)S(1)} collective-permute-done((bf16[352,704]{1,0:T(8,128)(2,1)S(1)}, bf16[352,704]{1,0:T(8,128)(2,1)S(1)}, u32[]{:S(2)}, u32[]{:S(2)}) %collective-permute-start.38) | collective-permute-done | bytes 495648 | tf_op jit(solution)/shard_map/ppermute | solution.py:595
  (782 shorter events, 755.6 us)
Async XLA Ops:
  7.2 57.1 %all-gather.11.cloned.1.call-start = ((), (), s32[]{:S(2)}) async-start(), calls=%async_computation.5 | async-start | bytes 4595712 | tf_op jit(solution)/shard_map/all_gather | solution.py:829
  8.0 98.3 %all-gather.15.cloned.1.call-start = ((), (), s32[]{:S(2)}) async-start(), calls=%async_computation.7 | async-start | bytes 2228224 | tf_op jit(solution)/shard_map/all_gather | solution.py:829
  8.7 142.1 %all-gather.23.cloned.1.call-start = ((), (), s32[]{:S(2)}) async-start(), calls=%async_computation.12 | async-start | bytes 2715648 | tf_op jit(solution)/shard_map/all_gather | solution.py:808
  10.4 185.8 %all-gather.17.cloned.1.call-start = ((), (), s32[]{:S(2)}) async-start(), calls=%async_computation.8 | async-start | bytes 3063808 | tf_op jit(solution)/shard_map/all_gather | solution.py:829
  10.9 249.2 %all-gather.25.cloned.1.call-start = ((), (), s32[]{:S(2)}) async-start(), calls=%async_computation.13 | async-start | bytes 6893568 | tf_op jit(solution)/shard_map/all_gather | solution.py:853
  12.8 309.2 %all-gather.13.cloned.1.call-start = ((), (), s32[]{:S(2)}) async-start(), calls=%async_computation.6 | async-start | bytes 6510592 | tf_op jit(solution)/shard_map/all_gather | solution.py:829
  22.5 469.4 %all-gather.19.cloned.1.call-start = ((), (), s32[]{:S(2)}) async-start(), calls=%async_computation.9 | async-start | bytes 9574400 | tf_op jit(solution)/shard_map/all_gather | solution.py:829
  23.2 537.3 %all-gather.21.cloned.1.call-start = ((), (), s32[]{:S(2)}) async-start(), calls=%async_computation.10 | async-start | bytes 19148800 | tf_op jit(solution)/shard_map/all_gather | solution.py:859
  25.1 85.0 %collective-permute-start.11 = (bf16[396,704]{1,0:T(8,128)(2,1)S(1)}, bf16[396,704]{1,0:T(8,128)(2,1)S(1)}, u32[]{:S(2)}, u32[]{:S(2)}) collective-permute-start(bf16[396,704]{1,0:T(8,128)(2,1)S(1)} %copy-done.100), channel_id=1, source_target_pairs={{0,1},{1,0},{2,3},{3,2},{4,5},{5,4},{6,7},{7,6},{8,9},{9,8},{10,11... | collective-permute-start | bytes 1672712 | tf_op jit(solution)/shard_map/ppermute | solution.py:488
  70.6 135.2 %collective-permute-start = (bf16[2816,704]{0,1:T(8,128)(2,1)}, bf16[2816,704]{0,1:T(8,128)(2,1)}, u32[]{:S(2)}, u32[]{:S(2)}) collective-permute-start(bf16[2816,704]{0,1:T(8,128)(2,1)} %copy.136), channel_id=1, source_target_pairs={{0,1},{1,0},{2,3},{3,2},{4,5},{5,4},{6,7},{7,6},{8,9},{9,8},{10,11... | collective-permute-start | bytes 11894792 | tf_op jit(solution)/shard_map/ppermute | solution.py:488
  111.9 876.0 %reduce-scatter.20.cloned.1.call-start = ((), (), s32[]{:S(2)}) async-start(), calls=%async_computation.16 | async-start | bytes 4212736
  216.3 105.7 %collective-permute-start.3 = (bf16[512,1408]{0,1:T(8,128)(2,1)}, bf16[512,1408]{0,1:T(8,128)(2,1)}, u32[]{:S(2)}, u32[]{:S(2)}) collective-permute-start(bf16[512,1408]{0,1:T(8,128)(2,1)} %add_convert_fusion.8), channel_id=1, source_target_pairs={{0,1},{1,0},{2,3},{3,2},{4,5},{5,4},{6,7},{7,6},{8,9},{9,8},{10,11... | collective-permute-start | bytes 4325384 | tf_op jit(solution)/shard_map/ppermute | solution.py:488
  266.1 161.3 %collective-permute-start.7 = (bf16[16,3,88,704]{3,2,0,1:T(8,128)(2,1)}, bf16[16,3,88,704]{3,2,0,1:T(8,128)(2,1)}, u32[]{:S(2)}, u32[]{:S(2)}) collective-permute-start(bf16[16,3,88,704]{3,2,0,1:T(8,128)(2,1)} %copy.138), channel_id=1, source_target_pairs={{0,1},{1,0},{2,3},{3,2},{4,5},{5,4},{6,7},{7,6},{8,9},{9,8},{10,11... | collective-permute-start | bytes 17842184 | tf_op jit(solution)/shard_map/ppermute | solution.py:488
  490.7 58.9 %collective-permute-start.13 = (bf16[512,1408]{0,1:T(8,128)(2,1)}, bf16[512,1408]{0,1:T(8,128)(2,1)}, u32[]{:S(2)}, u32[]{:S(2)}) collective-permute-start(bf16[512,1408]{0,1:T(8,128)(2,1)} %bitcast_convert_fusion), channel_id=1, source_target_pairs={{0,1},{1,0},{2,3},{3,2},{4,5},{5,4},{6,7},{7,6},{8,9},{9,8},{10,11... | collective-permute-start | bytes 4325384 | tf_op jit(solution)/shard_map/ppermute | solution.py:488
  724.2 271.7 %reduce-scatter.22.cloned.1.call-start = ((), (), s32[]{:S(2)}) async-start(), calls=%async_computation.17 | async-start | bytes 4212736
  724.3 69.8 %collective-permute-start.17 = (bf16[704,3168]{1,0:T(8,128)(2,1)}, bf16[704,3168]{1,0:T(8,128)(2,1)}, u32[]{:S(2)}, u32[]{:S(2)}) collective-permute-start(bf16[704,3168]{1,0:T(8,128)(2,1)} %convolution_convert_fusion.5), channel_id=1, source_target_pairs={{0,2},{2,0},{4,6},{6,4},{8,10},{10,8},{12,14},{14,12},{16,18},{18,... | collective-permute-start | bytes 13381640 | tf_op jit(solution)/shard_map/ppermute | solution.py:484
  724.4 66.1 %collective-permute-start.16 = (bf16[2,792,704]{2,1,0:T(8,128)(2,1)}, bf16[2,792,704]{2,1,0:T(8,128)(2,1)}, u32[]{:S(2)}, u32[]{:S(2)}) collective-permute-start(bf16[2,792,704]{2,1,0:T(8,128)(2,1)} %dynamic-slice_bitcast_fusion), channel_id=1, source_target_pairs={{0,4},{2,6},{4,0},{6,2},{8,12},{10,14},{12,8},{14,10},{16,20},{18,... | collective-permute-start | bytes 6690824 | tf_op jit(solution)/shard_map/ppermute | solution.py:484
  735.8 463.0 %reduce-scatter.16.cloned.1.call-start = ((), (), s32[]{:S(2)}) async-start(), calls=%async_computation.14 | async-start | bytes 2228224
  849.4 351.2 %reduce-scatter.14.cloned.1.call-start = ((), (), s32[]{:S(2)}) async-start(), calls=%async_computation.11 | async-start | bytes 3063808 | tf_op jit(solution)/shard_map/reduce_scatter | solution.py:835
  856.8 345.5 %reduce-scatter.18.cloned.1.call-start = ((), (), s32[]{:S(2)}) async-start(), calls=%async_computation.15 | async-start | bytes 4212736
  876.3 126.6 %collective-permute-start.21 = (bf16[2,176,3168]{2,1,0:T(8,128)(2,1)}, bf16[2,176,3168]{2,1,0:T(8,128)(2,1)}, u32[]{:S(2)}, u32[]{:S(2)}) collective-permute-start(bf16[2,176,3168]{2,1,0:T(8,128)(2,1)} %dynamic-slice_bitcast_fusion.1), channel_id=1, source_target_pairs={{0,4},{2,6},{4,0},{6,2},{8,12},{10,14},{12,8},{14,10},{16,20},{18,... | collective-permute-start | bytes 6690824 | tf_op jit(solution)/shard_map/ppermute | solution.py:484
  968.7 58.2 %collective-permute-start.20 = (bf16[792,704]{1,0:T(8,128)(2,1)}, bf16[792,704]{1,0:T(8,128)(2,1)}, u32[]{:S(2)}, u32[]{:S(2)}) collective-permute-start(bf16[792,704]{1,0:T(8,128)(2,1)} %fusion.67), channel_id=1, source_target_pairs={{16,0},{18,2},{20,4},{22,6},{24,8},{26,10},{28,12},{30,14},{1,17},... | collective-permute-start | bytes 3345416 | tf_op jit(solution)/shard_map/ppermute | solution.py:595
  1083.1 67.2 %collective-permute-start.24 = (bf16[176,3168]{1,0:T(8,128)(2,1)}, bf16[176,3168]{1,0:T(8,128)(2,1)}, u32[]{:S(2)}, u32[]{:S(2)}) collective-permute-start(bf16[176,3168]{1,0:T(8,128)(2,1)} %fusion.73), channel_id=1, source_target_pairs={{16,0},{17,1},{20,4},{21,5},{24,8},{25,9},{28,12},{29,13},{2,18},{... | collective-permute-start | bytes 3345416 | tf_op jit(solution)/shard_map/ppermute | solution.py:595
  1084.6 67.6 %collective-permute-start.25 = (bf16[704,2112]{1,0:T(8,128)(2,1)}, bf16[704,2112]{1,0:T(8,128)(2,1)}, u32[]{:S(2)}, u32[]{:S(2)}) collective-permute-start(bf16[704,2112]{1,0:T(8,128)(2,1)} %convolution_convert_fusion.8), channel_id=1, source_target_pairs={{0,2},{2,0},{4,6},{6,4},{8,10},{10,8},{12,14},{14,12},{16,18},{18,... | collective-permute-start | bytes 8921096 | tf_op jit(solution)/shard_map/ppermute | solution.py:484
  (226 other events, 6359.7 us)
Sparse Core Ops, SparseCore 0:
  10.3 53.9 all-gather.10
  66.4 39.7 all-gather.14
  109.0 41.7 all-gather.22
  153.0 43.1 all-gather.16
  198.7 61.3 all-gather.24
  262.7 59.3 all-gather.12
  324.2 77.4 all-gather.18
  403.9 93.1 all-gather.20
  724.3 93.5 reduce-scatter.19
  821.6 95.1 reduce-scatter.21
  920.5 83.8 reduce-scatter.15
  1008.5 72.2 reduce-scatter.13
  1084.6 90.2 reduce-scatter.17
